TPU v7x, 256 devices: a whole 4x4x8 slice. The times are simulated.
256 devices in a mesh: ctx: 32 (over z, y_lo, core), chan: 8 (over y_hi, x).
Axes of the slice: x: 4, y: 4 (y_hi: 2, y_lo: 2; y = y_hi * 2 + y_lo), z: 8, core: 2. Of those that a mesh axis runs over, the one named last changes fastest.
Arguments:
- sequence: float32 [32, 524288], P('chan', 'ctx'), may hold values from -6 to 6
- filter_taps: float32 [2, 524288], P(None, 'ctx'), may hold values from -6 to 6
- skip_gain: float32 [32], P('chan'), may hold values from 0.5 to 1.5
- cotangent: float32 [32, 524288], P('chan', 'ctx'), may hold values from -6 to 6
Outputs:
- convolved: float32 [32, 524288], P('chan', 'ctx')
- seq_grad: float32 [32, 524288], P('chan', 'ctx')
- filter_grad: float32 [2, 524288], P(None, 'ctx')
All inputs are finite; a program needn't handle non-finite values.
Results may differ from a plain program's by a relative error of at most 0.0003.
Values sent between devices are 32-bit elements; how exact they have to be, the bound alone decides.
No kernel may reach another device: no remote copies, remote signals or barrier semaphores. Data moves between devices by JAX's collectives and lax.ppermute only.
A program may use at most 128 MiB of HBM per device.

v0:
```python
import jax
import jax.numpy as jnp
from jax import lax
from jax.sharding import PartitionSpec as P

P_SIZE = 128
Q = 64


HIGHEST_PRECISION = lax.Precision.HIGHEST
FULL_TURN = 6.283185307179586


def turn_tables(row_index, column_index, modulus, orientation, factor):
    products = row_index[:, None] * column_index[None, :]
    angles = (products % modulus).astype(jnp.float32) * (FULL_TURN / modulus)
    return (factor * jnp.cos(angles), orientation * factor * jnp.sin(angles))


def contract(pattern, operand, matrix):
    return jnp.einsum(pattern, operand, matrix, precision=HIGHEST_PRECISION)


def apply_dft(pattern, real_part, imag_part, cosines, sine_table):
    new_real = contract(pattern, real_part, cosines) + contract(pattern, imag_part, sine_table)
    new_imag = contract(pattern, imag_part, cosines) - contract(pattern, real_part, sine_table)
    return (new_real, new_imag)


def rotate(real_part, imag_part, cosines, sine_table):
    return (
        real_part * cosines + imag_part * sine_table,
        imag_part * cosines - real_part * sine_table,
    )


def complex_product(left_real, left_imag, right_real, right_imag, conj_left):
    if conj_left:
        return (
            left_real * right_real + left_imag * right_imag,
            left_real * right_imag - left_imag * right_real,
        )
    return (
        left_real * right_real - left_imag * right_imag,
        left_real * right_imag + left_imag * right_real,
    )


def outer_twist(real_part, imag_part, orientation):
    flat_local = real_part.shape[2]
    position = lax.axis_index("ctx") * flat_local + jnp.arange(flat_local, dtype=jnp.int32)
    cosines, sine_table = turn_tables(
        jnp.arange(Q, dtype=jnp.int32), position, Q * P_SIZE * P_SIZE, orientation, 1.0
    )
    return rotate(real_part, imag_part, cosines, sine_table)


def outer_tables():
    return turn_tables(
        jnp.arange(Q // 2, dtype=jnp.int32), jnp.arange(Q, dtype=jnp.int32), Q, 1.0, 1.0
    )


def open_real(blocks):
    cosines, sine_table = outer_tables()
    real_part = contract("maf,ak->mkf", blocks, cosines)
    imag_part = -contract("maf,ak->mkf", blocks, sine_table)
    return outer_twist(real_part, imag_part, 1.0)


def finish_forward(pieces):
    item_count = pieces[0].shape[0]
    row_count = pieces[0].shape[1]
    real_part = pieces[0].reshape(item_count, row_count, P_SIZE, P_SIZE)
    imag_part = pieces[1].reshape(item_count, row_count, P_SIZE, P_SIZE)
    digits = jnp.arange(P_SIZE, dtype=jnp.int32)
    cosines, sine_table = turn_tables(digits, digits, P_SIZE, 1.0, 1.0)
    real_part, imag_part = apply_dft("mkbc,bd->mkdc", real_part, imag_part, cosines, sine_table)
    twist_cosine, twist_sine = turn_tables(Q * digits, digits, Q * P_SIZE * P_SIZE, 1.0, 1.0)
    real_part, imag_part = rotate(real_part, imag_part, twist_cosine, twist_sine)
    return apply_dft("mkdc,ce->mkde", real_part, imag_part, cosines, sine_table)


def inner_forward(real_part, imag_part):
    return finish_forward(
        (
            lax.all_to_all(real_part, "ctx", split_axis=1, concat_axis=2, tiled=True),
            lax.all_to_all(imag_part, "ctx", split_axis=1, concat_axis=2, tiled=True),
        )
    )


def inner_inverse(real_part, imag_part):
    digits = jnp.arange(P_SIZE, dtype=jnp.int32)
    cosines, sine_table = turn_tables(digits, digits, P_SIZE, -1.0, 1.0)
    real_part, imag_part = apply_dft("mkde,ec->mkdc", real_part, imag_part, cosines, sine_table)
    twist_cosine, twist_sine = turn_tables(Q * digits, digits, Q * P_SIZE * P_SIZE, -1.0, 1.0)
    real_part, imag_part = rotate(real_part, imag_part, twist_cosine, twist_sine)
    real_part, imag_part = apply_dft("mkdc,db->mkbc", real_part, imag_part, cosines, sine_table)
    item_count = real_part.shape[0]
    row_count = real_part.shape[1]
    return (
        real_part.reshape(item_count, row_count, P_SIZE * P_SIZE),
        imag_part.reshape(item_count, row_count, P_SIZE * P_SIZE),
    )


def outer_inverse(real_part, imag_part):
    length = Q * P_SIZE * P_SIZE // 2
    factor = length ** (-0.5) / (Q * P_SIZE * P_SIZE)
    twisted_real, twisted_imag = outer_twist(
        lax.all_to_all(real_part, "ctx", split_axis=2, concat_axis=1, tiled=True),
        lax.all_to_all(imag_part, "ctx", split_axis=2, concat_axis=1, tiled=True),
        -1.0,
    )
    cosines, sine_table = turn_tables(
        jnp.arange(Q, dtype=jnp.int32), jnp.arange(Q // 2, dtype=jnp.int32), Q, -1.0, factor
    )
    return contract("mkf,ka->maf", twisted_real, cosines) + contract(
        "mkf,ka->maf", twisted_imag, sine_table
    )


def body(sequence, filter_taps, skip_gain, cotangent):
    channels, seq_len = sequence.shape
    groups = filter_taps.shape[0]
    plane_size = P_SIZE * P_SIZE
    stacked = jnp.concatenate([sequence, filter_taps, cotangent], axis=0)
    total_rows = stacked.shape[0]
    spectra = open_real(
        lax.all_to_all(
            stacked.reshape(total_rows, -1, plane_size),
            "ctx",
            split_axis=2,
            concat_axis=1,
            tiled=True,
        )
    )
    spec_real, spec_imag = inner_forward(spectra[0], spectra[1])
    shape_tail = spec_real.shape[1:]
    signal_real = spec_real[:channels].reshape((groups, 2) + shape_tail)
    signal_imag = spec_imag[:channels].reshape((groups, 2) + shape_tail)
    filter_real = spec_real[channels : channels + groups][:, None]
    filter_imag = spec_imag[channels : channels + groups][:, None]
    grad_real = spec_real[channels + groups :].reshape((groups, 2) + shape_tail)
    grad_imag = spec_imag[channels + groups :].reshape((groups, 2) + shape_tail)
    out_real, out_imag = complex_product(filter_real, filter_imag, signal_real, signal_imag, False)
    back_real, back_imag = complex_product(filter_real, filter_imag, grad_real, grad_imag, True)
    tap_real, tap_imag = complex_product(signal_real, signal_imag, grad_real, grad_imag, True)
    joined_real = jnp.concatenate(
        [
            out_real.reshape((channels,) + shape_tail),
            back_real.reshape((channels,) + shape_tail),
            tap_real.sum(axis=1),
        ],
        axis=0,
    )
    joined_imag = jnp.concatenate(
        [
            out_imag.reshape((channels,) + shape_tail),
            back_imag.reshape((channels,) + shape_tail),
            tap_imag.sum(axis=1),
        ],
        axis=0,
    )
    front_real, front_imag = inner_inverse(joined_real, joined_imag)
    closed = outer_inverse(front_real, front_imag)
    restored = lax.all_to_all(closed, "ctx", split_axis=1, concat_axis=2, tiled=True).reshape(
        total_rows, seq_len
    )
    conv_terms = restored[:channels]
    grad_terms = restored[channels : 2 * channels]
    tap_local = restored[2 * channels :]
    skip_column = skip_gain[:, None]
    convolved = conv_terms + skip_column * sequence
    seq_grad = grad_terms + skip_column * cotangent
    filter_grad = lax.psum(tap_local, "chan")
    return (convolved, seq_grad, filter_grad)


def solution(mesh):
    return jax.shard_map(
        body,
        mesh=mesh,
        in_specs=(P("chan", "ctx"), P(None, "ctx"), P("chan"), P("chan", "ctx")),
        out_specs=(P("chan", "ctx"), P("chan", "ctx"), P(None, "ctx")),
        check_vma=False,
    )
```

profile of v0, /device:TPU:32, one launch (start us, length us, event | category | flops | bytes accessed | tf_op | source)
XLA Modules:
  0.0 640.6 jit_solution(16699141753571216129)
XLA Ops:
  7.2 1.3 pad_maximum_fusion.2
  8.5 4.6 copy.64
  13.1 0.5 broadcast.436
  13.6 74.5 %reduce = f32[16384,10]{1,0:T(8,128)} reduce(f32[16384,1,10]{2,1,0:T(1,128)} %bitcast.154, f32[]{:T(128)} %broadcast.436), dimensions={1}, to_apply=%bitcast.134.reduce_sub_computation | reduce | bytes 1310724
  88.1 9.5 %reshape.230 = f32[32,1,5120]{2,1,0:T(1,128)} reshape(f32[16384,10]{1,0:T(8,128)} %reduce) | data formatting | bytes 1310720
  97.6 10.0 %all-to-all-start = ((f32[32,1,5120]{2,1,0:T(1,128)}), f32[32,1,5120]{2,1,0:T(1,128)S(1)}, u32[]{:S(2)}, u32[]{:S(2)}) async-start(f32[32,1,5120]{2,1,0:T(1,128)} %reshape.230), calls=%async_computation | async-start | bytes 1310720 | tf_op jit(solution)/shard_map/all_to_all | solution.py:131
  107.6 1.2 broadcast_multiply_fusion
  108.8 18.3 %all-to-all-done = f32[32,1,5120]{2,1,0:T(1,128)S(1)} async-done(((f32[32,1,5120]{2,1,0:T(1,128)}), f32[32,1,5120]{2,1,0:T(1,128)S(1)}, u32[]{:S(2)}, u32[]{:S(2)}) %all-to-all-start) | async-done | bytes 655392 | tf_op jit(solution)/shard_map/all_to_all | solution.py:131
  127.1 2.2 reduce.1
  129.3 14.5 %reshape.231 = f32[16384,1,10]{2,1,0:T(1,128)} reshape(f32[32,5120]{1,0:T(8,128)S(1)} %reduce.1) | data formatting | bytes 1310720
  143.8 5.2 copy.98
  149.0 1.3 convolution_negate_fusion
  150.3 1.6 subtract_bitcast_fusion
  152.0 2.1 copy.68
  154.1 5.0 all-to-all-start.2
  159.1 2.1 copy.66
  161.2 48.5 %all-to-all-done.2 = f32[10,64,512]{2,0,1:T(8,128)S(1)} async-done(((f32[10,64,512]{2,0,1:T(8,128)}), f32[10,64,512]{2,0,1:T(8,128)S(1)}, u32[]{:S(2)}, u32[]{:S(2)}) %all-to-all-start.2) | async-done | bytes 1310752 | tf_op jit(solution)/shard_map/all_to_all | solution.py:88
  209.7 5.8 all-to-all-start.1
  215.5 0.3 broadcast_multiply_fusion.1
  216.1 1.8 copy.111
  217.9 1.4 reshape.212
  219.3 2.5 fusion.60
  221.8 44.3 %all-to-all-done.1 = f32[10,64,512]{2,0,1:T(8,128)} async-done(((f32[10,64,512]{2,0,1:T(8,128)}), f32[10,64,512]{2,0,1:T(8,128)}, u32[]{:S(2)}, u32[]{:S(2)}) %all-to-all-start.1) | async-done | bytes 1310752 | tf_op jit(solution)/shard_map/all_to_all | solution.py:87
  266.2 3.4 copy.112
  269.6 1.8 reshape.211
  271.4 1.5 fusion.62
  272.9 1.5 convolution_subtract_fusion.3
  274.4 1.5 convolution_add_fusion.3
  275.9 1.5 fusion.2
  277.4 1.5 fusion.6
  278.9 1.5 convolution_subtract_fusion.2
  280.5 1.5 convolution_add_fusion.2
  282.0 0.2 bitcast_reduce_fusion.1
  282.2 0.4 fusion.28
  282.6 1.6 fusion.23
  284.2 1.5 fusion.22
  285.7 1.4 convolution_add_fusion.1
  287.1 1.4 convolution_subtract_fusion.1
  288.6 1.5 fusion.32
  290.1 2.6 fusion
  292.7 13.6 %copy.107 = f32[10,2,128,128]{0,1,3,2:T(2,128)} copy(f32[10,2,128,128]{3,2,1,0:T(8,128)} %fusion) | data formatting | bytes 2621440 | tf_op jit(solution)/shard_map/reshape | solution.py:103
  306.3 28.2 %reshape.232 = f32[32,1,10240]{2,1,0:T(1,128)} reshape(f32[16384,2,10]{2,1,0:T(2,128)} %bitcast.150) | data formatting | bytes 2621440
  334.6 6.1 all-to-all-start.3
  340.7 1.5 fusion.33
  342.2 2.6 fusion.1
  344.8 13.6 %copy.108 = f32[10,2,128,128]{0,1,3,2:T(2,128)} copy(f32[10,2,128,128]{3,2,1,0:T(8,128)} %fusion.1) | data formatting | bytes 2621440 | tf_op jit(solution)/shard_map/reshape | solution.py:104
  358.4 28.3 %reshape.234 = f32[32,1,10240]{2,1,0:T(1,128)} reshape(f32[16384,2,10]{2,1,0:T(2,128)} %bitcast.151) | data formatting | bytes 2621440
  386.7 8.4 %all-to-all-start.4 = ((f32[32,1,10240]{2,1,0:T(1,128)}), f32[32,1,10240]{2,1,0:T(1,128)}, u32[]{:S(2)}, u32[]{:S(2)}) async-start(f32[32,1,10240]{2,1,0:T(1,128)} %reshape.234), calls=%async_computation.4 | async-start | bytes 2621440 | tf_op jit(solution)/shard_map/all_to_all | solution.py:113
  395.1 5.1 reduce.2
  400.2 29.1 %reshape.233 = f32[16384,2,10]{2,1,0:T(2,128)} reshape(f32[32,10240]{1,0:T(8,128)S(1)} %reduce.2) | data formatting | bytes 2621440
  429.3 19.6 %copy.83 = f32[10,32,2,512]{3,2,1,0:T(2,128)S(1)} copy(f32[10,32,2,512]{0,2,3,1:T(2,128)} %bitcast.152) | data formatting | bytes 2621440 | tf_op jit(solution)/shard_map/all_to_all | solution.py:112
  448.8 0.9 all_to_all.75
  449.8 5.1 reduce.3
  454.8 28.7 %reshape.235 = f32[16384,2,10]{2,1,0:T(2,128)} reshape(f32[32,10240]{1,0:T(8,128)S(1)} %reduce.3) | data formatting | bytes 2621440
  483.5 20.2 %copy.85 = f32[10,32,2,512]{3,2,1,0:T(2,128)} copy(f32[10,32,2,512]{0,2,3,1:T(2,128)} %bitcast.153) | data formatting | bytes 2621440 | tf_op jit(solution)/shard_map/all_to_all | solution.py:113
  503.7 2.3 all_to_all.79
  506.0 1.0 fusion.8
  507.0 1.0 fusion.19
  508.0 0.4 copy.86
  508.5 36.3 %all_to_all.87 = f32[10,32,512]{2,0,1:T(8,128)S(1)} all-to-all(f32[10,32,512]{2,0,1:T(8,128)S(1)} %copy.86), channel_id=1, replica_groups=mesh['ctx'=32,'chan'=8] {'ctx'}, dimensions={1} | all-to-all | bytes 1310720 | tf_op jit(solution)/shard_map/all_to_all | solution.py:168
  544.7 0.7 slice.57
  545.6 1.0 multiply_add_fusion.7
  546.6 85.4 %all-reduce.2.cloned.1.call-done = f32[2,16384]{1,0:T(2,128)} async-done(((f32[2,16384]{1,0:T(2,128)}), f32[2,16384]{1,0:T(2,128)}) %all-reduce.2.cloned.1.call-update) | async-done | bytes 131088 | tf_op jit(solution)/shard_map/psum | solution.py:177
  632.0 1.6 copy.114
  (22 shorter events, 0.5 us)
Async XLA Ops:
  97.6 29.5 %all-to-all-start = ((f32[32,1,5120]{2,1,0:T(1,128)}), f32[32,1,5120]{2,1,0:T(1,128)S(1)}, u32[]{:S(2)}, u32[]{:S(2)}) async-start(f32[32,1,5120]{2,1,0:T(1,128)} %reshape.230), calls=%async_computation | async-start | bytes 1310720 | tf_op jit(solution)/shard_map/all_to_all | solution.py:131
  154.1 55.6 %all-to-all-start.2 = ((f32[10,64,512]{2,0,1:T(8,128)}), f32[10,64,512]{2,0,1:T(8,128)S(1)}, u32[]{:S(2)}, u32[]{:S(2)}) async-start(f32[10,64,512]{2,0,1:T(8,128)} %copy.68), calls=%async_computation.2 | async-start | bytes 4194304 | tf_op jit(solution)/shard_map/all_to_all | solution.py:88
  209.7 56.4 %all-to-all-start.1 = ((f32[10,64,512]{2,0,1:T(8,128)}), f32[10,64,512]{2,0,1:T(8,128)}, u32[]{:S(2)}, u32[]{:S(2)}) async-start(f32[10,64,512]{2,0,1:T(8,128)} %copy.66), calls=%async_computation.1 | async-start | bytes 4194304 | tf_op jit(solution)/shard_map/all_to_all | solution.py:87
  271.4 1.5 copy-start
  334.6 52.1 %all-to-all-start.3 = ((f32[32,1,10240]{2,1,0:T(1,128)}), f32[32,1,10240]{2,1,0:T(1,128)}, u32[]{:S(2)}, u32[]{:S(2)}) async-start(f32[32,1,10240]{2,1,0:T(1,128)} %reshape.232), calls=%async_computation.3 | async-start | bytes 2621440 | tf_op jit(solution)/shard_map/all_to_all | solution.py:112
  386.7 63.1 %all-to-all-start.4 = ((f32[32,1,10240]{2,1,0:T(1,128)}), f32[32,1,10240]{2,1,0:T(1,128)}, u32[]{:S(2)}, u32[]{:S(2)}) async-start(f32[32,1,10240]{2,1,0:T(1,128)} %reshape.234), calls=%async_computation.4 | async-start | bytes 2621440 | tf_op jit(solution)/shard_map/all_to_all | solution.py:113
  395.1 236.9 %all-reduce.2.cloned.1.call-start = ((), (), s32[]{:S(2)}) async-start(), calls=%async_computation.6 | async-start | bytes 262144 | tf_op jit(solution)/shard_map/psum | solution.py:177
  503.7 2.3 copy-start.1
  508.5 37.1 %copy-start.2 = (f32[4,16384]{1,0:T(4,128)S(1)}, f32[4,16384]{1,0:T(4,128)}, u32[]{:S(2)}) copy-start(f32[4,16384]{1,0:T(4,128)} %param.7) | copy-start | bytes 786436
  508.5 37.1 %copy-start.3 = (f32[4,16384]{1,0:T(4,128)S(1)}, f32[4,16384]{1,0:T(4,128)}, u32[]{:S(2)}) copy-start(f32[4,16384]{1,0:T(4,128)} %param.4) | copy-start | bytes 786436
  508.5 37.1 %copy-start.4 = (f32[4]{0:T(128)S(1)}, f32[4]{0:T(128)}, u32[]{:S(2)}) copy-start(f32[4]{0:T(128)} %param.6) | copy-start | bytes 52
Sparse Core Ops, SparseCore 0:
  545.6 86.3 all-reduce.1
where the time goes:
time: 653 us; the launch traced here: 641 us
  local copies, waits for them, and re-layouts  234 us (36%)
  waiting for transfers between devices  197 us (30%)
  other arithmetic  91.2 us (14%)
  blocking collectives  36.3 us (6%)
  starting transfers between devices  35.4 us (5%)
  matrix products  32.2 us (5%)
  between operations  14.6 us (2%)
    unnamed x18, local copies, waits for them, and re-layouts  140 us
    psum x1, waiting for transfers between devices, body(): filter_grad = lax.psum(tap_local, 'chan')  85.4 us
    unnamed x1, other arithmetic  74.5 us
    all_to_all x1, waiting for transfers between devices, inner_forward(): lax.all_to_all(imag_part, 'ctx', split_axis=1, concat_axis=2, tiled=True)  48.5 us
    all_to_all x1, waiting for transfers between devices, inner_forward(): lax.all_to_all(real_part, 'ctx', split_axis=1, concat_axis=2, tiled=True)  44.3 us
    all_to_all x1, blocking collectives, body(): lax.all_to_all(closed, 'ctx', split_axis=1, concat_axis=2, tiled=True)  36.3 us
    dot_general x20, matrix products, contract(): return jnp.einsum(pattern, operand, matrix, precision=HIGHEST_PRECISION)  32.2 us
    all_to_all x2, local copies, waits for them, and re-layouts, outer_inverse(): lax.all_to_all(imag_part, 'ctx', split_axis=2, concat_axis=1, tiled=True)  22.5 us
  transfers between devices with their start and end apart: 6, of which 4 were waited for; matrix products, arithmetic and copies ran while one was open for 17% of the time, Pallas kernels for 0%

commit v1 on v0

v1 whole, which is shorter than its diff:
```python
import numpy as np
import jax
import jax.numpy as jnp
from jax import lax
from jax.experimental import pallas as pl
from jax.experimental.pallas import tpu as pltpu
from jax.sharding import PartitionSpec as P
import ml_dtypes

SIDE = 128
BLOCK = SIDE * SIDE
BLOCKS = 32
SUB = SIDE // BLOCKS
ROWS = 2 * SIDE
PAD = 4
TILE = 4
VMEM_LIMIT = 40 * 1024 * 1024


def two_parts(table):
    high = table.astype(ml_dtypes.bfloat16)
    low = (table - high.astype(np.float64)).astype(ml_dtypes.bfloat16)
    return high, low


def make_tables():
    row = np.arange(ROWS)
    coarse = SUB * (row // (2 * SUB)) + row % SUB
    signal = (row // SUB) % 2
    position = np.arange(SIDE)
    turn = 2.0 * np.pi
    angle = turn * ((coarse[:, None] + 0.25) * position[None, :] / SIDE)
    own = (signal[:, None] == np.arange(2)[None, :])[:, :, None]
    cosine = (own * np.cos(angle)[:, None, :]).reshape(ROWS, 2 * SIDE)
    sine = (own * np.sin(angle)[:, None, :]).reshape(ROWS, 2 * SIDE)
    forward_outer = np.concatenate([cosine, -sine], axis=0)
    factor = (BLOCKS * BLOCK) ** (-0.5) / BLOCK
    inverse_outer = factor * np.concatenate([cosine.T, -sine.T], axis=1)
    angle = turn * ((coarse[:, None] + 0.25) * position[None, :] / BLOCK)
    twist = np.stack([np.cos(angle), np.sin(angle)]).astype(np.float32)
    angle = turn * ((position[:, None] * position[None, :]) % SIDE / SIDE)
    cosine, sine = np.cos(angle), np.sin(angle)
    forward_inner = np.block([[cosine, -sine], [sine, cosine]])
    inverse_inner = np.block([[cosine, sine], [-sine, cosine]])
    return (
        two_parts(forward_outer) + two_parts(forward_inner),
        two_parts(inverse_inner) + two_parts(inverse_outer),
        twist,
    )


FORWARD_TABLES, INVERSE_TABLES, TWIST = make_tables()


def split(values):
    high = values.astype(jnp.bfloat16)
    return high, (values - high.astype(jnp.float32)).astype(jnp.bfloat16)


def dot(left, right):
    return jnp.dot(left, right, preferred_element_type=jnp.float32)


def dot_three(left, right):
    return dot(left[0], right[0]) + (dot(left[0], right[1]) + dot(left[1], right[0]))


def spread(source, rows, count):
    for a in range(SIDE):
        rows[pl.ds(a, count, stride=SIDE), :] = source[:, a * SIDE : (a + 1) * SIDE]


def forward_kernel(seq_ref, cot_ref, taps_ref, oh_ref, ol_ref, ih_ref, il_ref, twist_ref, out_ref, rows):
    spread(seq_ref, rows.at[0 : 4 * SIDE], 4)
    spread(cot_ref, rows.at[4 * SIDE : 8 * SIDE], 4)
    spread(taps_ref, rows.at[8 * SIDE : 10 * SIDE], 2)

    def row(index):
        return rows[index * SIDE : (index + 1) * SIDE, :]

    firsts = (0, 1, 4, 5, 8)
    seconds = (2, 3, 6, 7, 9)
    signals = jnp.concatenate(
        [
            jnp.concatenate([row(i) for i in firsts], axis=1),
            jnp.concatenate([row(i) for i in seconds], axis=1),
        ],
        axis=0,
    )
    opened = dot_three((oh_ref[...], ol_ref[...]), split(signals))
    cosine, sine = twist_ref[0], twist_ref[1]
    inner = (ih_ref[...], il_ref[...])
    for p in range(5):
        real = opened[:ROWS, p * SIDE : (p + 1) * SIDE]
        imag = opened[ROWS:, p * SIDE : (p + 1) * SIDE]
        both = jnp.concatenate([real * cosine + imag * sine, imag * cosine - real * sine], axis=1)
        spectrum = dot_three(split(both), inner)
        out_ref[:, 16 * p : 16 * p + 8, :] = spectrum[:, :SIDE].reshape(BLOCKS, 8, SIDE)
        out_ref[:, 16 * p + 8 : 16 * p + 16, :] = spectrum[:, SIDE:].reshape(BLOCKS, 8, SIDE)


def forward_blocks(sequence, cotangent, taps):
    tables = [jnp.asarray(t) for t in FORWARD_TABLES]
    return pl.pallas_call(
        forward_kernel,
        out_shape=jax.ShapeDtypeStruct((BLOCKS, 80, SIDE), jnp.float32),
        in_specs=[pl.BlockSpec(memory_space=pltpu.VMEM)] * 8,
        out_specs=pl.BlockSpec(memory_space=pltpu.VMEM),
        scratch_shapes=[pltpu.VMEM((10 * SIDE, SIDE), jnp.float32)],
        compiler_params=pltpu.CompilerParams(vmem_limit_bytes=VMEM_LIMIT),
        name="forward_blocks",
    )(sequence, cotangent, taps, *tables, jnp.asarray(TWIST))


def middle_kernel(in_ref, out_ref, kernels):
    for slot, p in enumerate((4, 0, 1)):
        kernels[slot, :PAD] = jnp.zeros((PAD, 16, SIDE), jnp.float32)
        top = 16 * p
        kernels[slot, PAD, :, :] = in_ref[0, top : top + 16, :]

        def fill(j, carry, slot=slot, top=top):
            kernels[slot, PAD + j, 0:8, :] = in_ref[j, top : top + 8, :] - in_ref[j - 1, top + 8 : top + 16, :]
            kernels[slot, PAD + j, 8:16, :] = in_ref[j, top + 8 : top + 16, :] + in_ref[j - 1, top : top + 8, :]
            return carry

        lax.fori_loop(1, BLOCKS, fill, 0, unroll=4)

    tiles = BLOCKS // TILE

    def products(slot, p, lag0, b0, causal, totals):
        window = [
            (kernels[slot, PAD + lag0 + d, 0:8, :], kernels[slot, PAD + lag0 + d, 8:16, :])
            for d in range(1 - TILE, TILE)
        ]
        totals = list(totals)
        for s in range(TILE):
            xr = in_ref[b0 + s, 16 * p : 16 * p + 8, :]
            xi = in_ref[b0 + s, 16 * p + 8 : 16 * p + 16, :]
            for i in range(TILE):
                kr, ki = window[TILE - 1 + ((i - s) if causal else (s - i))]
                tr, ti = totals[2 * i], totals[2 * i + 1]
                if causal:
                    totals[2 * i] = tr + kr * xr - ki * xi
                    totals[2 * i + 1] = ti + kr * xi + ki * xr
                else:
                    totals[2 * i] = tr + kr * xr + ki * xi
                    totals[2 * i + 1] = ti + kr * xi - ki * xr
        return tuple(totals)

    def store(m0, p, totals):
        for i in range(TILE):
            out_ref[m0 + i, 16 * p : 16 * p + 8, :] = totals[2 * i]
            out_ref[m0 + i, 16 * p + 8 : 16 * p + 16, :] = totals[2 * i + 1]

    zero = tuple(jnp.zeros((8, SIDE), jnp.float32) for _ in range(2 * TILE))

    def one_tile(t, carry):
        m0 = t * TILE
        for p in (0, 1):
            totals = lax.fori_loop(
                0, t + 1, lambda u, c, p=p: products(0, p, (t - u) * TILE, u * TILE, True, c), zero
            )
            store(m0, p, totals)
        for p in (2, 3):
            totals = lax.fori_loop(
                t, tiles, lambda u, c, p=p: products(0, p, (u - t) * TILE, u * TILE, False, c), zero
            )
            store(m0, p, totals)
        totals = zero
        for q in (0, 1):
            totals = lax.fori_loop(
                t, tiles, lambda u, c, q=q: products(1 + q, 2 + q, (u - t) * TILE, u * TILE, False, c), totals
            )
        store(m0, 4, totals)
        return carry

    lax.fori_loop(0, tiles, one_tile, 0)


def middle_blocks(spectra):
    return pl.pallas_call(
        middle_kernel,
        out_shape=jax.ShapeDtypeStruct((BLOCKS, 80, SIDE), jnp.float32),
        in_specs=[pl.BlockSpec(memory_space=pltpu.VMEM)],
        out_specs=pl.BlockSpec(memory_space=pltpu.VMEM),
        scratch_shapes=[pltpu.VMEM((3, PAD + BLOCKS, 16, SIDE), jnp.float32)],
        compiler_params=pltpu.CompilerParams(vmem_limit_bytes=VMEM_LIMIT),
        name="middle_blocks",
    )(spectra)


def inverse_kernel(
    in_ref, seq_ref, cot_ref, skip_ref, ih_ref, il_ref, oh_ref, ol_ref, twist_ref, y_ref, g_ref, f_ref, rows
):
    cosine, sine = twist_ref[0], twist_ref[1]
    inner = (ih_ref[...], il_ref[...])
    closing = []
    for p in range(5):
        both = jnp.concatenate(
            [
                in_ref[:, 16 * p : 16 * p + 8, :].reshape(ROWS, SIDE),
                in_ref[:, 16 * p + 8 : 16 * p + 16, :].reshape(ROWS, SIDE),
            ],
            axis=1,
        )
        turned = dot_three(split(both), inner)
        real, imag = turned[:, :SIDE], turned[:, SIDE:]
        closing.append(jnp.concatenate([real * cosine - imag * sine, imag * cosine + real * sine], axis=0))
    closed = dot_three((oh_ref[...], ol_ref[...]), split(jnp.concatenate(closing, axis=1)))
    firsts = (0, 1, 4, 5, 8)
    seconds = (2, 3, 6, 7, 9)
    for p in range(5):
        for half, place in enumerate((firsts[p], seconds[p])):
            rows[place * SIDE : (place + 1) * SIDE, :] = closed[
                half * SIDE : (half + 1) * SIDE, p * SIDE : (p + 1) * SIDE
            ]
    skip = jnp.broadcast_to(skip_ref[...], (4, SIDE))
    for a in range(SIDE):
        lanes = slice(a * SIDE, (a + 1) * SIDE)
        y_ref[:, lanes] = rows[pl.ds(a, 4, stride=SIDE), :] + skip * seq_ref[:, lanes]
        g_ref[:, lanes] = rows[pl.ds(4 * SIDE + a, 4, stride=SIDE), :] + skip * cot_ref[:, lanes]
        f_ref[:, lanes] = rows[pl.ds(8 * SIDE + a, 2, stride=SIDE), :]


def inverse_blocks(products, sequence, cotangent, skip_gain):
    tables = [jnp.asarray(t) for t in INVERSE_TABLES]
    return pl.pallas_call(
        inverse_kernel,
        out_shape=(
            jax.ShapeDtypeStruct((4, BLOCK), jnp.float32),
            jax.ShapeDtypeStruct((4, BLOCK), jnp.float32),
            jax.ShapeDtypeStruct((2, BLOCK), jnp.float32),
        ),
        in_specs=[pl.BlockSpec(memory_space=pltpu.VMEM)] * 9,
        out_specs=(pl.BlockSpec(memory_space=pltpu.VMEM),) * 3,
        scratch_shapes=[pltpu.VMEM((10 * SIDE, SIDE), jnp.float32)],
        compiler_params=pltpu.CompilerParams(vmem_limit_bytes=VMEM_LIMIT),
        name="inverse_blocks",
    )(products, sequence, cotangent, skip_gain[:, None], *tables, jnp.asarray(TWIST))


def exchange(blocks):
    return lax.all_to_all(blocks, "ctx", split_axis=0, concat_axis=0, tiled=True)


def sum_over_chan(values, size):
    for flip in (1, 3, 4):
        if flip < size:
            values = values + lax.ppermute(values, "chan", [(i, i ^ flip) for i in range(size)])
    return values


def solution(mesh):
    chan = mesh.shape["chan"]

    def body(sequence, filter_taps, skip_gain, cotangent):
        spectra = exchange(forward_blocks(sequence, cotangent, filter_taps))
        products = exchange(middle_blocks(spectra))
        convolved, seq_grad, taps_grad = inverse_blocks(products, sequence, cotangent, skip_gain)
        return convolved, seq_grad, sum_over_chan(taps_grad, chan)

    return jax.shard_map(
        body,
        mesh=mesh,
        in_specs=(P("chan", "ctx"), P(None, "ctx"), P("chan"), P("chan", "ctx")),
        out_specs=(P("chan", "ctx"), P("chan", "ctx"), P(None, "ctx")),
        check_vma=False,
    )
```

time: 653 us -> 121 us (0.19); the launches traced: 641 us -> 120 us
  local copies, waits for them, and re-layouts: 234 us -> 7.59 us
  waiting for transfers between devices: 197 us -> 44.1 us
  other arithmetic: 91.2 us -> 0.86 us
  matrix products: 32.2 us -> 0 us
  starting transfers between devices: 35.4 us -> 12.3 us
  between operations: 14.6 us -> 0.75 us
  Pallas kernels: 0 us -> 10.8 us
  blocking collectives: 36.3 us -> 43.3 us
    unnamed x18 -> x32, local copies, waits for them, and re-layouts: 140 us -> 7.5 us
    psum x1 -> x0, waiting for transfers between devices: 85.4 us -> none  [body(): filter_grad = lax.psum(tap_local, 'chan')]
    all_to_all x5 -> x1, waiting for transfers between devices: 111 us -> 33.7 us  [exchange(): lax.all_to_all(blocks, 'ctx', split_axis=0, concat_axis=0, tiled=True)]
    unnamed x1 -> x0, other arithmetic: 74.5 us -> none
    all_to_all x7 -> x0, local copies, waits for them, and re-layouts: 53.4 us -> none  [the longest x2 22.5 us: outer_inverse(): lax.all_to_all(imag_part, 'ctx', split_axis=2, concat_axis=1, tiled=True)]
    dot_general x20 -> x0, matrix products: 32.2 us -> none  [contract(): return jnp.einsum(pattern, operand, matrix, precision=HIGHEST_PRECISION)]
    all_to_all x5 -> x1, starting transfers between devices: 35.3 us -> 4.97 us  [exchange(): lax.all_to_all(blocks, 'ctx', split_axis=0, concat_axis=0, tiled=True)]
    reshape x4 -> x0, local copies, waits for them, and re-layouts: 30.3 us -> none  [the longest x1 13.6 us: inner_inverse(): real_part.reshape(item_count, row_count, P_SIZE * P_SIZE)]
  transfers between devices with their start and end apart: 6 -> 4, of which waited for: 4 -> 4; matrix products, arithmetic and copies ran while one was open for 17% -> 0% of each run, Pallas kernels for 0% -> 0%
where the time goes in v1:
time: 121 us; the launch traced here: 120 us
  waiting for transfers between devices  44.1 us (36%)
  blocking collectives  43.3 us (36%)
  starting transfers between devices  12.3 us (10%)
  Pallas kernels  10.8 us (9%)
  local copies, waits for them, and re-layouts  7.59 us (6%)
    all_to_all x1, blocking collectives, exchange(): lax.all_to_all(blocks, 'ctx', split_axis=0, concat_axis=0, tiled=True)  43.3 us
    all_to_all x1, waiting for transfers between devices, exchange(): lax.all_to_all(blocks, 'ctx', split_axis=0, concat_axis=0, tiled=True)  33.7 us
    ppermute x3, waiting for transfers between devices, sum_over_chan(): lax.ppermute(values, 'chan', [(i, i ^ flip) for i in range(size)])  10.5 us
    unnamed x32, local copies, waits for them, and re-layouts  7.5 us
    ppermute x3, starting transfers between devices, sum_over_chan(): lax.ppermute(values, 'chan', [(i, i ^ flip) for i in range(size)])  7.33 us
    pallas_call x1, Pallas kernels, middle_blocks(): pl.pallas_call(middle_kernel, out_shape=jax.ShapeDtypeStruct((BLOCKS, 80,...  6.4 us
    all_to_all x1, starting transfers between devices, exchange(): lax.all_to_all(blocks, 'ctx', split_axis=0, concat_axis=0, tiled=True)  4.97 us
    pallas_call x1, Pallas kernels, inverse_blocks(): pl.pallas_call(inverse_kernel, out_shape=(jax.ShapeDtypeStruct((4, BLOCK)...  2.57 us
  transfers between devices with their start and end apart: 4, of which 4 were waited for; matrix products, arithmetic and copies ran while one was open for 0% of the time, Pallas kernels for 0%

profile of v1, /device:TPU:32, one launch (start us, length us, event | category | flops | bytes accessed | tf_op | source)
XLA Modules:
  0.0 119.7 jit_solution(8574005477309360933)
XLA Ops:
  0.6 0.0 copy-start
  0.6 0.9 copy-done
  1.6 0.0 copy-start.2
  1.6 0.9 copy-done.2
  2.5 0.0 copy-start.4
  2.5 0.9 copy-done.4
  3.5 0.0 copy-start.8
  3.5 0.9 copy-done.8
  4.4 0.0 copy-start.9
  4.4 0.9 copy-done.9
  5.4 0.0 copy-start.10
  5.4 0.9 copy-done.10
  6.3 0.0 copy-start.13
  6.3 0.9 copy-done.13
  7.2 0.0 copy-start.14
  7.2 0.9 copy-done.14
  8.1 1.8 %forward_blocks.1 = f32[32,80,128]{2,1,0:T(8,128)S(1)} custom-call(f32[4,16384]{1,0:T(4,128)S(1)} %copy-done, f32[4,16384]{1,0:T(4,128)S(1)} %copy-done.2, f32[2,16384]{1,0:T(2,128)S(1)} %copy-done.10, bf16[512,256]{1,0:T(8,128)(2,1)S(1)} %copy-done.8, bf16[512,256]{1,0:T(8,128)(2,1)S(1)} %copy-done.9, bf16[256,256]{1,0:T(8,128)(2,1)S(1)} %copy-done.13, ...), custom_call_target="tpu_custom_call" | custom-call | tf_op jit(solution)/shard_map/forward_blocks/pallas_call | solution.py:104
  9.9 43.3 %all_to_all.10.in_ref = f32[32,80,128]{2,1,0:T(8,128)S(1)} all-to-all(f32[32,80,128]{2,1,0:T(8,128)S(1)} %forward_blocks.1), channel_id=1, replica_groups=mesh['ctx'=32,'chan'=8] {'ctx'}, dimensions={0} | all-to-all | bytes 2621440 | tf_op jit(solution)/shard_map/all_to_all | solution.py:243
  53.2 6.4 %middle_blocks.1 = f32[32,80,128]{2,1,0:T(8,128)} custom-call(f32[32,80,128]{2,1,0:T(8,128)S(1)} %all_to_all.10.in_ref), custom_call_target="tpu_custom_call" | custom-call | tf_op jit(solution)/shard_map/middle_blocks/pallas_call | solution.py:181
  59.6 0.0 copy-start.15
  59.6 0.0 copy-start.1
  59.6 0.0 copy-start.3
  59.6 0.0 copy-start.5
  59.6 0.0 copy-start.6
  59.7 0.0 copy-start.7
  59.7 0.0 copy-start.11
  59.7 0.0 copy-start.12
  59.7 5.0 %all-to-all-start.1 = ((f32[32,80,128]{2,1,0:T(8,128)}), f32[32,80,128]{2,1,0:T(8,128)S(1)}, u32[]{:S(2)}, u32[]{:S(2)}) async-start(f32[32,80,128]{2,1,0:T(8,128)} %middle_blocks.1), calls=%async_computation.1 | async-start | bytes 2621440 | tf_op jit(solution)/shard_map/all_to_all | solution.py:243
  64.7 0.0 copy-done.15
  64.7 0.1 copy.16.skip_ref
  64.8 33.7 %all-to-all-done.1.in_ref = f32[32,80,128]{2,1,0:T(8,128)S(1)} async-done(((f32[32,80,128]{2,1,0:T(8,128)}), f32[32,80,128]{2,1,0:T(8,128)S(1)}, u32[]{:S(2)}, u32[]{:S(2)}) %all-to-all-start.1) | async-done | bytes 1310752 | tf_op jit(solution)/shard_map/all_to_all | solution.py:243
  98.4 0.0 copy-done.1
  98.4 0.0 copy-done.3
  98.5 0.0 copy-done.5
  98.5 0.0 copy-done.6
  98.5 0.0 copy-done.7
  98.5 0.0 copy-done.11
  98.5 0.0 copy-done.12
  98.5 2.6 %inverse_blocks.1 = (f32[4,16384]{1,0:T(4,128)}, f32[4,16384]{1,0:T(4,128)}, f32[2,16384]{1,0:T(2,128)S(1)}) custom-call(f32[32,80,128]{2,1,0:T(8,128)S(1)} %all-to-all-done.1.in_ref, f32[4,16384]{1,0:T(4,128)S(1)} %copy-done.1, f32[4,16384]{1,0:T(4,128)S(1)} %copy-done.3, f32[4,1]{1,0:T(4,128)S(1)} %copy.16.skip_ref, bf16[256,256]{1,0:T(8,128)(2,1)S(1)} %copy-done.11, ...), custom_call_target="tpu_custom_call" | custom-call | tf_op jit(solution)/shard_map/inverse_blocks/pallas_call | solution.py:227
  101.1 1.5 %collective-permute-start = (f32[2,16384]{1,0:T(2,128)S(1)}, f32[2,16384]{1,0:T(2,128)S(1)}, u32[]{:S(2)}, u32[]{:S(2)}) collective-permute-start(f32[2,16384]{1,0:T(2,128)S(1)} %get-tuple-element.8), channel_id=1, source_target_pairs={{0,1},{1,0},{2,3},{3,2},{4,5},{5,4},{6,7},{7,6},{8,9},{9,8},{10,11... | collective-permute-start | bytes 393224 | tf_op jit(solution)/shard_map/ppermute | solution.py:249
  102.6 3.5 %collective-permute-done = f32[2,16384]{1,0:T(2,128)S(1)} collective-permute-done((f32[2,16384]{1,0:T(2,128)S(1)}, f32[2,16384]{1,0:T(2,128)S(1)}, u32[]{:S(2)}, u32[]{:S(2)}) %collective-permute-start) | collective-permute-done | bytes 131104 | tf_op jit(solution)/shard_map/ppermute | solution.py:249
  106.0 0.1 add.9
  106.1 2.8 %collective-permute-start.1 = (f32[2,16384]{1,0:T(2,128)S(1)}, f32[2,16384]{1,0:T(2,128)S(1)}, u32[]{:S(2)}, u32[]{:S(2)}) collective-permute-start(f32[2,16384]{1,0:T(2,128)S(1)} %add.9), channel_id=1, source_target_pairs={{0,3},{1,2},{2,1},{3,0},{4,7},{5,6},{6,5},{7,4},{8,11},{9,10},{10,... | collective-permute-start | bytes 393224 | tf_op jit(solution)/shard_map/ppermute | solution.py:249
  108.9 3.4 %collective-permute-done.1 = f32[2,16384]{1,0:T(2,128)S(1)} collective-permute-done((f32[2,16384]{1,0:T(2,128)S(1)}, f32[2,16384]{1,0:T(2,128)S(1)}, u32[]{:S(2)}, u32[]{:S(2)}) %collective-permute-start.1) | collective-permute-done | bytes 131104 | tf_op jit(solution)/shard_map/ppermute | solution.py:249
  112.4 0.1 add.10
  112.4 3.0 %collective-permute-start.2 = (f32[2,16384]{1,0:T(2,128)S(1)}, f32[2,16384]{1,0:T(2,128)S(1)}, u32[]{:S(2)}, u32[]{:S(2)}) collective-permute-start(f32[2,16384]{1,0:T(2,128)S(1)} %add.10), channel_id=1, source_target_pairs={{0,4},{1,5},{2,6},{3,7},{4,0},{5,1},{6,2},{7,3},{8,12},{9,13},{10,... | collective-permute-start | bytes 393224 | tf_op jit(solution)/shard_map/ppermute | solution.py:249
  115.4 3.6 %collective-permute-done.2 = f32[2,16384]{1,0:T(2,128)S(1)} collective-permute-done((f32[2,16384]{1,0:T(2,128)S(1)}, f32[2,16384]{1,0:T(2,128)S(1)}, u32[]{:S(2)}, u32[]{:S(2)}) %collective-permute-start.2) | collective-permute-done | bytes 131104 | tf_op jit(solution)/shard_map/ppermute | solution.py:249
  119.0 0.7 add.11
Async XLA Ops:
  0.6 1.0 copy-start
  1.6 0.9 copy-start.2
  2.5 0.9 copy-start.4
  3.5 0.9 copy-start.8
  4.4 0.9 copy-start.9
  5.4 0.9 copy-start.10
  6.3 0.9 copy-start.13
  7.2 0.9 copy-start.14
  59.6 5.0 %copy-start.15 = (f32[4]{0:T(128)S(1)}, f32[4]{0:T(128)}, u32[]{:S(2)}) copy-start(f32[4]{0:T(128)} %param.15) | copy-start | bytes 52
  59.6 38.8 %copy-start.1 = (f32[4,16384]{1,0:T(4,128)S(1)}, f32[4,16384]{1,0:T(4,128)}, u32[]{:S(2)}) copy-start(f32[4,16384]{1,0:T(4,128)} %seq_ref.3) | copy-start | bytes 786436
  59.6 38.8 %copy-start.3 = (f32[4,16384]{1,0:T(4,128)S(1)}, f32[4,16384]{1,0:T(4,128)}, u32[]{:S(2)}) copy-start(f32[4,16384]{1,0:T(4,128)} %cot_ref.3) | copy-start | bytes 786436
  59.6 38.8 %copy-start.5 = (f32[2,256,128]{2,1,0:T(8,128)S(1)}, f32[2,256,128]{2,1,0:T(8,128)}, u32[]{:S(2)}) copy-start(f32[2,256,128]{2,1,0:T(8,128)} %constant.22.clone.twist_ref) | copy-start | bytes 786436
  59.6 38.8 %copy-start.6 = (bf16[256,512]{1,0:T(8,128)(2,1)S(1)}, bf16[256,512]{1,0:T(8,128)(2,1)}, u32[]{:S(2)}) copy-start(bf16[256,512]{1,0:T(8,128)(2,1)} %constant.25.clone.oh_ref) | copy-start | bytes 786436
  59.7 38.8 %copy-start.7 = (bf16[256,512]{1,0:T(8,128)(2,1)S(1)}, bf16[256,512]{1,0:T(8,128)(2,1)}, u32[]{:S(2)}) copy-start(bf16[256,512]{1,0:T(8,128)(2,1)} %constant.26.clone.ol_ref) | copy-start | bytes 786436
  59.7 38.8 %copy-start.11 = (bf16[256,256]{1,0:T(8,128)(2,1)S(1)}, bf16[256,256]{1,0:T(8,128)(2,1)}, u32[]{:S(2)}) copy-start(bf16[256,256]{1,0:T(8,128)(2,1)} %constant.23.clone.ih_ref) | copy-start | bytes 393220
  59.7 38.8 %copy-start.12 = (bf16[256,256]{1,0:T(8,128)(2,1)S(1)}, bf16[256,256]{1,0:T(8,128)(2,1)}, u32[]{:S(2)}) copy-start(bf16[256,256]{1,0:T(8,128)(2,1)} %constant.24.clone.il_ref) | copy-start | bytes 393220
  59.7 38.7 %all-to-all-start.1 = ((f32[32,80,128]{2,1,0:T(8,128)}), f32[32,80,128]{2,1,0:T(8,128)S(1)}, u32[]{:S(2)}, u32[]{:S(2)}) async-start(f32[32,80,128]{2,1,0:T(8,128)} %middle_blocks.1), calls=%async_computation.1 | async-start | bytes 2621440 | tf_op jit(solution)/shard_map/all_to_all | solution.py:243
  101.1 5.0 %collective-permute-start = (f32[2,16384]{1,0:T(2,128)S(1)}, f32[2,16384]{1,0:T(2,128)S(1)}, u32[]{:S(2)}, u32[]{:S(2)}) collective-permute-start(f32[2,16384]{1,0:T(2,128)S(1)} %get-tuple-element.8), channel_id=1, source_target_pairs={{0,1},{1,0},{2,3},{3,2},{4,5},{5,4},{6,7},{7,6},{8,9},{9,8},{10,11... | collective-permute-start | bytes 393224 | tf_op jit(solution)/shard_map/ppermute | solution.py:249
  106.1 6.3 %collective-permute-start.1 = (f32[2,16384]{1,0:T(2,128)S(1)}, f32[2,16384]{1,0:T(2,128)S(1)}, u32[]{:S(2)}, u32[]{:S(2)}) collective-permute-start(f32[2,16384]{1,0:T(2,128)S(1)} %add.9), channel_id=1, source_target_pairs={{0,3},{1,2},{2,1},{3,0},{4,7},{5,6},{6,5},{7,4},{8,11},{9,10},{10,... | collective-permute-start | bytes 393224 | tf_op jit(solution)/shard_map/ppermute | solution.py:249
  112.4 6.6 %collective-permute-start.2 = (f32[2,16384]{1,0:T(2,128)S(1)}, f32[2,16384]{1,0:T(2,128)S(1)}, u32[]{:S(2)}, u32[]{:S(2)}) collective-permute-start(f32[2,16384]{1,0:T(2,128)S(1)} %add.10), channel_id=1, source_target_pairs={{0,4},{1,5},{2,6},{3,7},{4,0},{5,1},{6,2},{7,3},{8,12},{9,13},{10,... | collective-permute-start | bytes 393224 | tf_op jit(solution)/shard_map/ppermute | solution.py:249

commit v2 on v1

v2 whole, which is shorter than its diff:
```python
import numpy as np
import jax
import jax.numpy as jnp
from jax import lax
from jax.experimental import pallas as pl
from jax.experimental.pallas import tpu as pltpu
from jax.sharding import PartitionSpec as P

SIDE = 128
BLOCK = SIDE * SIDE
BLOCKS = 32
SUB = SIDE // BLOCKS
ROWS = 2 * SIDE
POINTS = 2 * BLOCKS
VMEM_LIMIT = 40 * 1024 * 1024


def make_tables():
    row = np.arange(ROWS)
    coarse = SUB * (row // (2 * SUB)) + row % SUB
    signal = (row // SUB) % 2
    position = np.arange(SIDE)
    turn = 2.0 * np.pi
    angle = turn * ((coarse[:, None] + 0.25) * position[None, :] / SIDE)
    own = (signal[:, None] == np.arange(2)[None, :])[:, :, None]
    cosine = (own * np.cos(angle)[:, None, :]).reshape(ROWS, 2 * SIDE)
    sine = (own * np.sin(angle)[:, None, :]).reshape(ROWS, 2 * SIDE)
    forward_outer = np.concatenate([cosine, -sine], axis=0)
    factor = (BLOCKS * BLOCK) ** (-0.5) / BLOCK
    inverse_outer = factor * np.concatenate([cosine.T, -sine.T], axis=1)
    angle = turn * ((coarse[:, None] + 0.25) * position[None, :] / BLOCK)
    twist = np.stack([np.cos(angle), np.sin(angle)]).astype(np.float32)
    angle = turn * ((position[:, None] * position[None, :]) % SIDE / SIDE)
    cosine, sine = np.cos(angle), np.sin(angle)
    forward_inner = np.block([[cosine, -sine], [sine, cosine]])
    inverse_inner = np.block([[cosine, sine], [-sine, cosine]])
    single = np.float32
    return (
        (forward_outer.astype(single), forward_inner.astype(single), twist),
        (inverse_inner.astype(single), inverse_outer.astype(single), twist),
    )


def make_block_tables():
    block = np.arange(BLOCKS)
    point = np.arange(POINTS)
    angle = 2.0 * np.pi * ((point[:, None] * block[None, :]) % POINTS) / POINTS
    cosine, sine = np.cos(angle), np.sin(angle)
    tables = [np.block([[cosine, sine], [-sine, cosine]]).astype(np.float32)]
    step = np.exp(-2j * np.pi * point / POINTS)
    for spill in (1.0 + 1j * step, 1.0 - 1j * np.conj(step)):
        back = np.exp(1j * angle.T) * spill[None, :] / POINTS
        tables.append(np.block([[back.real, -back.imag], [back.imag, back.real]]).astype(np.float32))
    return tables


FORWARD_TABLES, INVERSE_TABLES = make_tables()
BLOCK_TABLES = make_block_tables()


def split(values):
    high = values.astype(jnp.bfloat16)
    return high, (values - high.astype(jnp.float32)).astype(jnp.bfloat16)


def dot(left, right):
    return jnp.dot(left, right, preferred_element_type=jnp.float32)


def dot_three(left, right):
    return dot(left[0], right[0]) + (dot(left[0], right[1]) + dot(left[1], right[0]))


def spread(source, rows, count):
    for a in range(SIDE):
        rows[pl.ds(a, count, stride=SIDE), :] = source[:, a * SIDE : (a + 1) * SIDE]


def forward_kernel(*refs):
    sources, out_ref, held, rows, sems = refs[:6], refs[6], refs[7:13], refs[13], refs[14]
    copies = [pltpu.make_async_copy(s, h, sems.at[i]) for i, (s, h) in enumerate(zip(sources, held))]
    for copy in copies:
        copy.start()
    seq_ref, cot_ref, taps_ref, outer_ref, inner_ref, twist_ref = held
    copies[0].wait()
    spread(seq_ref, rows.at[0 : 4 * SIDE], 4)
    copies[1].wait()
    spread(cot_ref, rows.at[4 * SIDE : 8 * SIDE], 4)
    copies[2].wait()
    spread(taps_ref, rows.at[8 * SIDE : 10 * SIDE], 2)
    for copy in copies[3:]:
        copy.wait()

    def row(index):
        return rows[index * SIDE : (index + 1) * SIDE, :]

    signals = jnp.concatenate(
        [
            jnp.concatenate([row(i) for i in (0, 1, 4, 5, 8)], axis=1),
            jnp.concatenate([row(i) for i in (2, 3, 6, 7, 9)], axis=1),
        ],
        axis=0,
    )
    opened = dot_three(split(outer_ref[...]), split(signals))
    cosine, sine = twist_ref[0], twist_ref[1]
    inner = split(inner_ref[...])
    for p in range(5):
        real = opened[:ROWS, p * SIDE : (p + 1) * SIDE]
        imag = opened[ROWS:, p * SIDE : (p + 1) * SIDE]
        both = jnp.concatenate([real * cosine + imag * sine, imag * cosine - real * sine], axis=1)
        spectrum = dot_three(split(both), inner)
        out_ref[:, 16 * p : 16 * p + 8, :] = spectrum[:, :SIDE].reshape(BLOCKS, 8, SIDE)
        out_ref[:, 16 * p + 8 : 16 * p + 16, :] = spectrum[:, SIDE:].reshape(BLOCKS, 8, SIDE)


def forward_blocks(sequence, cotangent, taps):
    operands = (sequence, cotangent, taps) + tuple(jnp.asarray(t) for t in FORWARD_TABLES)
    return pl.pallas_call(
        forward_kernel,
        out_shape=jax.ShapeDtypeStruct((BLOCKS, 80, SIDE), jnp.float32),
        in_specs=[pl.BlockSpec(memory_space=pl.ANY)] * 6,
        out_specs=pl.BlockSpec(memory_space=pltpu.VMEM),
        scratch_shapes=[pltpu.VMEM(v.shape, v.dtype) for v in operands]
        + [pltpu.VMEM((10 * SIDE, SIDE), jnp.float32), pltpu.SemaphoreType.DMA((6,))],
        compiler_params=pltpu.CompilerParams(vmem_limit_bytes=60 * 1024 * 1024),
        name="forward_blocks",
    )(*operands)


def middle_kernel(in_ref, there_ref, back_ref, adjoint_ref, out_ref, taps_ref):
    def three(values):
        high, low = split(values)
        return jnp.concatenate([high, low, high], axis=0)

    def wide(table):
        high, low = split(table[...])
        return jnp.concatenate([high, high, low], axis=1)

    there, back, adjoint = wide(there_ref), wide(back_ref), wide(adjoint_ref)

    def pair(p):
        halves = [
            jnp.concatenate(
                [in_ref[pl.ds(16 * p + 8 * h + r, BLOCKS, stride=80), :] for r in range(8)], axis=1
            )
            for h in range(2)
        ]
        points = dot(there, three(jnp.concatenate(halves, axis=0)))
        return points[:POINTS], points[POINTS:]

    def store(ref, p, width, table, real, imag):
        blocks = dot(table, three(jnp.concatenate([real, imag], axis=0)))
        for h in range(2):
            for r in range(8):
                ref[pl.ds(16 * p + 8 * h + r, BLOCKS, stride=width), :] = blocks[
                    BLOCKS * h : BLOCKS * (h + 1), r * SIDE : (r + 1) * SIDE
                ]

    signals = [pair(p) for p in range(4)]
    tap_real = tap_imag = 0.0
    for q in range(2):
        (xr, xi), (gr, gi) = signals[q], signals[2 + q]
        tap_real = tap_real + (xr * gr + xi * gi)
        tap_imag = tap_imag + (xr * gi - xi * gr)
    store(taps_ref, 0, 16, adjoint, tap_real, tap_imag)
    hr, hi = pair(4)
    for q in range(2):
        (xr, xi), (gr, gi) = signals[q], signals[2 + q]
        store(out_ref, q, 64, back, hr * xr - hi * xi, hr * xi + hi * xr)
        store(out_ref, 2 + q, 64, adjoint, hr * gr + hi * gi, hr * gi - hi * gr)


def middle_blocks(spectra):
    tables = [jnp.asarray(t) for t in BLOCK_TABLES]
    products, taps = pl.pallas_call(
        middle_kernel,
        out_shape=(
            jax.ShapeDtypeStruct((BLOCKS * 64, SIDE), jnp.float32),
            jax.ShapeDtypeStruct((BLOCKS * 16, SIDE), jnp.float32),
        ),
        in_specs=[pl.BlockSpec(memory_space=pltpu.VMEM)] * 4,
        out_specs=(pl.BlockSpec(memory_space=pltpu.VMEM),) * 2,
        compiler_params=pltpu.CompilerParams(vmem_limit_bytes=VMEM_LIMIT),
        name="middle_blocks",
    )(spectra.reshape(BLOCKS * 80, SIDE), *tables)
    return products.reshape(BLOCKS, 64, SIDE), taps.reshape(BLOCKS, 16, SIDE)


def closed_blocks(in_ref, inner_ref, outer_ref, twist_ref, rows, count):
    cosine, sine = twist_ref[0], twist_ref[1]
    inner = split(inner_ref[...])
    closing = []
    for p in range(count):
        both = jnp.concatenate(
            [
                in_ref[:, 16 * p : 16 * p + 8, :].reshape(ROWS, SIDE),
                in_ref[:, 16 * p + 8 : 16 * p + 16, :].reshape(ROWS, SIDE),
            ],
            axis=1,
        )
        turned = dot_three(split(both), inner)
        real, imag = turned[:, :SIDE], turned[:, SIDE:]
        closing.append(jnp.concatenate([real * cosine - imag * sine, imag * cosine + real * sine], axis=0))
    closed = dot_three(split(outer_ref[...]), split(jnp.concatenate(closing, axis=1)))
    for p in range(count):
        for half in range(2):
            place = 4 * (p // 2) + 2 * half + p % 2 if count > 1 else half
            rows[place * SIDE : (place + 1) * SIDE, :] = closed[
                half * SIDE : (half + 1) * SIDE, p * SIDE : (p + 1) * SIDE
            ]


def taps_kernel(in_ref, inner_ref, outer_ref, twist_ref, f_ref, rows):
    closed_blocks(in_ref, inner_ref, outer_ref, twist_ref, rows, 1)
    for a in range(SIDE):
        f_ref[:, a * SIDE : (a + 1) * SIDE] = rows[pl.ds(a, 2, stride=SIDE), :]


def inverse_kernel(
    in_ref, seq_ref, cot_ref, skip_ref, inner_ref, outer_ref, twist_ref, y_ref, g_ref, rows
):
    closed_blocks(in_ref, inner_ref, outer_ref, twist_ref, rows, 4)
    skip = jnp.broadcast_to(skip_ref[...], (4, SIDE))
    for a in range(SIDE):
        lanes = slice(a * SIDE, (a + 1) * SIDE)
        y_ref[:, lanes] = rows[pl.ds(a, 4, stride=SIDE), :] + skip * seq_ref[:, lanes]
        g_ref[:, lanes] = rows[pl.ds(4 * SIDE + a, 4, stride=SIDE), :] + skip * cot_ref[:, lanes]


def taps_blocks(products):
    tables = [jnp.asarray(t) for t in INVERSE_TABLES]
    return pl.pallas_call(
        taps_kernel,
        out_shape=jax.ShapeDtypeStruct((2, BLOCK), jnp.float32),
        in_specs=[pl.BlockSpec(memory_space=pltpu.VMEM)] * 4,
        out_specs=pl.BlockSpec(memory_space=pltpu.VMEM),
        scratch_shapes=[pltpu.VMEM((2 * SIDE, SIDE), jnp.float32)],
        compiler_params=pltpu.CompilerParams(vmem_limit_bytes=VMEM_LIMIT),
        name="taps_blocks",
    )(products, *tables)


def inverse_blocks(products, sequence, cotangent, skip_gain):
    tables = [jnp.asarray(t) for t in INVERSE_TABLES]
    return pl.pallas_call(
        inverse_kernel,
        out_shape=(jax.ShapeDtypeStruct((4, BLOCK), jnp.float32),) * 2,
        in_specs=[pl.BlockSpec(memory_space=pltpu.VMEM)] * 7,
        out_specs=(pl.BlockSpec(memory_space=pltpu.VMEM),) * 2,
        scratch_shapes=[pltpu.VMEM((8 * SIDE, SIDE), jnp.float32)],
        compiler_params=pltpu.CompilerParams(vmem_limit_bytes=VMEM_LIMIT),
        name="inverse_blocks",
    )(products, sequence, cotangent, skip_gain[:, None], *tables)


def exchange(blocks):
    return lax.all_to_all(blocks, "ctx", split_axis=0, concat_axis=0, tiled=True)


def sum_over_chan(values, size):
    for flip in (1, 3, 4):
        if flip < size:
            values = values + lax.ppermute(values, "chan", [(i, i ^ flip) for i in range(size)])
    return values


def solution(mesh):
    chan = mesh.shape["chan"]

    def body(sequence, filter_taps, skip_gain, cotangent):
        spectra = exchange(forward_blocks(sequence, cotangent, filter_taps))
        products, taps = middle_blocks(spectra)
        taps = exchange(taps)
        taps, products = lax.optimization_barrier((taps, products))
        taps_grad = sum_over_chan(taps_blocks(taps), chan)
        convolved, seq_grad = inverse_blocks(exchange(products), sequence, cotangent, skip_gain)
        return convolved, seq_grad, taps_grad

    return jax.shard_map(
        body,
        mesh=mesh,
        in_specs=(P("chan", "ctx"), P(None, "ctx"), P("chan"), P("chan", "ctx")),
        out_specs=(P("chan", "ctx"), P("chan", "ctx"), P(None, "ctx")),
        check_vma=False,
    )
```

time: 121 us -> 104 us (0.86)
  waiting for transfers between devices: 44.1 us -> 18.8 us
  blocking collectives: 43.3 us -> 59.3 us
  local copies, waits for them, and re-layouts: 7.59 us -> 0.14 us
    all_to_all x1, waiting for transfers between devices: 33.7 us -> 6.22 us  [exchange(): lax.all_to_all(blocks, 'ctx', split_axis=0, concat_axis=0, tiled=True)]
    all_to_all x1 -> x2, blocking collectives: 43.3 us -> 59.3 us  [exchange(): lax.all_to_all(blocks, 'ctx', split_axis=0, concat_axis=0, tiled=True)]
    unnamed x32 -> x18, local copies, waits for them, and re-layouts: 7.5 us -> 0.05 us
    pallas_call x1 -> x2, Pallas kernels: 6.4 us -> 4.08 us  [the longest x1 3.19 us: middle_blocks(): pl.pallas_call(middle_kernel, out_shape=(jax.ShapeDtypeStruct((BLOCKS * 6...]
    pallas_call x1, Pallas kernels: 1.84 us -> 4.03 us  [forward_blocks(): pl.pallas_call(forward_kernel, out_shape=jax.ShapeDtypeStruct((BLOCKS, 80...]
    ppermute x3, waiting for transfers between devices: 10.5 us -> 12.6 us  [sum_over_chan(): lax.ppermute(values, 'chan', [(i, i ^ flip) for i in range(size)])]
  transfers between devices with their start and end apart: 4 -> 4, of which waited for: 4 -> 4; matrix products, arithmetic and copies ran while one was open for 0% -> 1% of each run, Pallas kernels for 0% -> 1%
where the time goes in v2:
time: 104 us; the launch traced here: 102 us
  blocking collectives  59.3 us (57%)
  waiting for transfers between devices  18.8 us (18%)
  starting transfers between devices  12 us (12%)
  Pallas kernels  10.3 us (10%)
    all_to_all x2, blocking collectives, exchange(): lax.all_to_all(blocks, 'ctx', split_axis=0, concat_axis=0, tiled=True)  59.3 us
    ppermute x3, waiting for transfers between devices, sum_over_chan(): lax.ppermute(values, 'chan', [(i, i ^ flip) for i in range(size)])  12.6 us
    ppermute x3, starting transfers between devices, sum_over_chan(): lax.ppermute(values, 'chan', [(i, i ^ flip) for i in range(size)])  7.43 us
    all_to_all x1, waiting for transfers between devices, exchange(): lax.all_to_all(blocks, 'ctx', split_axis=0, concat_axis=0, tiled=True)  6.22 us
    all_to_all x1, starting transfers between devices, exchange(): lax.all_to_all(blocks, 'ctx', split_axis=0, concat_axis=0, tiled=True)  4.55 us
    pallas_call x1, Pallas kernels, forward_blocks(): pl.pallas_call(forward_kernel, out_shape=jax.ShapeDtypeStruct((BLOCKS, 80...  4.03 us
    pallas_call x1, Pallas kernels, middle_blocks(): pl.pallas_call(middle_kernel, out_shape=(jax.ShapeDtypeStruct((BLOCKS * 6...  3.19 us
    pallas_call x1, Pallas kernels, inverse_blocks(): pl.pallas_call(inverse_kernel, out_shape=(jax.ShapeDtypeStruct((4, BLOCK)...  2.22 us
  transfers between devices with their start and end apart: 4, of which 4 were waited for; matrix products, arithmetic and copies ran while one was open for 1% of the time, Pallas kernels for 1%

profile of v2, /device:TPU:32, one launch (start us, length us, event | category | flops | bytes accessed | tf_op | source)
XLA Modules:
  0.0 102.2 jit_solution(8991711443443120816)
XLA Ops:
  0.6 4.0 %forward_blocks.1 = f32[32,80,128]{2,1,0:T(8,128)} custom-call(f32[4,16384]{1,0:T(4,128)} %seq_ref.1, f32[4,16384]{1,0:T(4,128)} %cot_ref.1, f32[2,16384]{1,0:T(2,128)} %refs_2_.1, f32[512,256]{1,0:T(8,128)} %constant.16.clone.refs_3_, f32[256,256]{1,0:T(8,128)} %constant.17.clone.refs_4_, f32[2,256,128]{2,1,0:T(8,128)} %constant.18.clone.refs_5_.twist_ref), custom_call_target="tpu_custom_call" | custom-call | tf_op jit(solution)/shard_map/forward_blocks/pallas_call | solution.py:118
  4.7 0.0 copy-start.5
  4.7 0.0 copy-start.6
  4.7 0.0 copy-start.7
  4.7 43.6 %all_to_all.15 = f32[32,80,128]{2,1,0:T(8,128)S(1)} all-to-all(f32[32,80,128]{2,1,0:T(8,128)} %forward_blocks.1), channel_id=1, replica_groups=mesh['ctx'=32,'chan'=8] {'ctx'}, dimensions={0} | all-to-all | bytes 2621440 | tf_op jit(solution)/shard_map/all_to_all | solution.py:257
  48.3 0.0 copy-done.5
  48.3 0.0 copy-done.6
  48.3 0.0 copy-done.7
  48.4 3.2 %middle_blocks.1 = (f32[2048,128]{1,0:T(8,128)}, f32[512,128]{1,0:T(8,128)S(1)}) custom-call(f32[2560,128]{1,0:T(8,128)S(1)} %bitcast.4, f32[128,64]{1,0:T(8,128)S(1)} %copy-done.5, f32[64,128]{1,0:T(8,128)S(1)} %copy-done.6, f32[64,128]{1,0:T(8,128)S(1)} %copy-done.7), custom_call_target="tpu_custom_call" | custom-call | tf_op jit(solution)/shard_map/middle_blocks/pallas_call | solution.py:175
  51.5 0.0 copy-start
  51.5 0.0 copy-start.1
  51.5 0.0 copy-start.4
  51.6 15.7 %all_to_all.16.in_ref = f32[32,16,128]{2,1,0:T(8,128)S(1)} all-to-all(f32[32,16,128]{2,1,0:T(8,128)S(1)} %bitcast.5), channel_id=1, replica_groups=mesh['ctx'=32,'chan'=8] {'ctx'}, dimensions={0} | all-to-all | bytes 524288 | tf_op jit(solution)/shard_map/all_to_all | solution.py:257
  67.3 4.6 %all-to-all-start.2 = ((f32[32,64,128]{2,1,0:T(8,128)}), f32[32,64,128]{2,1,0:T(8,128)S(1)}, u32[]{:S(2)}, u32[]{:S(2)}) async-start(f32[32,64,128]{2,1,0:T(8,128)} %bitcast.2), calls=%async_computation.2 | async-start | bytes 2097152 | tf_op jit(solution)/shard_map/all_to_all | solution.py:257
  71.8 0.0 copy-done
  71.8 0.0 copy-done.1
  71.8 0.0 copy-done.4
  71.8 0.0 copy-start.8
  71.9 0.0 copy-start.2
  71.9 0.0 copy-start.3
  71.9 0.9 taps_blocks.1
  72.8 1.6 %collective-permute-start = (f32[2,16384]{1,0:T(2,128)S(1)}, f32[2,16384]{1,0:T(2,128)S(1)}, u32[]{:S(2)}, u32[]{:S(2)}) collective-permute-start(f32[2,16384]{1,0:T(2,128)S(1)} %taps_blocks.1), channel_id=1, source_target_pairs={{0,1},{1,0},{2,3},{3,2},{4,5},{5,4},{6,7},{7,6},{8,9},{9,8},{10,11... | collective-permute-start | bytes 393224 | tf_op jit(solution)/shard_map/ppermute | solution.py:263
  74.4 4.1 %collective-permute-done = f32[2,16384]{1,0:T(2,128)S(1)} collective-permute-done((f32[2,16384]{1,0:T(2,128)S(1)}, f32[2,16384]{1,0:T(2,128)S(1)}, u32[]{:S(2)}, u32[]{:S(2)}) %collective-permute-start) | collective-permute-done | bytes 131104 | tf_op jit(solution)/shard_map/ppermute | solution.py:263
  78.4 0.1 add.9
  78.5 2.9 %collective-permute-start.1 = (f32[2,16384]{1,0:T(2,128)S(1)}, f32[2,16384]{1,0:T(2,128)S(1)}, u32[]{:S(2)}, u32[]{:S(2)}) collective-permute-start(f32[2,16384]{1,0:T(2,128)S(1)} %add.9), channel_id=1, source_target_pairs={{0,3},{1,2},{2,1},{3,0},{4,7},{5,6},{6,5},{7,4},{8,11},{9,10},{10,... | collective-permute-start | bytes 393224 | tf_op jit(solution)/shard_map/ppermute | solution.py:263
  81.3 3.4 %collective-permute-done.1 = f32[2,16384]{1,0:T(2,128)S(1)} collective-permute-done((f32[2,16384]{1,0:T(2,128)S(1)}, f32[2,16384]{1,0:T(2,128)S(1)}, u32[]{:S(2)}, u32[]{:S(2)}) %collective-permute-start.1) | collective-permute-done | bytes 131104 | tf_op jit(solution)/shard_map/ppermute | solution.py:263
  84.7 0.1 add.10
  84.8 3.0 %collective-permute-start.2 = (f32[2,16384]{1,0:T(2,128)S(1)}, f32[2,16384]{1,0:T(2,128)S(1)}, u32[]{:S(2)}, u32[]{:S(2)}) collective-permute-start(f32[2,16384]{1,0:T(2,128)S(1)} %add.10), channel_id=1, source_target_pairs={{0,4},{1,5},{2,6},{3,7},{4,0},{5,1},{6,2},{7,3},{8,12},{9,13},{10,... | collective-permute-start | bytes 393224 | tf_op jit(solution)/shard_map/ppermute | solution.py:263
  87.8 0.0 copy-done.8
  87.8 0.1 copy.15.skip_ref
  87.9 5.1 %collective-permute-done.2 = f32[2,16384]{1,0:T(2,128)S(1)} collective-permute-done((f32[2,16384]{1,0:T(2,128)S(1)}, f32[2,16384]{1,0:T(2,128)S(1)}, u32[]{:S(2)}, u32[]{:S(2)}) %collective-permute-start.2) | collective-permute-done | bytes 131104 | tf_op jit(solution)/shard_map/ppermute | solution.py:263
  93.0 0.7 add.11
  93.7 6.2 %all-to-all-done.2.in_ref = f32[32,64,128]{2,1,0:T(8,128)S(1)} async-done(((f32[32,64,128]{2,1,0:T(8,128)}), f32[32,64,128]{2,1,0:T(8,128)S(1)}, u32[]{:S(2)}, u32[]{:S(2)}) %all-to-all-start.2) | async-done | bytes 1048608 | tf_op jit(solution)/shard_map/all_to_all | solution.py:257
  100.0 0.0 copy-done.2
  100.0 0.0 copy-done.3
  100.0 2.2 %inverse_blocks.1 = (f32[4,16384]{1,0:T(4,128)}, f32[4,16384]{1,0:T(4,128)}) custom-call(f32[32,64,128]{2,1,0:T(8,128)S(1)} %all-to-all-done.2.in_ref, f32[4,16384]{1,0:T(4,128)S(1)} %copy-done.2, f32[4,16384]{1,0:T(4,128)S(1)} %copy-done.3, f32[4,1]{1,0:T(4,128)S(1)} %copy.15.skip_ref, f32[256,256]{1,0:T(8,128)S(1)} %copy-done.4, f32[256,512]{1,0:T(8,128)S(1)} %copy-done.1, ...), custom_call_target="tpu_custom_call" | custom-call | tf_op jit(solution)/shard_map/inverse_blocks/pallas_call | solution.py:245
Async XLA Ops:
  4.7 43.7 %copy-start.5 = (f32[128,64]{1,0:T(8,128)S(1)}, f32[128,64]{1,0:T(8,128)}, u32[]{:S(2)}) copy-start(f32[128,64]{1,0:T(8,128)} %constant.19.clone.there_ref) | copy-start | bytes 98308
  4.7 43.7 %copy-start.6 = (f32[64,128]{1,0:T(8,128)S(1)}, f32[64,128]{1,0:T(8,128)}, u32[]{:S(2)}) copy-start(f32[64,128]{1,0:T(8,128)} %constant.20.clone.back_ref) | copy-start | bytes 98308
  4.7 43.7 %copy-start.7 = (f32[64,128]{1,0:T(8,128)S(1)}, f32[64,128]{1,0:T(8,128)}, u32[]{:S(2)}) copy-start(f32[64,128]{1,0:T(8,128)} %constant.21.clone.adjoint_ref) | copy-start | bytes 98308
  51.5 20.3 %copy-start = (f32[2,256,128]{2,1,0:T(8,128)S(1)}, f32[2,256,128]{2,1,0:T(8,128)}, u32[]{:S(2)}) copy-start(f32[2,256,128]{2,1,0:T(8,128)} %constant.18.clone.refs_5_.twist_ref) | copy-start | bytes 786436
  51.5 20.3 %copy-start.1 = (f32[256,512]{1,0:T(8,128)S(1)}, f32[256,512]{1,0:T(8,128)}, u32[]{:S(2)}) copy-start(f32[256,512]{1,0:T(8,128)} %constant.23.clone.outer_ref) | copy-start | bytes 1572868
  51.5 20.3 %copy-start.4 = (f32[256,256]{1,0:T(8,128)S(1)}, f32[256,256]{1,0:T(8,128)}, u32[]{:S(2)}) copy-start(f32[256,256]{1,0:T(8,128)} %constant.22.clone.inner_ref) | copy-start | bytes 786436
  67.3 32.7 %all-to-all-start.2 = ((f32[32,64,128]{2,1,0:T(8,128)}), f32[32,64,128]{2,1,0:T(8,128)S(1)}, u32[]{:S(2)}, u32[]{:S(2)}) async-start(f32[32,64,128]{2,1,0:T(8,128)} %bitcast.2), calls=%async_computation.2 | async-start | bytes 2097152 | tf_op jit(solution)/shard_map/all_to_all | solution.py:257
  71.8 16.0 %copy-start.8 = (f32[4]{0:T(128)S(1)}, f32[4]{0:T(128)}, u32[]{:S(2)}) copy-start(f32[4]{0:T(128)} %param.14) | copy-start | bytes 52
  71.9 28.1 %copy-start.2 = (f32[4,16384]{1,0:T(4,128)S(1)}, f32[4,16384]{1,0:T(4,128)}, u32[]{:S(2)}) copy-start(f32[4,16384]{1,0:T(4,128)} %seq_ref.1) | copy-start | bytes 786436
  71.9 28.1 %copy-start.3 = (f32[4,16384]{1,0:T(4,128)S(1)}, f32[4,16384]{1,0:T(4,128)}, u32[]{:S(2)}) copy-start(f32[4,16384]{1,0:T(4,128)} %cot_ref.1) | copy-start | bytes 786436
  72.8 5.6 %collective-permute-start = (f32[2,16384]{1,0:T(2,128)S(1)}, f32[2,16384]{1,0:T(2,128)S(1)}, u32[]{:S(2)}, u32[]{:S(2)}) collective-permute-start(f32[2,16384]{1,0:T(2,128)S(1)} %taps_blocks.1), channel_id=1, source_target_pairs={{0,1},{1,0},{2,3},{3,2},{4,5},{5,4},{6,7},{7,6},{8,9},{9,8},{10,11... | collective-permute-start | bytes 393224 | tf_op jit(solution)/shard_map/ppermute | solution.py:263
  78.5 6.3 %collective-permute-start.1 = (f32[2,16384]{1,0:T(2,128)S(1)}, f32[2,16384]{1,0:T(2,128)S(1)}, u32[]{:S(2)}, u32[]{:S(2)}) collective-permute-start(f32[2,16384]{1,0:T(2,128)S(1)} %add.9), channel_id=1, source_target_pairs={{0,3},{1,2},{2,1},{3,0},{4,7},{5,6},{6,5},{7,4},{8,11},{9,10},{10,... | collective-permute-start | bytes 393224 | tf_op jit(solution)/shard_map/ppermute | solution.py:263
  84.8 8.2 %collective-permute-start.2 = (f32[2,16384]{1,0:T(2,128)S(1)}, f32[2,16384]{1,0:T(2,128)S(1)}, u32[]{:S(2)}, u32[]{:S(2)}) collective-permute-start(f32[2,16384]{1,0:T(2,128)S(1)} %add.10), channel_id=1, source_target_pairs={{0,4},{1,5},{2,6},{3,7},{4,0},{5,1},{6,2},{7,3},{8,12},{9,13},{10,... | collective-permute-start | bytes 393224 | tf_op jit(solution)/shard_map/ppermute | solution.py:263

commit v3 on v2

v3 whole, which is shorter than its diff:
```python
import numpy as np
import jax
import jax.numpy as jnp
from jax import lax
from jax.experimental import pallas as pl
from jax.experimental.pallas import tpu as pltpu
from jax.sharding import PartitionSpec as P

SIDE = 128
BLOCK = SIDE * SIDE
BLOCKS = 32
SUB = SIDE // BLOCKS
POINTS = 2 * BLOCKS
CHAN = 8
OUT_ROWS = 66
BACK_ROWS = 64
TAPS_ROWS = 16
PAIRS = ((0, 2), (1, 3), (4, 6), (5, 7), (8, 9))
VMEM_LIMIT = 40 * 1024 * 1024
VMEM_FULL = 60 * 1024 * 1024


def make_tables():
    digit = np.arange(SIDE)
    turn = 2.0 * np.pi
    single = np.float32
    angle = turn * ((digit[:, None] + 0.25) * digit[None, :] / SIDE)
    cosine, sine = np.cos(angle), np.sin(angle)
    forward_outer = np.concatenate([cosine, -sine], axis=0)
    factor = (BLOCKS * BLOCK) ** (-0.5) / BLOCK
    inverse_outer = factor * np.concatenate([cosine.T, -sine.T], axis=1)
    angle = turn * ((digit[:, None] + 0.25) * digit[None, :] / BLOCK)
    twist = np.stack([np.cos(angle), np.sin(angle)])
    angle = turn * ((digit[:, None] * digit[None, :]) % SIDE / SIDE)
    cosine, sine = np.cos(angle), np.sin(angle)
    forward_inner = np.block([[cosine, -sine], [sine, cosine]])
    inverse_inner = np.block([[cosine, sine], [-sine, cosine]])
    return (
        tuple(t.astype(single) for t in (forward_outer, forward_inner, twist)),
        tuple(t.astype(single) for t in (inverse_inner, inverse_outer, twist)),
    )


def make_block_tables():
    block = np.arange(BLOCKS)
    point = np.arange(POINTS)
    angle = 2.0 * np.pi * ((point[:, None] * block[None, :]) % POINTS) / POINTS
    cosine, sine = np.cos(angle), np.sin(angle)
    tables = [np.block([[cosine, sine], [-sine, cosine]])]
    step = np.exp(-2j * np.pi * point / POINTS)
    for spill in (1.0 + 1j * step, 1.0 - 1j * np.conj(step)):
        back = np.exp(1j * angle.T) * spill[None, :] / POINTS
        tables.append(np.block([[back.real, -back.imag], [back.imag, back.real]]))
    return tuple(t.astype(np.float32) for t in tables)


FORWARD_TABLES, INVERSE_TABLES = make_tables()
THERE, BACK, ADJOINT = make_block_tables()


def split(values):
    high = values.astype(jnp.bfloat16)
    return high, (values - high.astype(jnp.float32)).astype(jnp.bfloat16)


def dot(left, right):
    return jnp.dot(left, right, preferred_element_type=jnp.float32)


def dot_three(left, right):
    (lh, ll), (rh, rl) = split(left), split(right)
    return dot(lh, rh) + (dot(lh, rl) + dot(ll, rh))


def dot_wide(left, right):
    (lh, ll), (rh, rl) = split(left), split(right)
    return dot(jnp.concatenate([lh, lh, ll], axis=1), jnp.concatenate([rh, rl, rh], axis=0))


def call(kernel, name, out_shape, operands, scratch=(), own_copies=False):
    space = pl.ANY if own_copies else pltpu.VMEM
    many = isinstance(out_shape[0], tuple)
    shapes = tuple(jax.ShapeDtypeStruct(s, jnp.float32) for s in (out_shape if many else (out_shape,)))
    outs = (pl.BlockSpec(memory_space=pltpu.VMEM),) * len(shapes)
    return pl.pallas_call(
        kernel,
        out_shape=shapes if many else shapes[0],
        in_specs=[pl.BlockSpec(memory_space=space)] * len(operands),
        out_specs=outs if many else outs[0],
        scratch_shapes=list(scratch),
        compiler_params=pltpu.CompilerParams(vmem_limit_bytes=VMEM_FULL if own_copies else VMEM_LIMIT),
        name=name,
    )(*operands)


def spread(source, rows, first, count):
    for a in range(SIDE):
        rows[pl.ds(first * SIDE + a, count, stride=SIDE), :] = source[:, a * SIDE : (a + 1) * SIDE]


def forward_kernel(*refs):
    sources, out_ref, held, rows, spectra, sems = refs[:6], refs[6], refs[7:13], refs[13], refs[14], refs[15]
    copies = [pltpu.make_async_copy(s, h, sems.at[i]) for i, (s, h) in enumerate(zip(sources, held))]
    for copy in copies:
        copy.start()
    seq_ref, cot_ref, taps_ref, outer_ref, inner_ref, twist_ref = held
    copies[0].wait()
    spread(seq_ref, rows, 0, 4)
    copies[1].wait()
    spread(cot_ref, rows, 4, 4)
    copies[2].wait()
    spread(taps_ref, rows, 8, 2)
    for copy in copies[3:]:
        copy.wait()

    signals = jnp.concatenate([rows[i * SIDE : (i + 1) * SIDE, :] for i in range(10)], axis=1)
    opened = dot_wide(outer_ref[...], signals)
    cosine, sine = twist_ref[0], twist_ref[1]
    inner = inner_ref[...]
    chan = lax.axis_index("chan")
    for p, pair in enumerate(PAIRS):
        twisted = []
        for i in pair:
            real = opened[:SIDE, i * SIDE : (i + 1) * SIDE]
            imag = opened[SIDE:, i * SIDE : (i + 1) * SIDE]
            twisted.append(jnp.concatenate([real * cosine + imag * sine, imag * cosine - real * sine], axis=1))
        spectrum = dot_three(jnp.concatenate(twisted, axis=0), inner)
        for h in range(2):
            held_rows = spectra.at[2 * p + h]
            held_rows[...] = spectrum[:, h * SIDE : (h + 1) * SIDE]
            picked = [held_rows[pl.ds((r // SUB) * SIDE + r % SUB, BLOCKS, stride=SUB), :] for r in range(8)]
            if p < 4:
                for r in range(8):
                    out_ref[pl.ds(16 * p + 8 * h + r, BLOCKS, stride=OUT_ROWS), :] = picked[r]
            else:
                share = picked[0]
                for r in range(1, 8):
                    share = jnp.where(chan == r, picked[r], share)
                out_ref[pl.ds(64 + h, BLOCKS, stride=OUT_ROWS), :] = share


def forward_blocks(sequence, cotangent, taps):
    operands = (sequence, cotangent, taps) + tuple(jnp.asarray(t) for t in FORWARD_TABLES)
    scratch = [pltpu.VMEM(v.shape, v.dtype) for v in operands] + [
        pltpu.VMEM((10 * SIDE, SIDE), jnp.float32),
        pltpu.VMEM((10, 2 * SIDE, SIDE), jnp.float32),
        pltpu.SemaphoreType.DMA((6,)),
    ]
    return call(forward_kernel, "forward_blocks", (BLOCKS * OUT_ROWS, SIDE), operands, scratch, True)


def points_of(in_ref, there, p):
    halves = [
        jnp.concatenate(
            [in_ref[pl.ds(16 * p + 8 * h + r, BLOCKS, stride=OUT_ROWS), :] for r in range(8)], axis=1
        )
        for h in range(2)
    ]
    points = dot_wide(there, jnp.concatenate(halves, axis=0))
    return points[:POINTS], points[POINTS:]


def blocks_of(ref, p, width, table, real, imag):
    blocks = dot_wide(table, jnp.concatenate([real, imag], axis=0))
    for h in range(2):
        for r in range(8):
            ref[pl.ds(16 * p + 8 * h + r, BLOCKS, stride=width), :] = blocks[
                BLOCKS * h : BLOCKS * (h + 1), r * SIDE : (r + 1) * SIDE
            ]


def taps_products_kernel(in_ref, there_ref, adjoint_ref, taps_ref, share_ref):
    for h in range(2):
        share_ref[BLOCKS * h : BLOCKS * (h + 1), :] = in_ref[pl.ds(64 + h, BLOCKS, stride=OUT_ROWS), :]
    there = there_ref[...]
    real = imag = 0.0
    for q in range(2):
        xr, xi = points_of(in_ref, there, q)
        gr, gi = points_of(in_ref, there, 2 + q)
        real = real + (xr * gr + xi * gi)
        imag = imag + (xr * gi - xi * gr)
    blocks_of(taps_ref, 0, TAPS_ROWS, adjoint_ref[...], real, imag)


def taps_products(spectra):
    operands = (spectra, jnp.asarray(THERE), jnp.asarray(ADJOINT))
    return call(
        taps_products_kernel, "taps_products", ((BLOCKS * TAPS_ROWS, SIDE), (2 * BLOCKS, SIDE)), operands
    )


def products_kernel(*refs):
    in_ref, shares = refs[0], refs[1 : 1 + CHAN]
    there_ref, back_ref, adjoint_ref, out_ref, taps = refs[1 + CHAN :]
    chan = lax.axis_index("chan")
    for flip in range(CHAN):
        taps[chan ^ flip] = shares[flip][...]
    there, back, adjoint = there_ref[...], back_ref[...], adjoint_ref[...]
    points = dot_wide(there, jnp.concatenate([taps[r] for r in range(8)], axis=1))
    hr, hi = points[:POINTS], points[POINTS:]
    for q in range(2):
        xr, xi = points_of(in_ref, there, q)
        blocks_of(out_ref, q, BACK_ROWS, back, hr * xr - hi * xi, hr * xi + hi * xr)
        gr, gi = points_of(in_ref, there, 2 + q)
        blocks_of(out_ref, 2 + q, BACK_ROWS, adjoint, hr * gr + hi * gi, hr * gi - hi * gr)


def products(spectra, shares):
    operands = (spectra, *shares) + tuple(jnp.asarray(t) for t in (THERE, BACK, ADJOINT))
    scratch = [pltpu.VMEM((CHAN, 2 * BLOCKS, SIDE), jnp.float32)]
    return call(products_kernel, "products", (BLOCKS * BACK_ROWS, SIDE), operands, scratch)


def close(in_ref, inner_ref, outer_ref, twist_ref, gathered, rows, pairs, width):
    count = 2 * len(pairs)
    for p, pair in enumerate(pairs):
        for h in range(2):
            for r in range(8):
                gathered[h, pl.ds(pair[r // SUB] * SIDE + r % SUB, BLOCKS, stride=SUB), :] = in_ref[
                    pl.ds(16 * p + 8 * h + r, BLOCKS, stride=width), :
                ]
    turned = dot_three(jnp.concatenate([gathered[0], gathered[1]], axis=1), inner_ref[...])
    cosine, sine = twist_ref[0], twist_ref[1]
    columns = []
    for i in range(count):
        real = turned[i * SIDE : (i + 1) * SIDE, :SIDE]
        imag = turned[i * SIDE : (i + 1) * SIDE, SIDE:]
        columns.append(jnp.concatenate([real * cosine - imag * sine, imag * cosine + real * sine], axis=0))
    closed = dot_three(outer_ref[...], jnp.concatenate(columns, axis=1))
    for i in range(count):
        rows[i * SIDE : (i + 1) * SIDE, :] = closed[:, i * SIDE : (i + 1) * SIDE]


def taps_kernel(in_ref, inner_ref, outer_ref, twist_ref, f_ref, gathered, rows):
    close(in_ref, inner_ref, outer_ref, twist_ref, gathered, rows, ((0, 1),), TAPS_ROWS)
    for a in range(SIDE):
        f_ref[:, a * SIDE : (a + 1) * SIDE] = rows[pl.ds(a, 2, stride=SIDE), :]


def inverse_kernel(in_ref, seq_ref, cot_ref, skip_ref, inner_ref, outer_ref, twist_ref, y_ref, g_ref, gathered, rows):
    close(in_ref, inner_ref, outer_ref, twist_ref, gathered, rows, PAIRS[:4], BACK_ROWS)
    skip = jnp.broadcast_to(skip_ref[...], (4, SIDE))
    for a in range(SIDE):
        lanes = slice(a * SIDE, (a + 1) * SIDE)
        y_ref[:, lanes] = rows[pl.ds(a, 4, stride=SIDE), :] + skip * seq_ref[:, lanes]
        g_ref[:, lanes] = rows[pl.ds(4 * SIDE + a, 4, stride=SIDE), :] + skip * cot_ref[:, lanes]


def close_scratch(count):
    return [pltpu.VMEM((2, count * SIDE, SIDE), jnp.float32), pltpu.VMEM((count * SIDE, SIDE), jnp.float32)]


def taps_blocks(spectra):
    operands = (spectra,) + tuple(jnp.asarray(t) for t in INVERSE_TABLES)
    return call(taps_kernel, "taps_blocks", (2, BLOCK), operands, close_scratch(2))


def inverse_blocks(spectra, sequence, cotangent, skip_gain):
    operands = (spectra, sequence, cotangent, skip_gain[:, None]) + tuple(jnp.asarray(t) for t in INVERSE_TABLES)
    return call(inverse_kernel, "inverse_blocks", ((4, BLOCK), (4, BLOCK)), operands, close_scratch(8))


def exchange(blocks):
    rows = blocks.shape[0] // BLOCKS
    tall = 1 if rows % 8 else 8
    cut = blocks.reshape(BLOCKS, rows // tall, tall, SIDE)
    return lax.all_to_all(cut, "ctx", split_axis=0, concat_axis=0, tiled=True).reshape(blocks.shape)


def flip_chan(values, flip):
    return lax.ppermute(values, "chan", [(i, i ^ flip) for i in range(CHAN)])


def sum_over_chan(values):
    for flip in (1, 3, 4):
        values = values + flip_chan(values, flip)
    return values


def body(sequence, filter_taps, skip_gain, cotangent):
    spectra = exchange(forward_blocks(sequence, cotangent, filter_taps))
    taps, share = taps_products(spectra)
    taps = exchange(taps)
    shares = [share] + [flip_chan(share, flip) for flip in (1, 2, 3)]
    shares = shares + [flip_chan(s, 4) for s in shares]
    back = products(spectra, shares)
    taps, back = lax.optimization_barrier((taps, back))
    taps_grad = sum_over_chan(taps_blocks(taps))
    convolved, seq_grad = inverse_blocks(exchange(back), sequence, cotangent, skip_gain)
    return convolved, seq_grad, taps_grad


def solution(mesh):
    return jax.shard_map(
        body,
        mesh=mesh,
        in_specs=(P("chan", "ctx"), P(None, "ctx"), P("chan"), P("chan", "ctx")),
        out_specs=(P("chan", "ctx"), P("chan", "ctx"), P(None, "ctx")),
        check_vma=False,
    )
```

time: 104 us -> 110 us (1.058)
  blocking collectives: 59.3 us -> 39.4 us
  starting transfers between devices: 12 us -> 30.1 us
  waiting for transfers between devices: 18.8 us -> 25.5 us
  Pallas kernels: 10.3 us -> 11.5 us
    all_to_all x2 -> x1, blocking collectives: 59.3 us -> 39.4 us  [exchange(): lax.all_to_all(cut, 'ctx', split_axis=0, concat_axis=0, tiled=True)]
    ppermute x3 -> x10, starting transfers between devices: 7.43 us -> 17.5 us  [flip_chan(): return lax.ppermute(values, 'chan', [(i, i ^ flip) for i in range(CHAN)])]
    all_to_all x1 -> x2, starting transfers between devices: 4.55 us -> 12.5 us  [exchange(): lax.all_to_all(cut, 'ctx', split_axis=0, concat_axis=0, tiled=True)]
    ppermute x3 -> x10, waiting for transfers between devices: 12.6 us -> 17.6 us  [flip_chan(): return lax.ppermute(values, 'chan', [(i, i ^ flip) for i in range(CHAN)])]
    all_to_all x1 -> x2, waiting for transfers between devices: 6.22 us -> 7.88 us  [exchange(): lax.all_to_all(cut, 'ctx', split_axis=0, concat_axis=0, tiled=True)]
    pallas_call x4 -> x5, Pallas kernels: 10.3 us -> 11.5 us  [call(): pl.pallas_call(kernel, out_shape=shapes if many else shapes[0], in_specs=...]
  transfers between devices with their start and end apart: 4 -> 12, of which waited for: 4 -> 7; matrix products, arithmetic and copies ran while one was open for 1% -> 1% of each run, Pallas kernels for 1% -> 3%
where the time goes in v3:
time: 110 us; the launch traced here: 108 us
  blocking collectives  39.4 us (36%)
  starting transfers between devices  30.1 us (27%)
  waiting for transfers between devices  25.5 us (23%)
  Pallas kernels  11.5 us (10%)
    all_to_all x1, blocking collectives, exchange(): lax.all_to_all(cut, 'ctx', split_axis=0, concat_axis=0, tiled=True)  39.4 us
    ppermute x10, waiting for transfers between devices, flip_chan(): return lax.ppermute(values, 'chan', [(i, i ^ flip) for i in range(CHAN)])  17.6 us
    ppermute x10, starting transfers between devices, flip_chan(): return lax.ppermute(values, 'chan', [(i, i ^ flip) for i in range(CHAN)])  17.5 us
    all_to_all x2, starting transfers between devices, exchange(): lax.all_to_all(cut, 'ctx', split_axis=0, concat_axis=0, tiled=True)  12.5 us
    pallas_call x5, Pallas kernels, call(): pl.pallas_call(kernel, out_shape=shapes if many else shapes[0], in_specs=...  11.5 us
    all_to_all x2, waiting for transfers between devices, exchange(): lax.all_to_all(cut, 'ctx', split_axis=0, concat_axis=0, tiled=True)  7.88 us
  transfers between devices with their start and end apart: 12, of which 7 were waited for; matrix products, arithmetic and copies ran while one was open for 1% of the time, Pallas kernels for 3%

profile of v3, /device:TPU:32, one launch (start us, length us, event | category | flops | bytes accessed | tf_op | source)
XLA Modules:
  0.0 108.2 jit_solution(15046825862881242188)
XLA Ops:
  0.6 3.6 %forward_blocks.1 = f32[2112,128]{1,0:T(8,128)} custom-call(f32[4,16384]{1,0:T(4,128)} %seq_ref.1, f32[4,16384]{1,0:T(4,128)} %cot_ref.1, f32[2,16384]{1,0:T(2,128)} %refs_2_.1, f32[256,128]{1,0:T(8,128)} %constant.16.clone.refs_3_, f32[256,256]{1,0:T(8,128)} %constant.17.clone.refs_4_, f32[2,128,128]{2,1,0:T(8,128)} %constant.18.clone.refs_5_.twist_ref), custom_call_target="tpu_custom_call" | custom-call | tf_op jit(solution)/shard_map/forward_blocks/pallas_call | solution.py:85
  4.2 0.0 copy-start.5
  4.2 0.0 copy-start.6
  4.2 39.4 %all_to_all.15 = f32[32,66,1,128]{3,2,1,0:T(1,128)S(1)} all-to-all(f32[32,66,1,128]{3,2,1,0:T(1,128)} %bitcast.11), channel_id=1, replica_groups=mesh['ctx'=32,'chan'=8] {'ctx'}, dimensions={0} | all-to-all | bytes 2162688 | tf_op jit(solution)/shard_map/all_to_all | solution.py:267
  43.7 0.0 copy-start.7
  43.7 0.0 copy-done.5
  43.7 0.0 copy-done.6
  43.7 1.5 %taps_products.1 = (f32[512,128]{1,0:T(8,128)}, f32[64,128]{1,0:T(8,128)S(1)}) custom-call(f32[2112,128]{1,0:T(8,128)S(1)} %bitcast.7, f32[128,64]{1,0:T(8,128)S(1)} %copy-done.5, f32[64,128]{1,0:T(8,128)S(1)} %copy-done.6), custom_call_target="tpu_custom_call" | custom-call | tf_op jit(solution)/shard_map/taps_products/pallas_call | solution.py:85
  45.2 4.6 %all-to-all-start.1 = ((f32[32,2,8,128]{3,2,1,0:T(8,128)}), f32[32,2,8,128]{3,2,1,0:T(8,128)S(1)}, u32[]{:S(2)}, u32[]{:S(2)}) async-start(f32[32,2,8,128]{3,2,1,0:T(8,128)} %bitcast.2), calls=%async_computation.1 | async-start | bytes 524288 | tf_op jit(solution)/shard_map/all_to_all | solution.py:267
  49.8 1.6 %collective-permute-start = (f32[64,128]{1,0:T(8,128)S(1)}, f32[64,128]{1,0:T(8,128)S(1)}, u32[]{:S(2)}, u32[]{:S(2)}) collective-permute-start(f32[64,128]{1,0:T(8,128)S(1)} %get-tuple-element.10.refs_1_), channel_id=1, source_target_pairs={{0,1},{1,0},{2,3},{3,2},{4,5},{5,4},{6,7},{7,6},{8,9},{9,8},{10,11... | collective-permute-start | bytes 98312 | tf_op jit(solution)/shard_map/ppermute | solution.py:271
  51.4 2.7 %collective-permute-start.1 = (f32[64,128]{1,0:T(8,128)S(1)}, f32[64,128]{1,0:T(8,128)S(1)}, u32[]{:S(2)}, u32[]{:S(2)}) collective-permute-start(f32[64,128]{1,0:T(8,128)S(1)} %get-tuple-element.10.refs_1_), channel_id=1, source_target_pairs={{0,2},{1,3},{2,0},{3,1},{4,6},{5,7},{6,4},{7,5},{8,10},{9,11},{10,... | collective-permute-start | bytes 98312 | tf_op jit(solution)/shard_map/ppermute | solution.py:271
  54.1 0.5 collective-permute-start.2
  54.6 2.9 %collective-permute-start.3 = (f32[64,128]{1,0:T(8,128)S(1)}, f32[64,128]{1,0:T(8,128)S(1)}, u32[]{:S(2)}, u32[]{:S(2)}) collective-permute-start(f32[64,128]{1,0:T(8,128)S(1)} %get-tuple-element.10.refs_1_), channel_id=1, source_target_pairs={{0,4},{1,5},{2,6},{3,7},{4,0},{5,1},{6,2},{7,3},{8,12},{9,13},{10,... | collective-permute-start | bytes 98312 | tf_op jit(solution)/shard_map/ppermute | solution.py:271
  57.5 0.0 collective-permute-done.refs_2_
  57.5 0.6 collective-permute-start.4
  58.2 0.0 collective-permute-done.1.refs_3_
  58.2 2.9 %collective-permute-start.5 = (f32[64,128]{1,0:T(8,128)S(1)}, f32[64,128]{1,0:T(8,128)S(1)}, u32[]{:S(2)}, u32[]{:S(2)}) collective-permute-start(f32[64,128]{1,0:T(8,128)S(1)} %collective-permute-done.1.refs_3_), channel_id=1, source_target_pairs={{0,4},{1,5},{2,6},{3,7},{4,0},{5,1},{6,2},{7,3},{8,12},{9,13},{10,... | collective-permute-start | bytes 98312 | tf_op jit(solution)/shard_map/ppermute | solution.py:271
  61.1 0.0 collective-permute-done.2.refs_4_
  61.1 1.1 %collective-permute-start.6 = (f32[64,128]{1,0:T(8,128)S(1)}, f32[64,128]{1,0:T(8,128)S(1)}, u32[]{:S(2)}, u32[]{:S(2)}) collective-permute-start(f32[64,128]{1,0:T(8,128)S(1)} %collective-permute-done.2.refs_4_), channel_id=1, source_target_pairs={{0,4},{1,5},{2,6},{3,7},{4,0},{5,1},{6,2},{7,3},{8,12},{9,13},{10,... | collective-permute-start | bytes 98312 | tf_op jit(solution)/shard_map/ppermute | solution.py:271
  62.2 0.0 collective-permute-done.3.refs_5_
  62.2 0.8 collective-permute-done.4.refs_6_
  63.0 0.6 collective-permute-done.5.refs_7_
  63.6 2.9 %collective-permute-done.6.refs_8_ = f32[64,128]{1,0:T(8,128)S(1)} collective-permute-done((f32[64,128]{1,0:T(8,128)S(1)}, f32[64,128]{1,0:T(8,128)S(1)}, u32[]{:S(2)}, u32[]{:S(2)}) %collective-permute-start.6) | collective-permute-done | bytes 32800 | tf_op jit(solution)/shard_map/ppermute | solution.py:271
  66.5 0.0 copy-done.7
  66.5 3.0 %products.1 = f32[2048,128]{1,0:T(8,128)} custom-call(f32[2112,128]{1,0:T(8,128)S(1)} %bitcast.8, f32[64,128]{1,0:T(8,128)S(1)} %get-tuple-element.10.refs_1_, f32[64,128]{1,0:T(8,128)S(1)} %collective-permute-done.refs_2_, f32[64,128]{1,0:T(8,128)S(1)} %collective-permute-done.1.refs_3_, f32[64,128]{1,0:T(8,128)S(1)} %collective-permute-done.2.refs_4_, ...), custom_call_target="tpu_custom_call" | custom-call | tf_op jit(solution)/shard_map/products/pallas_call | solution.py:85
  69.5 0.0 copy-start
  69.5 0.0 copy-start.3
  69.5 0.0 copy-start.4
  69.5 0.0 all-to-all-done.1
  69.5 7.9 %all-to-all-start.2 = ((f32[32,8,8,128]{3,2,1,0:T(8,128)}), f32[32,8,8,128]{3,2,1,0:T(8,128)S(1)}, u32[]{:S(2)}, u32[]{:S(2)}) async-start(f32[32,8,8,128]{3,2,1,0:T(8,128)} %bitcast.4), calls=%async_computation.2 | async-start | bytes 2097152 | tf_op jit(solution)/shard_map/all_to_all | solution.py:267
  77.4 0.0 copy-done
  77.4 0.0 copy-done.3
  77.4 0.0 copy-done.4
  77.5 0.0 copy-start.8
  77.5 0.0 copy-start.1
  77.5 0.0 copy-start.2
  77.5 0.7 taps_blocks.1
  78.2 0.4 collective-permute-start.7
  78.5 5.3 %collective-permute-done.7 = f32[2,16384]{1,0:T(2,128)S(1)} collective-permute-done((f32[2,16384]{1,0:T(2,128)S(1)}, f32[2,16384]{1,0:T(2,128)S(1)}, u32[]{:S(2)}, u32[]{:S(2)}) %collective-permute-start.7) | collective-permute-done | bytes 131104 | tf_op jit(solution)/shard_map/ppermute | solution.py:271
  83.8 0.1 add.9
  83.9 2.9 %collective-permute-start.8 = (f32[2,16384]{1,0:T(2,128)S(1)}, f32[2,16384]{1,0:T(2,128)S(1)}, u32[]{:S(2)}, u32[]{:S(2)}) collective-permute-start(f32[2,16384]{1,0:T(2,128)S(1)} %add.9), channel_id=1, source_target_pairs={{0,3},{1,2},{2,1},{3,0},{4,7},{5,6},{6,5},{7,4},{8,11},{9,10},{10,... | collective-permute-start | bytes 393224 | tf_op jit(solution)/shard_map/ppermute | solution.py:271
  86.8 3.4 %collective-permute-done.8 = f32[2,16384]{1,0:T(2,128)S(1)} collective-permute-done((f32[2,16384]{1,0:T(2,128)S(1)}, f32[2,16384]{1,0:T(2,128)S(1)}, u32[]{:S(2)}, u32[]{:S(2)}) %collective-permute-start.8) | collective-permute-done | bytes 131104 | tf_op jit(solution)/shard_map/ppermute | solution.py:271
  90.1 0.1 add.10
  90.2 1.9 %collective-permute-start.9 = (f32[2,16384]{1,0:T(2,128)S(1)}, f32[2,16384]{1,0:T(2,128)S(1)}, u32[]{:S(2)}, u32[]{:S(2)}) collective-permute-start(f32[2,16384]{1,0:T(2,128)S(1)} %add.10), channel_id=1, source_target_pairs={{0,4},{1,5},{2,6},{3,7},{4,0},{5,1},{6,2},{7,3},{8,12},{9,13},{10,... | collective-permute-start | bytes 393224 | tf_op jit(solution)/shard_map/ppermute | solution.py:271
  92.1 0.0 copy-done.8
  92.1 0.1 copy.19.skip_ref
  92.2 4.6 %collective-permute-done.9 = f32[2,16384]{1,0:T(2,128)S(1)} collective-permute-done((f32[2,16384]{1,0:T(2,128)S(1)}, f32[2,16384]{1,0:T(2,128)S(1)}, u32[]{:S(2)}, u32[]{:S(2)}) %collective-permute-start.9) | collective-permute-done | bytes 131104 | tf_op jit(solution)/shard_map/ppermute | solution.py:271
  96.9 0.7 add.11
  97.6 7.9 %all-to-all-done.2 = f32[32,8,8,128]{3,2,1,0:T(8,128)S(1)} async-done(((f32[32,8,8,128]{3,2,1,0:T(8,128)}), f32[32,8,8,128]{3,2,1,0:T(8,128)S(1)}, u32[]{:S(2)}, u32[]{:S(2)}) %all-to-all-start.2) | async-done | bytes 1048608 | tf_op jit(solution)/shard_map/all_to_all | solution.py:267
  105.5 0.0 copy-done.1
  105.5 0.0 copy-done.2
  105.5 2.7 %inverse_blocks.1 = (f32[4,16384]{1,0:T(4,128)}, f32[4,16384]{1,0:T(4,128)}) custom-call(f32[2048,128]{1,0:T(8,128)S(1)} %bitcast.9, f32[4,16384]{1,0:T(4,128)S(1)} %copy-done.1, f32[4,16384]{1,0:T(4,128)S(1)} %copy-done.2, f32[4,1]{1,0:T(4,128)S(1)} %copy.19.skip_ref, f32[256,256]{1,0:T(8,128)S(1)} %copy-done.3, f32[128,256]{1,0:T(8,128)S(1)} %copy-done.4, ...), custom_call_target="tpu_custom_call" | custom-call | tf_op jit(solution)/shard_map/inverse_blocks/pallas_call | solution.py:85
Async XLA Ops:
  4.2 39.4 %copy-start.5 = (f32[128,64]{1,0:T(8,128)S(1)}, f32[128,64]{1,0:T(8,128)}, u32[]{:S(2)}) copy-start(f32[128,64]{1,0:T(8,128)} %constant.19.clone.there_ref.refs_9_) | copy-start | bytes 98308
  4.2 39.4 %copy-start.6 = (f32[64,128]{1,0:T(8,128)S(1)}, f32[64,128]{1,0:T(8,128)}, u32[]{:S(2)}) copy-start(f32[64,128]{1,0:T(8,128)} %constant.20.clone.adjoint_ref.refs_11_) | copy-start | bytes 98308
  43.7 22.8 %copy-start.7 = (f32[64,128]{1,0:T(8,128)S(1)}, f32[64,128]{1,0:T(8,128)}, u32[]{:S(2)}) copy-start(f32[64,128]{1,0:T(8,128)} %constant.21.clone.refs_10_) | copy-start | bytes 98308
  45.2 24.3 %all-to-all-start.1 = ((f32[32,2,8,128]{3,2,1,0:T(8,128)}), f32[32,2,8,128]{3,2,1,0:T(8,128)S(1)}, u32[]{:S(2)}, u32[]{:S(2)}) async-start(f32[32,2,8,128]{3,2,1,0:T(8,128)} %bitcast.2), calls=%async_computation.1 | async-start | bytes 524288 | tf_op jit(solution)/shard_map/all_to_all | solution.py:267
  49.8 7.7 %collective-permute-start = (f32[64,128]{1,0:T(8,128)S(1)}, f32[64,128]{1,0:T(8,128)S(1)}, u32[]{:S(2)}, u32[]{:S(2)}) collective-permute-start(f32[64,128]{1,0:T(8,128)S(1)} %get-tuple-element.10.refs_1_), channel_id=1, source_target_pairs={{0,1},{1,0},{2,3},{3,2},{4,5},{5,4},{6,7},{7,6},{8,9},{9,8},{10,11... | collective-permute-start | bytes 98312 | tf_op jit(solution)/shard_map/ppermute | solution.py:271
  51.4 6.7 %collective-permute-start.1 = (f32[64,128]{1,0:T(8,128)S(1)}, f32[64,128]{1,0:T(8,128)S(1)}, u32[]{:S(2)}, u32[]{:S(2)}) collective-permute-start(f32[64,128]{1,0:T(8,128)S(1)} %get-tuple-element.10.refs_1_), channel_id=1, source_target_pairs={{0,2},{1,3},{2,0},{3,1},{4,6},{5,7},{6,4},{7,5},{8,10},{9,11},{10,... | collective-permute-start | bytes 98312 | tf_op jit(solution)/shard_map/ppermute | solution.py:271
  54.1 6.9 %collective-permute-start.2 = (f32[64,128]{1,0:T(8,128)S(1)}, f32[64,128]{1,0:T(8,128)S(1)}, u32[]{:S(2)}, u32[]{:S(2)}) collective-permute-start(f32[64,128]{1,0:T(8,128)S(1)} %get-tuple-element.10.refs_1_), channel_id=1, source_target_pairs={{0,3},{1,2},{2,1},{3,0},{4,7},{5,6},{6,5},{7,4},{8,11},{9,10},{10,... | collective-permute-start | bytes 98312 | tf_op jit(solution)/shard_map/ppermute | solution.py:271
  54.6 7.6 %collective-permute-start.3 = (f32[64,128]{1,0:T(8,128)S(1)}, f32[64,128]{1,0:T(8,128)S(1)}, u32[]{:S(2)}, u32[]{:S(2)}) collective-permute-start(f32[64,128]{1,0:T(8,128)S(1)} %get-tuple-element.10.refs_1_), channel_id=1, source_target_pairs={{0,4},{1,5},{2,6},{3,7},{4,0},{5,1},{6,2},{7,3},{8,12},{9,13},{10,... | collective-permute-start | bytes 98312 | tf_op jit(solution)/shard_map/ppermute | solution.py:271
  57.5 5.4 %collective-permute-start.4 = (f32[64,128]{1,0:T(8,128)S(1)}, f32[64,128]{1,0:T(8,128)S(1)}, u32[]{:S(2)}, u32[]{:S(2)}) collective-permute-start(f32[64,128]{1,0:T(8,128)S(1)} %collective-permute-done.refs_2_), channel_id=1, source_target_pairs={{0,4},{1,5},{2,6},{3,7},{4,0},{5,1},{6,2},{7,3},{8,12},{9,13},{10,... | collective-permute-start | bytes 98312 | tf_op jit(solution)/shard_map/ppermute | solution.py:271
  58.2 5.4 %collective-permute-start.5 = (f32[64,128]{1,0:T(8,128)S(1)}, f32[64,128]{1,0:T(8,128)S(1)}, u32[]{:S(2)}, u32[]{:S(2)}) collective-permute-start(f32[64,128]{1,0:T(8,128)S(1)} %collective-permute-done.1.refs_3_), channel_id=1, source_target_pairs={{0,4},{1,5},{2,6},{3,7},{4,0},{5,1},{6,2},{7,3},{8,12},{9,13},{10,... | collective-permute-start | bytes 98312 | tf_op jit(solution)/shard_map/ppermute | solution.py:271
  61.1 5.4 %collective-permute-start.6 = (f32[64,128]{1,0:T(8,128)S(1)}, f32[64,128]{1,0:T(8,128)S(1)}, u32[]{:S(2)}, u32[]{:S(2)}) collective-permute-start(f32[64,128]{1,0:T(8,128)S(1)} %collective-permute-done.2.refs_4_), channel_id=1, source_target_pairs={{0,4},{1,5},{2,6},{3,7},{4,0},{5,1},{6,2},{7,3},{8,12},{9,13},{10,... | collective-permute-start | bytes 98312 | tf_op jit(solution)/shard_map/ppermute | solution.py:271
  69.5 7.9 %copy-start = (f32[2,128,128]{2,1,0:T(8,128)S(1)}, f32[2,128,128]{2,1,0:T(8,128)}, u32[]{:S(2)}) copy-start(f32[2,128,128]{2,1,0:T(8,128)} %constant.18.clone.refs_5_.twist_ref) | copy-start | bytes 393220
  69.5 7.9 %copy-start.3 = (f32[256,256]{1,0:T(8,128)S(1)}, f32[256,256]{1,0:T(8,128)}, u32[]{:S(2)}) copy-start(f32[256,256]{1,0:T(8,128)} %constant.22.clone.inner_ref) | copy-start | bytes 786436
  69.5 7.9 %copy-start.4 = (f32[128,256]{1,0:T(8,128)S(1)}, f32[128,256]{1,0:T(8,128)}, u32[]{:S(2)}) copy-start(f32[128,256]{1,0:T(8,128)} %constant.23.clone.outer_ref) | copy-start | bytes 393220
  69.5 36.0 %all-to-all-start.2 = ((f32[32,8,8,128]{3,2,1,0:T(8,128)}), f32[32,8,8,128]{3,2,1,0:T(8,128)S(1)}, u32[]{:S(2)}, u32[]{:S(2)}) async-start(f32[32,8,8,128]{3,2,1,0:T(8,128)} %bitcast.4), calls=%async_computation.2 | async-start | bytes 2097152 | tf_op jit(solution)/shard_map/all_to_all | solution.py:267
  77.5 14.7 %copy-start.8 = (f32[4]{0:T(128)S(1)}, f32[4]{0:T(128)}, u32[]{:S(2)}) copy-start(f32[4]{0:T(128)} %param.15) | copy-start | bytes 52
  77.5 28.0 %copy-start.1 = (f32[4,16384]{1,0:T(4,128)S(1)}, f32[4,16384]{1,0:T(4,128)}, u32[]{:S(2)}) copy-start(f32[4,16384]{1,0:T(4,128)} %seq_ref.1) | copy-start | bytes 786436
  77.5 28.0 %copy-start.2 = (f32[4,16384]{1,0:T(4,128)S(1)}, f32[4,16384]{1,0:T(4,128)}, u32[]{:S(2)}) copy-start(f32[4,16384]{1,0:T(4,128)} %cot_ref.1) | copy-start | bytes 786436
  78.2 5.6 %collective-permute-start.7 = (f32[2,16384]{1,0:T(2,128)S(1)}, f32[2,16384]{1,0:T(2,128)S(1)}, u32[]{:S(2)}, u32[]{:S(2)}) collective-permute-start(f32[2,16384]{1,0:T(2,128)S(1)} %taps_blocks.1), channel_id=1, source_target_pairs={{0,1},{1,0},{2,3},{3,2},{4,5},{5,4},{6,7},{7,6},{8,9},{9,8},{10,11... | collective-permute-start | bytes 393224 | tf_op jit(solution)/shard_map/ppermute | solution.py:271
  83.9 6.3 %collective-permute-start.8 = (f32[2,16384]{1,0:T(2,128)S(1)}, f32[2,16384]{1,0:T(2,128)S(1)}, u32[]{:S(2)}, u32[]{:S(2)}) collective-permute-start(f32[2,16384]{1,0:T(2,128)S(1)} %add.9), channel_id=1, source_target_pairs={{0,3},{1,2},{2,1},{3,0},{4,7},{5,6},{6,5},{7,4},{8,11},{9,10},{10,... | collective-permute-start | bytes 393224 | tf_op jit(solution)/shard_map/ppermute | solution.py:271
  90.2 6.7 %collective-permute-start.9 = (f32[2,16384]{1,0:T(2,128)S(1)}, f32[2,16384]{1,0:T(2,128)S(1)}, u32[]{:S(2)}, u32[]{:S(2)}) collective-permute-start(f32[2,16384]{1,0:T(2,128)S(1)} %add.10), channel_id=1, source_target_pairs={{0,4},{1,5},{2,6},{3,7},{4,0},{5,1},{6,2},{7,3},{8,12},{9,13},{10,... | collective-permute-start | bytes 393224 | tf_op jit(solution)/shard_map/ppermute | solution.py:271

commit v4 on v3

--- a/solution.py
+++ b/solution.py
@@ -12,7 +12,8 @@
 SUB = SIDE // BLOCKS
 POINTS = 2 * BLOCKS
 CHAN = 8
-OUT_ROWS = 66
+HALF = 4
+OUT_ROWS = 72
 BACK_ROWS = 64
 TAPS_ROWS = 16
 PAIRS = ((0, 2), (1, 3), (4, 6), (5, 7), (8, 9))
@@ -28,7 +29,12 @@
     cosine, sine = np.cos(angle), np.sin(angle)
     forward_outer = np.concatenate([cosine, -sine], axis=0)
     factor = (BLOCKS * BLOCK) ** (-0.5) / BLOCK
-    inverse_outer = factor * np.concatenate([cosine.T, -sine.T], axis=1)
+    row = np.arange(2 * SIDE)
+    coarse, signal = SUB * (row // (2 * SUB)) + row % SUB, (row // SUB) % 2
+    own = signal[None, :] == np.arange(2)[:, None]
+    pair_cosine = (own[:, None, :] * cosine[coarse].T[None]).reshape(2 * SIDE, 2 * SIDE)
+    pair_sine = (own[:, None, :] * sine[coarse].T[None]).reshape(2 * SIDE, 2 * SIDE)
+    inverse_outer = factor * np.concatenate([pair_cosine, -pair_sine], axis=1)
     angle = turn * ((digit[:, None] + 0.25) * digit[None, :] / BLOCK)
     twist = np.stack([np.cos(angle), np.sin(angle)])
     angle = turn * ((digit[:, None] * digit[None, :]) % SIDE / SIDE)
@@ -37,7 +43,7 @@
     inverse_inner = np.block([[cosine, sine], [-sine, cosine]])
     return (
         tuple(t.astype(single) for t in (forward_outer, forward_inner, twist)),
-        tuple(t.astype(single) for t in (inverse_inner, inverse_outer, twist)),
+        tuple(t.astype(single) for t in (inverse_inner, inverse_outer, twist[:, coarse])),
     )
 
 
@@ -117,7 +123,7 @@
     opened = dot_wide(outer_ref[...], signals)
     cosine, sine = twist_ref[0], twist_ref[1]
     inner = inner_ref[...]
-    chan = lax.axis_index("chan")
+    half = lax.axis_index("chan") // HALF
     for p, pair in enumerate(PAIRS):
         twisted = []
         for i in pair:
@@ -133,10 +139,10 @@
                 for r in range(8):
                     out_ref[pl.ds(16 * p + 8 * h + r, BLOCKS, stride=OUT_ROWS), :] = picked[r]
             else:
-                share = picked[0]
-                for r in range(1, 8):
-                    share = jnp.where(chan == r, picked[r], share)
-                out_ref[pl.ds(64 + h, BLOCKS, stride=OUT_ROWS), :] = share
+                for r in range(SUB):
+                    out_ref[pl.ds(64 + SUB * h + r, BLOCKS, stride=OUT_ROWS), :] = jnp.where(
+                        half == 0, picked[r], picked[SUB + r]
+                    )
 
 
 def forward_blocks(sequence, cotangent, taps):
@@ -170,8 +176,8 @@
 
 
 def taps_products_kernel(in_ref, there_ref, adjoint_ref, taps_ref, share_ref):
-    for h in range(2):
-        share_ref[BLOCKS * h : BLOCKS * (h + 1), :] = in_ref[pl.ds(64 + h, BLOCKS, stride=OUT_ROWS), :]
+    for r in range(8):
+        share_ref[BLOCKS * r : BLOCKS * (r + 1), :] = in_ref[pl.ds(64 + r, BLOCKS, stride=OUT_ROWS), :]
     there = there_ref[...]
     real = imag = 0.0
     for q in range(2):
@@ -185,18 +191,22 @@
 def taps_products(spectra):
     operands = (spectra, jnp.asarray(THERE), jnp.asarray(ADJOINT))
     return call(
-        taps_products_kernel, "taps_products", ((BLOCKS * TAPS_ROWS, SIDE), (2 * BLOCKS, SIDE)), operands
+        taps_products_kernel, "taps_products", ((BLOCKS * TAPS_ROWS, SIDE), (8 * BLOCKS, SIDE)), operands
     )
 
 
-def products_kernel(*refs):
-    in_ref, shares = refs[0], refs[1 : 1 + CHAN]
-    there_ref, back_ref, adjoint_ref, out_ref, taps = refs[1 + CHAN :]
-    chan = lax.axis_index("chan")
-    for flip in range(CHAN):
-        taps[chan ^ flip] = shares[flip][...]
+def products_kernel(in_ref, own_ref, other_ref, there_ref, back_ref, adjoint_ref, out_ref):
+    half = lax.axis_index("chan") // HALF
     there, back, adjoint = there_ref[...], back_ref[...], adjoint_ref[...]
-    points = dot_wide(there, jnp.concatenate([taps[r] for r in range(8)], axis=1))
+
+    def taps_row(f, h, c):
+        lines = slice(BLOCKS * (SUB * h + c), BLOCKS * (SUB * h + c + 1))
+        return jnp.where(half == f, own_ref[lines, :], other_ref[lines, :])
+
+    halves = [
+        jnp.concatenate([taps_row(f, h, c) for f in range(2) for c in range(SUB)], axis=1) for h in range(2)
+    ]
+    points = dot_wide(there, jnp.concatenate(halves, axis=0))
     hr, hi = points[:POINTS], points[POINTS:]
     for q in range(2):
         xr, xi = points_of(in_ref, there, q)
@@ -205,40 +215,38 @@
         blocks_of(out_ref, 2 + q, BACK_ROWS, adjoint, hr * gr + hi * gi, hr * gi - hi * gr)
 
 
-def products(spectra, shares):
-    operands = (spectra, *shares) + tuple(jnp.asarray(t) for t in (THERE, BACK, ADJOINT))
-    scratch = [pltpu.VMEM((CHAN, 2 * BLOCKS, SIDE), jnp.float32)]
-    return call(products_kernel, "products", (BLOCKS * BACK_ROWS, SIDE), operands, scratch)
-
-
-def close(in_ref, inner_ref, outer_ref, twist_ref, gathered, rows, pairs, width):
-    count = 2 * len(pairs)
-    for p, pair in enumerate(pairs):
-        for h in range(2):
-            for r in range(8):
-                gathered[h, pl.ds(pair[r // SUB] * SIDE + r % SUB, BLOCKS, stride=SUB), :] = in_ref[
-                    pl.ds(16 * p + 8 * h + r, BLOCKS, stride=width), :
-                ]
-    turned = dot_three(jnp.concatenate([gathered[0], gathered[1]], axis=1), inner_ref[...])
+def products(spectra, own, other):
+    operands = (spectra, own, other) + tuple(jnp.asarray(t) for t in (THERE, BACK, ADJOINT))
+    return call(products_kernel, "products", (BLOCKS * BACK_ROWS, SIDE), operands)
+
+
+def close(in_ref, inner_ref, outer_ref, twist_ref, rows, places):
     cosine, sine = twist_ref[0], twist_ref[1]
+    inner = inner_ref[...]
     columns = []
-    for i in range(count):
-        real = turned[i * SIDE : (i + 1) * SIDE, :SIDE]
-        imag = turned[i * SIDE : (i + 1) * SIDE, SIDE:]
+    for p in range(len(places)):
+        both = jnp.concatenate(
+            [in_ref[:, 16 * p + 8 * h : 16 * p + 8 * h + 8, :].reshape(2 * SIDE, SIDE) for h in range(2)], axis=1
+        )
+        turned = dot_three(both, inner)
+        real, imag = turned[:, :SIDE], turned[:, SIDE:]
         columns.append(jnp.concatenate([real * cosine - imag * sine, imag * cosine + real * sine], axis=0))
     closed = dot_three(outer_ref[...], jnp.concatenate(columns, axis=1))
-    for i in range(count):
-        rows[i * SIDE : (i + 1) * SIDE, :] = closed[:, i * SIDE : (i + 1) * SIDE]
-
-
-def taps_kernel(in_ref, inner_ref, outer_ref, twist_ref, f_ref, gathered, rows):
-    close(in_ref, inner_ref, outer_ref, twist_ref, gathered, rows, ((0, 1),), TAPS_ROWS)
+    for p, pair in enumerate(places):
+        for half, place in enumerate(pair):
+            rows[place * SIDE : (place + 1) * SIDE, :] = closed[
+                half * SIDE : (half + 1) * SIDE, p * SIDE : (p + 1) * SIDE
+            ]
+
+
+def taps_kernel(in_ref, inner_ref, outer_ref, twist_ref, f_ref, rows):
+    close(in_ref, inner_ref, outer_ref, twist_ref, rows, ((0, 1),))
     for a in range(SIDE):
         f_ref[:, a * SIDE : (a + 1) * SIDE] = rows[pl.ds(a, 2, stride=SIDE), :]
 
 
-def inverse_kernel(in_ref, seq_ref, cot_ref, skip_ref, inner_ref, outer_ref, twist_ref, y_ref, g_ref, gathered, rows):
-    close(in_ref, inner_ref, outer_ref, twist_ref, gathered, rows, PAIRS[:4], BACK_ROWS)
+def inverse_kernel(in_ref, seq_ref, cot_ref, skip_ref, inner_ref, outer_ref, twist_ref, y_ref, g_ref, rows):
+    close(in_ref, inner_ref, outer_ref, twist_ref, rows, PAIRS[:4])
     skip = jnp.broadcast_to(skip_ref[...], (4, SIDE))
     for a in range(SIDE):
         lanes = slice(a * SIDE, (a + 1) * SIDE)
@@ -246,25 +254,20 @@
         g_ref[:, lanes] = rows[pl.ds(4 * SIDE + a, 4, stride=SIDE), :] + skip * cot_ref[:, lanes]
 
 
-def close_scratch(count):
-    return [pltpu.VMEM((2, count * SIDE, SIDE), jnp.float32), pltpu.VMEM((count * SIDE, SIDE), jnp.float32)]
-
-
 def taps_blocks(spectra):
     operands = (spectra,) + tuple(jnp.asarray(t) for t in INVERSE_TABLES)
-    return call(taps_kernel, "taps_blocks", (2, BLOCK), operands, close_scratch(2))
+    return call(taps_kernel, "taps_blocks", (2, BLOCK), operands, [pltpu.VMEM((2 * SIDE, SIDE), jnp.float32)])
 
 
 def inverse_blocks(spectra, sequence, cotangent, skip_gain):
     operands = (spectra, sequence, cotangent, skip_gain[:, None]) + tuple(jnp.asarray(t) for t in INVERSE_TABLES)
-    return call(inverse_kernel, "inverse_blocks", ((4, BLOCK), (4, BLOCK)), operands, close_scratch(8))
+    scratch = [pltpu.VMEM((8 * SIDE, SIDE), jnp.float32)]
+    return call(inverse_kernel, "inverse_blocks", ((4, BLOCK), (4, BLOCK)), operands, scratch)
 
 
 def exchange(blocks):
-    rows = blocks.shape[0] // BLOCKS
-    tall = 1 if rows % 8 else 8
-    cut = blocks.reshape(BLOCKS, rows // tall, tall, SIDE)
-    return lax.all_to_all(cut, "ctx", split_axis=0, concat_axis=0, tiled=True).reshape(blocks.shape)
+    cut = blocks.reshape(BLOCKS, -1, SIDE)
+    return lax.all_to_all(cut, "ctx", split_axis=0, concat_axis=0, tiled=True)
 
 
 def flip_chan(values, flip):
@@ -278,12 +281,10 @@
 
 
 def body(sequence, filter_taps, skip_gain, cotangent):
-    spectra = exchange(forward_blocks(sequence, cotangent, filter_taps))
+    spectra = exchange(forward_blocks(sequence, cotangent, filter_taps)).reshape(BLOCKS * OUT_ROWS, SIDE)
     taps, share = taps_products(spectra)
     taps = exchange(taps)
-    shares = [share] + [flip_chan(share, flip) for flip in (1, 2, 3)]
-    shares = shares + [flip_chan(s, 4) for s in shares]
-    back = products(spectra, shares)
+    back = products(spectra, share, flip_chan(share, HALF))
     taps, back = lax.optimization_barrier((taps, back))
     taps_grad = sum_over_chan(taps_blocks(taps))
     convolved, seq_grad = inverse_blocks(exchange(back), sequence, cotangent, skip_gain)

time: 110 us -> 105 us (0.955)
  starting transfers between devices: 30.1 us -> 23.5 us
  blocking collectives: 39.4 us -> 41.2 us
    ppermute x10 -> x4, starting transfers between devices: 17.5 us -> 9.73 us  [flip_chan(): return lax.ppermute(values, 'chan', [(i, i ^ flip) for i in range(CHAN)])]
    all_to_all x1, blocking collectives: 39.4 us -> 41.2 us  [exchange(): return lax.all_to_all(cut, 'ctx', split_axis=0, concat_axis=0, tiled=True)]
    all_to_all x2, starting transfers between devices: 12.5 us -> 13.8 us  [exchange(): return lax.all_to_all(cut, 'ctx', split_axis=0, concat_axis=0, tiled=True)]
    ppermute x10 -> x4, waiting for transfers between devices: 17.6 us -> 17.1 us  [flip_chan(): return lax.ppermute(values, 'chan', [(i, i ^ flip) for i in range(CHAN)])]
  transfers between devices with their start and end apart: 12 -> 6, of which waited for: 7 -> 5; matrix products, arithmetic and copies ran while one was open for 1% -> 1% of each run, Pallas kernels for 3% -> 4%
where the time goes in v4:
time: 105 us; the launch traced here: 103 us
  blocking collectives  41.2 us (39%)
  waiting for transfers between devices  24.9 us (24%)
  starting transfers between devices  23.5 us (22%)
  Pallas kernels  11.4 us (11%)
    all_to_all x1, blocking collectives, exchange(): return lax.all_to_all(cut, 'ctx', split_axis=0, concat_axis=0, tiled=True)  41.2 us
    ppermute x4, waiting for transfers between devices, flip_chan(): return lax.ppermute(values, 'chan', [(i, i ^ flip) for i in range(CHAN)])  17.1 us
    all_to_all x2, starting transfers between devices, exchange(): return lax.all_to_all(cut, 'ctx', split_axis=0, concat_axis=0, tiled=True)  13.8 us
    pallas_call x5, Pallas kernels, call(): pl.pallas_call(kernel, out_shape=shapes if many else shapes[0], in_specs=...  11.4 us
    ppermute x4, starting transfers between devices, flip_chan(): return lax.ppermute(values, 'chan', [(i, i ^ flip) for i in range(CHAN)])  9.73 us
    all_to_all x2, waiting for transfers between devices, exchange(): return lax.all_to_all(cut, 'ctx', split_axis=0, concat_axis=0, tiled=True)  7.8 us
  transfers between devices with their start and end apart: 6, of which 5 were waited for; matrix products, arithmetic and copies ran while one was open for 1% of the time, Pallas kernels for 4%

profile of v4, /device:TPU:32, one launch (start us, length us, event | category | flops | bytes accessed | tf_op | source)
XLA Modules:
  0.0 102.7 jit_solution(18181102395253590091)
XLA Ops:
  0.6 3.7 %forward_blocks.1 = f32[2304,128]{1,0:T(8,128)} custom-call(f32[4,16384]{1,0:T(4,128)} %seq_ref.1, f32[4,16384]{1,0:T(4,128)} %cot_ref.1, f32[2,16384]{1,0:T(2,128)} %refs_2_.1, f32[256,128]{1,0:T(8,128)} %constant.18.clone.refs_3_, f32[256,256]{1,0:T(8,128)} %constant.19.clone.refs_4_, f32[2,128,128]{2,1,0:T(8,128)} %constant.20.clone.refs_5_), custom_call_target="tpu_custom_call" | custom-call | tf_op jit(solution)/shard_map/forward_blocks/pallas_call | solution.py:91
  4.3 0.0 copy-start.5
  4.3 0.0 copy-start.6
  4.4 41.2 %all_to_all.15 = f32[32,72,128]{2,1,0:T(8,128)S(1)} all-to-all(f32[32,72,128]{2,1,0:T(8,128)} %bitcast.7), channel_id=1, replica_groups=mesh['ctx'=32,'chan'=8] {'ctx'}, dimensions={0} | all-to-all | bytes 2359296 | tf_op jit(solution)/shard_map/all_to_all | solution.py:270
  45.5 0.0 copy-start.7
  45.5 0.0 copy-done.5
  45.5 0.0 copy-done.6
  45.6 1.5 %taps_products.1 = (f32[512,128]{1,0:T(8,128)}, f32[256,128]{1,0:T(8,128)S(1)}) custom-call(f32[2304,128]{1,0:T(8,128)S(1)} %bitcast.5, f32[128,64]{1,0:T(8,128)S(1)} %copy-done.5, f32[64,128]{1,0:T(8,128)S(1)} %copy-done.6), custom_call_target="tpu_custom_call" | custom-call | tf_op jit(solution)/shard_map/taps_products/pallas_call | solution.py:91
  47.1 4.6 %all-to-all-start.1 = ((f32[32,16,128]{2,1,0:T(8,128)}), f32[32,16,128]{2,1,0:T(8,128)S(1)}, u32[]{:S(2)}, u32[]{:S(2)}) async-start(f32[32,16,128]{2,1,0:T(8,128)} %bitcast.2), calls=%async_computation.1 | async-start | bytes 524288 | tf_op jit(solution)/shard_map/all_to_all | solution.py:270
  51.7 3.0 %collective-permute-start = (f32[256,128]{1,0:T(8,128)S(1)}, f32[256,128]{1,0:T(8,128)S(1)}, u32[]{:S(2)}, u32[]{:S(2)}) collective-permute-start(f32[256,128]{1,0:T(8,128)S(1)} %get-tuple-element.10.own_ref), channel_id=1, source_target_pairs={{0,4},{1,5},{2,6},{3,7},{4,0},{5,1},{6,2},{7,3},{8,12},{9,13},{10,... | collective-permute-start | bytes 393224 | tf_op jit(solution)/shard_map/ppermute | solution.py:274
  54.7 5.5 %collective-permute-done.other_ref = f32[256,128]{1,0:T(8,128)S(1)} collective-permute-done((f32[256,128]{1,0:T(8,128)S(1)}, f32[256,128]{1,0:T(8,128)S(1)}, u32[]{:S(2)}, u32[]{:S(2)}) %collective-permute-start) | collective-permute-done | bytes 131104 | tf_op jit(solution)/shard_map/ppermute | solution.py:274
  60.1 0.0 copy-done.7
  60.1 3.0 %products.1 = f32[2048,128]{1,0:T(8,128)} custom-call(f32[2304,128]{1,0:T(8,128)S(1)} %bitcast.6, f32[256,128]{1,0:T(8,128)S(1)} %get-tuple-element.10.own_ref, f32[256,128]{1,0:T(8,128)S(1)} %collective-permute-done.other_ref, f32[128,64]{1,0:T(8,128)S(1)} %copy-done.5, f32[64,128]{1,0:T(8,128)S(1)} %copy-done.7, f32[64,128]{1,0:T(8,128)S(1)} %copy-done.6), custom_call_target="tpu_custom_call" | custom-call | tf_op jit(solution)/shard_map/products/pallas_call | solution.py:91
  63.2 0.0 copy-start
  63.2 0.0 copy-start.3
  63.2 0.0 copy-start.4
  63.2 0.0 all-to-all-done.1.in_ref
  63.2 9.2 %all-to-all-start.2 = ((f32[32,64,128]{2,1,0:T(8,128)}), f32[32,64,128]{2,1,0:T(8,128)S(1)}, u32[]{:S(2)}, u32[]{:S(2)}) async-start(f32[32,64,128]{2,1,0:T(8,128)} %bitcast.3), calls=%async_computation.2 | async-start | bytes 2097152 | tf_op jit(solution)/shard_map/all_to_all | solution.py:270
  72.4 0.0 copy-done
  72.4 0.0 copy-done.3
  72.5 0.0 copy-done.4
  72.5 0.0 copy-start.8
  72.5 0.0 copy-start.1
  72.5 0.0 copy-start.2
  72.5 0.9 taps_blocks.1
  73.4 1.6 %collective-permute-start.1 = (f32[2,16384]{1,0:T(2,128)S(1)}, f32[2,16384]{1,0:T(2,128)S(1)}, u32[]{:S(2)}, u32[]{:S(2)}) collective-permute-start(f32[2,16384]{1,0:T(2,128)S(1)} %taps_blocks.1), channel_id=1, source_target_pairs={{0,1},{1,0},{2,3},{3,2},{4,5},{5,4},{6,7},{7,6},{8,9},{9,8},{10,11... | collective-permute-start | bytes 393224 | tf_op jit(solution)/shard_map/ppermute | solution.py:274
  75.0 4.1 %collective-permute-done.1 = f32[2,16384]{1,0:T(2,128)S(1)} collective-permute-done((f32[2,16384]{1,0:T(2,128)S(1)}, f32[2,16384]{1,0:T(2,128)S(1)}, u32[]{:S(2)}, u32[]{:S(2)}) %collective-permute-start.1) | collective-permute-done | bytes 131104 | tf_op jit(solution)/shard_map/ppermute | solution.py:274
  79.0 0.1 add.9
  79.1 2.8 %collective-permute-start.2 = (f32[2,16384]{1,0:T(2,128)S(1)}, f32[2,16384]{1,0:T(2,128)S(1)}, u32[]{:S(2)}, u32[]{:S(2)}) collective-permute-start(f32[2,16384]{1,0:T(2,128)S(1)} %add.9), channel_id=1, source_target_pairs={{0,3},{1,2},{2,1},{3,0},{4,7},{5,6},{6,5},{7,4},{8,11},{9,10},{10,... | collective-permute-start | bytes 393224 | tf_op jit(solution)/shard_map/ppermute | solution.py:274
  82.0 3.4 %collective-permute-done.2 = f32[2,16384]{1,0:T(2,128)S(1)} collective-permute-done((f32[2,16384]{1,0:T(2,128)S(1)}, f32[2,16384]{1,0:T(2,128)S(1)}, u32[]{:S(2)}, u32[]{:S(2)}) %collective-permute-start.2) | collective-permute-done | bytes 131104 | tf_op jit(solution)/shard_map/ppermute | solution.py:274
  85.4 0.1 add.10
  85.5 2.3 %collective-permute-start.3 = (f32[2,16384]{1,0:T(2,128)S(1)}, f32[2,16384]{1,0:T(2,128)S(1)}, u32[]{:S(2)}, u32[]{:S(2)}) collective-permute-start(f32[2,16384]{1,0:T(2,128)S(1)} %add.10), channel_id=1, source_target_pairs={{0,4},{1,5},{2,6},{3,7},{4,0},{5,1},{6,2},{7,3},{8,12},{9,13},{10,... | collective-permute-start | bytes 393224 | tf_op jit(solution)/shard_map/ppermute | solution.py:274
  87.8 0.0 copy-done.8
  87.8 0.1 copy.16.skip_ref
  87.9 4.1 %collective-permute-done.3 = f32[2,16384]{1,0:T(2,128)S(1)} collective-permute-done((f32[2,16384]{1,0:T(2,128)S(1)}, f32[2,16384]{1,0:T(2,128)S(1)}, u32[]{:S(2)}, u32[]{:S(2)}) %collective-permute-start.3) | collective-permute-done | bytes 131104 | tf_op jit(solution)/shard_map/ppermute | solution.py:274
  92.0 0.7 add.11
  92.7 7.8 %all-to-all-done.2.in_ref = f32[32,64,128]{2,1,0:T(8,128)S(1)} async-done(((f32[32,64,128]{2,1,0:T(8,128)}), f32[32,64,128]{2,1,0:T(8,128)S(1)}, u32[]{:S(2)}, u32[]{:S(2)}) %all-to-all-start.2) | async-done | bytes 1048608 | tf_op jit(solution)/shard_map/all_to_all | solution.py:270
  100.5 0.0 copy-done.1
  100.5 0.0 copy-done.2
  100.5 2.2 %inverse_blocks.1 = (f32[4,16384]{1,0:T(4,128)}, f32[4,16384]{1,0:T(4,128)}) custom-call(f32[32,64,128]{2,1,0:T(8,128)S(1)} %all-to-all-done.2.in_ref, f32[4,16384]{1,0:T(4,128)S(1)} %copy-done.1, f32[4,16384]{1,0:T(4,128)S(1)} %copy-done.2, f32[4,1]{1,0:T(4,128)S(1)} %copy.16.skip_ref, f32[256,256]{1,0:T(8,128)S(1)} %copy-done.3, f32[256,512]{1,0:T(8,128)S(1)} %copy-done, ...), custom_call_target="tpu_custom_call" | custom-call | tf_op jit(solution)/shard_map/inverse_blocks/pallas_call | solution.py:91
Async XLA Ops:
  4.3 41.2 %copy-start.5 = (f32[128,64]{1,0:T(8,128)S(1)}, f32[128,64]{1,0:T(8,128)}, u32[]{:S(2)}) copy-start(f32[128,64]{1,0:T(8,128)} %constant.21.clone.there_ref) | copy-start | bytes 98308
  4.3 41.2 %copy-start.6 = (f32[64,128]{1,0:T(8,128)S(1)}, f32[64,128]{1,0:T(8,128)}, u32[]{:S(2)}) copy-start(f32[64,128]{1,0:T(8,128)} %constant.22.clone.adjoint_ref) | copy-start | bytes 98308
  45.5 14.6 %copy-start.7 = (f32[64,128]{1,0:T(8,128)S(1)}, f32[64,128]{1,0:T(8,128)}, u32[]{:S(2)}) copy-start(f32[64,128]{1,0:T(8,128)} %constant.23.clone.back_ref) | copy-start | bytes 98308
  47.1 16.1 %all-to-all-start.1 = ((f32[32,16,128]{2,1,0:T(8,128)}), f32[32,16,128]{2,1,0:T(8,128)S(1)}, u32[]{:S(2)}, u32[]{:S(2)}) async-start(f32[32,16,128]{2,1,0:T(8,128)} %bitcast.2), calls=%async_computation.1 | async-start | bytes 524288 | tf_op jit(solution)/shard_map/all_to_all | solution.py:270
  51.7 8.4 %collective-permute-start = (f32[256,128]{1,0:T(8,128)S(1)}, f32[256,128]{1,0:T(8,128)S(1)}, u32[]{:S(2)}, u32[]{:S(2)}) collective-permute-start(f32[256,128]{1,0:T(8,128)S(1)} %get-tuple-element.10.own_ref), channel_id=1, source_target_pairs={{0,4},{1,5},{2,6},{3,7},{4,0},{5,1},{6,2},{7,3},{8,12},{9,13},{10,... | collective-permute-start | bytes 393224 | tf_op jit(solution)/shard_map/ppermute | solution.py:274
  63.2 9.3 %copy-start = (f32[256,512]{1,0:T(8,128)S(1)}, f32[256,512]{1,0:T(8,128)}, u32[]{:S(2)}) copy-start(f32[256,512]{1,0:T(8,128)} %constant.25.clone.outer_ref) | copy-start | bytes 1572868
  63.2 9.3 %copy-start.3 = (f32[256,256]{1,0:T(8,128)S(1)}, f32[256,256]{1,0:T(8,128)}, u32[]{:S(2)}) copy-start(f32[256,256]{1,0:T(8,128)} %constant.24.clone.inner_ref) | copy-start | bytes 786436
  63.2 9.3 %copy-start.4 = (f32[2,256,128]{2,1,0:T(8,128)S(1)}, f32[2,256,128]{2,1,0:T(8,128)}, u32[]{:S(2)}) copy-start(f32[2,256,128]{2,1,0:T(8,128)} %constant.26.clone.twist_ref) | copy-start | bytes 786436
  63.2 37.3 %all-to-all-start.2 = ((f32[32,64,128]{2,1,0:T(8,128)}), f32[32,64,128]{2,1,0:T(8,128)S(1)}, u32[]{:S(2)}, u32[]{:S(2)}) async-start(f32[32,64,128]{2,1,0:T(8,128)} %bitcast.3), calls=%async_computation.2 | async-start | bytes 2097152 | tf_op jit(solution)/shard_map/all_to_all | solution.py:270
  72.5 15.3 %copy-start.8 = (f32[4]{0:T(128)S(1)}, f32[4]{0:T(128)}, u32[]{:S(2)}) copy-start(f32[4]{0:T(128)} %param.15) | copy-start | bytes 52
  72.5 28.0 %copy-start.1 = (f32[4,16384]{1,0:T(4,128)S(1)}, f32[4,16384]{1,0:T(4,128)}, u32[]{:S(2)}) copy-start(f32[4,16384]{1,0:T(4,128)} %seq_ref.1) | copy-start | bytes 786436
  72.5 28.0 %copy-start.2 = (f32[4,16384]{1,0:T(4,128)S(1)}, f32[4,16384]{1,0:T(4,128)}, u32[]{:S(2)}) copy-start(f32[4,16384]{1,0:T(4,128)} %cot_ref.1) | copy-start | bytes 786436
  73.4 5.6 %collective-permute-start.1 = (f32[2,16384]{1,0:T(2,128)S(1)}, f32[2,16384]{1,0:T(2,128)S(1)}, u32[]{:S(2)}, u32[]{:S(2)}) collective-permute-start(f32[2,16384]{1,0:T(2,128)S(1)} %taps_blocks.1), channel_id=1, source_target_pairs={{0,1},{1,0},{2,3},{3,2},{4,5},{5,4},{6,7},{7,6},{8,9},{9,8},{10,11... | collective-permute-start | bytes 393224 | tf_op jit(solution)/shard_map/ppermute | solution.py:274
  79.1 6.3 %collective-permute-start.2 = (f32[2,16384]{1,0:T(2,128)S(1)}, f32[2,16384]{1,0:T(2,128)S(1)}, u32[]{:S(2)}, u32[]{:S(2)}) collective-permute-start(f32[2,16384]{1,0:T(2,128)S(1)} %add.9), channel_id=1, source_target_pairs={{0,3},{1,2},{2,1},{3,0},{4,7},{5,6},{6,5},{7,4},{8,11},{9,10},{10,... | collective-permute-start | bytes 393224 | tf_op jit(solution)/shard_map/ppermute | solution.py:274
  85.5 6.6 %collective-permute-start.3 = (f32[2,16384]{1,0:T(2,128)S(1)}, f32[2,16384]{1,0:T(2,128)S(1)}, u32[]{:S(2)}, u32[]{:S(2)}) collective-permute-start(f32[2,16384]{1,0:T(2,128)S(1)} %add.10), channel_id=1, source_target_pairs={{0,4},{1,5},{2,6},{3,7},{4,0},{5,1},{6,2},{7,3},{8,12},{9,13},{10,... | collective-permute-start | bytes 393224 | tf_op jit(solution)/shard_map/ppermute | solution.py:274

commit v5 on v4

--- a/solution.py
+++ b/solution.py
@@ -12,8 +12,7 @@
 SUB = SIDE // BLOCKS
 POINTS = 2 * BLOCKS
 CHAN = 8
-HALF = 4
-OUT_ROWS = 72
+OUT_ROWS = 80
 BACK_ROWS = 64
 TAPS_ROWS = 16
 PAIRS = ((0, 2), (1, 3), (4, 6), (5, 7), (8, 9))
@@ -87,7 +86,7 @@
     space = pl.ANY if own_copies else pltpu.VMEM
     many = isinstance(out_shape[0], tuple)
     shapes = tuple(jax.ShapeDtypeStruct(s, jnp.float32) for s in (out_shape if many else (out_shape,)))
-    outs = (pl.BlockSpec(memory_space=pltpu.VMEM),) * len(shapes)
+    outs = (pl.BlockSpec(memory_space=space),) * len(shapes)
     return pl.pallas_call(
         kernel,
         out_shape=shapes if many else shapes[0],
@@ -105,7 +104,7 @@
 
 
 def forward_kernel(*refs):
-    sources, out_ref, held, rows, spectra, sems = refs[:6], refs[6], refs[7:13], refs[13], refs[14], refs[15]
+    sources, out_ref, held, rows, sent, sems = refs[:6], refs[6], refs[7:13], refs[13], refs[14], refs[15]
     copies = [pltpu.make_async_copy(s, h, sems.at[i]) for i, (s, h) in enumerate(zip(sources, held))]
     for copy in copies:
         copy.start()
@@ -123,7 +122,8 @@
     opened = dot_wide(outer_ref[...], signals)
     cosine, sine = twist_ref[0], twist_ref[1]
     inner = inner_ref[...]
-    half = lax.axis_index("chan") // HALF
+    low = lax.broadcasted_iota(jnp.int32, (SIDE // 8, 8, SIDE), 1) < SUB
+    leaving = []
     for p, pair in enumerate(PAIRS):
         twisted = []
         for i in pair:
@@ -132,27 +132,28 @@
             twisted.append(jnp.concatenate([real * cosine + imag * sine, imag * cosine - real * sine], axis=1))
         spectrum = dot_three(jnp.concatenate(twisted, axis=0), inner)
         for h in range(2):
-            held_rows = spectra.at[2 * p + h]
-            held_rows[...] = spectrum[:, h * SIDE : (h + 1) * SIDE]
-            picked = [held_rows[pl.ds((r // SUB) * SIDE + r % SUB, BLOCKS, stride=SUB), :] for r in range(8)]
-            if p < 4:
-                for r in range(8):
-                    out_ref[pl.ds(16 * p + 8 * h + r, BLOCKS, stride=OUT_ROWS), :] = picked[r]
-            else:
-                for r in range(SUB):
-                    out_ref[pl.ds(64 + SUB * h + r, BLOCKS, stride=OUT_ROWS), :] = jnp.where(
-                        half == 0, picked[r], picked[SUB + r]
-                    )
+            first, second = (
+                spectrum[i * SIDE : (i + 1) * SIDE, h * SIDE : (h + 1) * SIDE].reshape(SIDE // 8, 8, SIDE)
+                for i in range(2)
+            )
+            sent[p, :, 0, 8 * h : 8 * h + 8, :] = jnp.where(low, first, pltpu.roll(second, SUB, 1))
+            sent[p, :, 1, 8 * h : 8 * h + 8, :] = jnp.where(low, pltpu.roll(first, SUB, 1), second)
+        copy = pltpu.make_async_copy(sent.at[p], out_ref.at[:, :, 16 * p : 16 * p + 16, :], sems.at[6 + p])
+        copy.start()
+        leaving.append(copy)
+    for copy in leaving:
+        copy.wait()
 
 
 def forward_blocks(sequence, cotangent, taps):
     operands = (sequence, cotangent, taps) + tuple(jnp.asarray(t) for t in FORWARD_TABLES)
     scratch = [pltpu.VMEM(v.shape, v.dtype) for v in operands] + [
         pltpu.VMEM((10 * SIDE, SIDE), jnp.float32),
-        pltpu.VMEM((10, 2 * SIDE, SIDE), jnp.float32),
-        pltpu.SemaphoreType.DMA((6,)),
+        pltpu.VMEM((5, BLOCKS // 2, 2, 16, SIDE), jnp.float32),
+        pltpu.SemaphoreType.DMA((11,)),
     ]
-    return call(forward_kernel, "forward_blocks", (BLOCKS * OUT_ROWS, SIDE), operands, scratch, True)
+    shape = (BLOCKS // 2, 2, OUT_ROWS, SIDE)
+    return call(forward_kernel, "forward_blocks", shape, operands, scratch, True)
 
 
 def points_of(in_ref, there, p):
@@ -175,9 +176,7 @@
             ]
 
 
-def taps_products_kernel(in_ref, there_ref, adjoint_ref, taps_ref, share_ref):
-    for r in range(8):
-        share_ref[BLOCKS * r : BLOCKS * (r + 1), :] = in_ref[pl.ds(64 + r, BLOCKS, stride=OUT_ROWS), :]
+def taps_products_kernel(in_ref, there_ref, adjoint_ref, taps_ref):
     there = there_ref[...]
     real = imag = 0.0
     for q in range(2):
@@ -190,24 +189,12 @@
 
 def taps_products(spectra):
     operands = (spectra, jnp.asarray(THERE), jnp.asarray(ADJOINT))
-    return call(
-        taps_products_kernel, "taps_products", ((BLOCKS * TAPS_ROWS, SIDE), (8 * BLOCKS, SIDE)), operands
-    )
-
-
-def products_kernel(in_ref, own_ref, other_ref, there_ref, back_ref, adjoint_ref, out_ref):
-    half = lax.axis_index("chan") // HALF
+    return call(taps_products_kernel, "taps_products", (BLOCKS * TAPS_ROWS, SIDE), operands)
+
+
+def products_kernel(in_ref, there_ref, back_ref, adjoint_ref, out_ref):
     there, back, adjoint = there_ref[...], back_ref[...], adjoint_ref[...]
-
-    def taps_row(f, h, c):
-        lines = slice(BLOCKS * (SUB * h + c), BLOCKS * (SUB * h + c + 1))
-        return jnp.where(half == f, own_ref[lines, :], other_ref[lines, :])
-
-    halves = [
-        jnp.concatenate([taps_row(f, h, c) for f in range(2) for c in range(SUB)], axis=1) for h in range(2)
-    ]
-    points = dot_wide(there, jnp.concatenate(halves, axis=0))
-    hr, hi = points[:POINTS], points[POINTS:]
+    hr, hi = points_of(in_ref, there, 4)
     for q in range(2):
         xr, xi = points_of(in_ref, there, q)
         blocks_of(out_ref, q, BACK_ROWS, back, hr * xr - hi * xi, hr * xi + hi * xr)
@@ -215,8 +202,8 @@
         blocks_of(out_ref, 2 + q, BACK_ROWS, adjoint, hr * gr + hi * gi, hr * gi - hi * gr)
 
 
-def products(spectra, own, other):
-    operands = (spectra, own, other) + tuple(jnp.asarray(t) for t in (THERE, BACK, ADJOINT))
+def products(spectra):
+    operands = (spectra,) + tuple(jnp.asarray(t) for t in (THERE, BACK, ADJOINT))
     return call(products_kernel, "products", (BLOCKS * BACK_ROWS, SIDE), operands)
 
 
@@ -282,9 +269,8 @@
 
 def body(sequence, filter_taps, skip_gain, cotangent):
     spectra = exchange(forward_blocks(sequence, cotangent, filter_taps)).reshape(BLOCKS * OUT_ROWS, SIDE)
-    taps, share = taps_products(spectra)
-    taps = exchange(taps)
-    back = products(spectra, share, flip_chan(share, HALF))
+    taps = exchange(taps_products(spectra))
+    back = products(spectra)
     taps, back = lax.optimization_barrier((taps, back))
     taps_grad = sum_over_chan(taps_blocks(taps))
     convolved, seq_grad = inverse_blocks(exchange(back), sequence, cotangent, skip_gain)

time: 105 us -> 103 us (0.981)
  starting transfers between devices: 23.5 us -> 16.9 us
  blocking collectives: 41.2 us -> 43.6 us
  waiting for transfers between devices: 24.9 us -> 27.2 us
    all_to_all x2, waiting for transfers between devices: 7.8 us -> 14.6 us  [exchange(): return lax.all_to_all(cut, 'ctx', split_axis=0, concat_axis=0, tiled=True)]
    ppermute x4 -> x3, waiting for transfers between devices: 17.1 us -> 12.6 us  [flip_chan(): return lax.ppermute(values, 'chan', [(i, i ^ flip) for i in range(CHAN)])]
    all_to_all x2, starting transfers between devices: 13.8 us -> 9.53 us  [exchange(): return lax.all_to_all(cut, 'ctx', split_axis=0, concat_axis=0, tiled=True)]
    all_to_all x1, blocking collectives: 41.2 us -> 43.6 us  [exchange(): return lax.all_to_all(cut, 'ctx', split_axis=0, concat_axis=0, tiled=True)]
    ppermute x4 -> x3, starting transfers between devices: 9.73 us -> 7.41 us  [flip_chan(): return lax.ppermute(values, 'chan', [(i, i ^ flip) for i in range(CHAN)])]
  transfers between devices with their start and end apart: 6 -> 5, of which waited for: 5 -> 5; matrix products, arithmetic and copies ran while one was open for 1% -> 1% of each run, Pallas kernels for 4% -> 4%
where the time goes in v5:
time: 103 us; the launch traced here: 101 us
  blocking collectives  43.6 us (42%)
  waiting for transfers between devices  27.2 us (26%)
  starting transfers between devices  16.9 us (16%)
  Pallas kernels  11.3 us (11%)
    all_to_all x1, blocking collectives, exchange(): return lax.all_to_all(cut, 'ctx', split_axis=0, concat_axis=0, tiled=True)  43.6 us
    all_to_all x2, waiting for transfers between devices, exchange(): return lax.all_to_all(cut, 'ctx', split_axis=0, concat_axis=0, tiled=True)  14.6 us
    ppermute x3, waiting for transfers between devices, flip_chan(): return lax.ppermute(values, 'chan', [(i, i ^ flip) for i in range(CHAN)])  12.6 us
    pallas_call x5, Pallas kernels, call(): pl.pallas_call(kernel, out_shape=shapes if many else shapes[0], in_specs=...  11.3 us
    all_to_all x2, starting transfers between devices, exchange(): return lax.all_to_all(cut, 'ctx', split_axis=0, concat_axis=0, tiled=True)  9.53 us
    ppermute x3, starting transfers between devices, flip_chan(): return lax.ppermute(values, 'chan', [(i, i ^ flip) for i in range(CHAN)])  7.41 us
  transfers between devices with their start and end apart: 5, of which 5 were waited for; matrix products, arithmetic and copies ran while one was open for 1% of the time, Pallas kernels for 4%

profile of v5, /device:TPU:32, one launch (start us, length us, event | category | flops | bytes accessed | tf_op | source)
XLA Modules:
  0.0 100.8 jit_solution(132918972221358256)
XLA Ops:
  0.6 3.4 %forward_blocks.1 = f32[16,2,80,128]{3,2,1,0:T(8,128)} custom-call(f32[4,16384]{1,0:T(4,128)} %seq_ref.1, f32[4,16384]{1,0:T(4,128)} %cot_ref.1, f32[2,16384]{1,0:T(2,128)} %refs_2_.1, f32[256,128]{1,0:T(8,128)} %constant.18.clone.refs_3_, f32[256,256]{1,0:T(8,128)} %constant.19.clone.refs_4_, f32[2,128,128]{2,1,0:T(8,128)} %constant.20.clone.refs_5_), custom_call_target="tpu_custom_call" | custom-call | tf_op jit(solution)/shard_map/forward_blocks/pallas_call | solution.py:90
  4.1 0.0 copy-start.5
  4.1 0.0 copy-start.6
  4.1 43.6 %all_to_all.15 = f32[32,80,128]{2,1,0:T(8,128)S(1)} all-to-all(f32[32,80,128]{2,1,0:T(8,128)} %bitcast.7), channel_id=1, replica_groups=mesh['ctx'=32,'chan'=8] {'ctx'}, dimensions={0} | all-to-all | bytes 2621440 | tf_op jit(solution)/shard_map/all_to_all | solution.py:257
  47.7 0.0 copy-start.7
  47.7 0.0 copy-done.5
  47.7 0.0 copy-done.6
  47.7 1.6 %taps_products.1 = f32[512,128]{1,0:T(8,128)} custom-call(f32[2560,128]{1,0:T(8,128)S(1)} %bitcast.5, f32[128,64]{1,0:T(8,128)S(1)} %copy-done.5, f32[64,128]{1,0:T(8,128)S(1)} %copy-done.6), custom_call_target="tpu_custom_call" | custom-call | tf_op jit(solution)/shard_map/taps_products/pallas_call | solution.py:90
  49.4 4.8 %all-to-all-start.1 = ((f32[32,16,128]{2,1,0:T(8,128)}), f32[32,16,128]{2,1,0:T(8,128)S(1)}, u32[]{:S(2)}, u32[]{:S(2)}) async-start(f32[32,16,128]{2,1,0:T(8,128)} %bitcast.2), calls=%async_computation.1 | async-start | bytes 524288 | tf_op jit(solution)/shard_map/all_to_all | solution.py:257
  54.1 0.0 copy-done.7
  54.1 3.1 %products.1 = f32[2048,128]{1,0:T(8,128)} custom-call(f32[2560,128]{1,0:T(8,128)S(1)} %bitcast.6, f32[128,64]{1,0:T(8,128)S(1)} %copy-done.5, f32[64,128]{1,0:T(8,128)S(1)} %copy-done.7, f32[64,128]{1,0:T(8,128)S(1)} %copy-done.6), custom_call_target="tpu_custom_call" | custom-call | tf_op jit(solution)/shard_map/products/pallas_call | solution.py:90
  57.2 0.0 copy-start
  57.2 0.0 copy-start.3
  57.2 0.0 copy-start.4
  57.2 8.4 %all-to-all-done.1.in_ref = f32[32,16,128]{2,1,0:T(8,128)S(1)} async-done(((f32[32,16,128]{2,1,0:T(8,128)}), f32[32,16,128]{2,1,0:T(8,128)S(1)}, u32[]{:S(2)}, u32[]{:S(2)}) %all-to-all-start.1) | async-done | bytes 262176 | tf_op jit(solution)/shard_map/all_to_all | solution.py:257
  65.6 4.8 %all-to-all-start.2 = ((f32[32,64,128]{2,1,0:T(8,128)}), f32[32,64,128]{2,1,0:T(8,128)S(1)}, u32[]{:S(2)}, u32[]{:S(2)}) async-start(f32[32,64,128]{2,1,0:T(8,128)} %bitcast.3), calls=%async_computation.2 | async-start | bytes 2097152 | tf_op jit(solution)/shard_map/all_to_all | solution.py:257
  70.4 0.0 copy-done
  70.4 0.0 copy-done.3
  70.4 0.0 copy-done.4
  70.5 0.0 copy-start.8
  70.5 0.0 copy-start.1
  70.5 0.0 copy-start.2
  70.5 0.9 taps_blocks.1
  71.4 1.6 %collective-permute-start = (f32[2,16384]{1,0:T(2,128)S(1)}, f32[2,16384]{1,0:T(2,128)S(1)}, u32[]{:S(2)}, u32[]{:S(2)}) collective-permute-start(f32[2,16384]{1,0:T(2,128)S(1)} %taps_blocks.1), channel_id=1, source_target_pairs={{0,1},{1,0},{2,3},{3,2},{4,5},{5,4},{6,7},{7,6},{8,9},{9,8},{10,11... | collective-permute-start | bytes 393224 | tf_op jit(solution)/shard_map/ppermute | solution.py:261
  73.0 4.1 %collective-permute-done = f32[2,16384]{1,0:T(2,128)S(1)} collective-permute-done((f32[2,16384]{1,0:T(2,128)S(1)}, f32[2,16384]{1,0:T(2,128)S(1)}, u32[]{:S(2)}, u32[]{:S(2)}) %collective-permute-start) | collective-permute-done | bytes 131104 | tf_op jit(solution)/shard_map/ppermute | solution.py:261
  77.0 0.1 add.9
  77.1 2.8 %collective-permute-start.1 = (f32[2,16384]{1,0:T(2,128)S(1)}, f32[2,16384]{1,0:T(2,128)S(1)}, u32[]{:S(2)}, u32[]{:S(2)}) collective-permute-start(f32[2,16384]{1,0:T(2,128)S(1)} %add.9), channel_id=1, source_target_pairs={{0,3},{1,2},{2,1},{3,0},{4,7},{5,6},{6,5},{7,4},{8,11},{9,10},{10,... | collective-permute-start | bytes 393224 | tf_op jit(solution)/shard_map/ppermute | solution.py:261
  79.9 3.4 %collective-permute-done.1 = f32[2,16384]{1,0:T(2,128)S(1)} collective-permute-done((f32[2,16384]{1,0:T(2,128)S(1)}, f32[2,16384]{1,0:T(2,128)S(1)}, u32[]{:S(2)}, u32[]{:S(2)}) %collective-permute-start.1) | collective-permute-done | bytes 131104 | tf_op jit(solution)/shard_map/ppermute | solution.py:261
  83.4 0.1 add.10
  83.4 3.0 %collective-permute-start.2 = (f32[2,16384]{1,0:T(2,128)S(1)}, f32[2,16384]{1,0:T(2,128)S(1)}, u32[]{:S(2)}, u32[]{:S(2)}) collective-permute-start(f32[2,16384]{1,0:T(2,128)S(1)} %add.10), channel_id=1, source_target_pairs={{0,4},{1,5},{2,6},{3,7},{4,0},{5,1},{6,2},{7,3},{8,12},{9,13},{10,... | collective-permute-start | bytes 393224 | tf_op jit(solution)/shard_map/ppermute | solution.py:261
  86.4 0.0 copy-done.8
  86.4 0.1 copy.16.skip_ref
  86.5 5.1 %collective-permute-done.2 = f32[2,16384]{1,0:T(2,128)S(1)} collective-permute-done((f32[2,16384]{1,0:T(2,128)S(1)}, f32[2,16384]{1,0:T(2,128)S(1)}, u32[]{:S(2)}, u32[]{:S(2)}) %collective-permute-start.2) | collective-permute-done | bytes 131104 | tf_op jit(solution)/shard_map/ppermute | solution.py:261
  91.6 0.7 add.11
  92.3 6.2 %all-to-all-done.2.in_ref = f32[32,64,128]{2,1,0:T(8,128)S(1)} async-done(((f32[32,64,128]{2,1,0:T(8,128)}), f32[32,64,128]{2,1,0:T(8,128)S(1)}, u32[]{:S(2)}, u32[]{:S(2)}) %all-to-all-start.2) | async-done | bytes 1048608 | tf_op jit(solution)/shard_map/all_to_all | solution.py:257
  98.6 0.0 copy-done.1
  98.6 0.0 copy-done.2
  98.6 2.2 %inverse_blocks.1 = (f32[4,16384]{1,0:T(4,128)}, f32[4,16384]{1,0:T(4,128)}) custom-call(f32[32,64,128]{2,1,0:T(8,128)S(1)} %all-to-all-done.2.in_ref, f32[4,16384]{1,0:T(4,128)S(1)} %copy-done.1, f32[4,16384]{1,0:T(4,128)S(1)} %copy-done.2, f32[4,1]{1,0:T(4,128)S(1)} %copy.16.skip_ref, f32[256,256]{1,0:T(8,128)S(1)} %copy-done.3, f32[256,512]{1,0:T(8,128)S(1)} %copy-done, ...), custom_call_target="tpu_custom_call" | custom-call | tf_op jit(solution)/shard_map/inverse_blocks/pallas_call | solution.py:90
Async XLA Ops:
  4.1 43.7 %copy-start.5 = (f32[128,64]{1,0:T(8,128)S(1)}, f32[128,64]{1,0:T(8,128)}, u32[]{:S(2)}) copy-start(f32[128,64]{1,0:T(8,128)} %constant.21.clone.there_ref) | copy-start | bytes 98308
  4.1 43.7 %copy-start.6 = (f32[64,128]{1,0:T(8,128)S(1)}, f32[64,128]{1,0:T(8,128)}, u32[]{:S(2)}) copy-start(f32[64,128]{1,0:T(8,128)} %constant.22.clone.adjoint_ref) | copy-start | bytes 98308
  47.7 6.4 %copy-start.7 = (f32[64,128]{1,0:T(8,128)S(1)}, f32[64,128]{1,0:T(8,128)}, u32[]{:S(2)}) copy-start(f32[64,128]{1,0:T(8,128)} %constant.23.clone.back_ref) | copy-start | bytes 98308
  49.4 16.3 %all-to-all-start.1 = ((f32[32,16,128]{2,1,0:T(8,128)}), f32[32,16,128]{2,1,0:T(8,128)S(1)}, u32[]{:S(2)}, u32[]{:S(2)}) async-start(f32[32,16,128]{2,1,0:T(8,128)} %bitcast.2), calls=%async_computation.1 | async-start | bytes 524288 | tf_op jit(solution)/shard_map/all_to_all | solution.py:257
  57.2 13.2 %copy-start = (f32[256,512]{1,0:T(8,128)S(1)}, f32[256,512]{1,0:T(8,128)}, u32[]{:S(2)}) copy-start(f32[256,512]{1,0:T(8,128)} %constant.25.clone.outer_ref) | copy-start | bytes 1572868
  57.2 13.2 %copy-start.3 = (f32[256,256]{1,0:T(8,128)S(1)}, f32[256,256]{1,0:T(8,128)}, u32[]{:S(2)}) copy-start(f32[256,256]{1,0:T(8,128)} %constant.24.clone.inner_ref) | copy-start | bytes 786436
  57.2 13.2 %copy-start.4 = (f32[2,256,128]{2,1,0:T(8,128)S(1)}, f32[2,256,128]{2,1,0:T(8,128)}, u32[]{:S(2)}) copy-start(f32[2,256,128]{2,1,0:T(8,128)} %constant.26.clone.twist_ref) | copy-start | bytes 786436
  65.6 32.9 %all-to-all-start.2 = ((f32[32,64,128]{2,1,0:T(8,128)}), f32[32,64,128]{2,1,0:T(8,128)S(1)}, u32[]{:S(2)}, u32[]{:S(2)}) async-start(f32[32,64,128]{2,1,0:T(8,128)} %bitcast.3), calls=%async_computation.2 | async-start | bytes 2097152 | tf_op jit(solution)/shard_map/all_to_all | solution.py:257
  70.5 16.0 %copy-start.8 = (f32[4]{0:T(128)S(1)}, f32[4]{0:T(128)}, u32[]{:S(2)}) copy-start(f32[4]{0:T(128)} %param.15) | copy-start | bytes 52
  70.5 28.1 %copy-start.1 = (f32[4,16384]{1,0:T(4,128)S(1)}, f32[4,16384]{1,0:T(4,128)}, u32[]{:S(2)}) copy-start(f32[4,16384]{1,0:T(4,128)} %seq_ref.1) | copy-start | bytes 786436
  70.5 28.1 %copy-start.2 = (f32[4,16384]{1,0:T(4,128)S(1)}, f32[4,16384]{1,0:T(4,128)}, u32[]{:S(2)}) copy-start(f32[4,16384]{1,0:T(4,128)} %cot_ref.1) | copy-start | bytes 786436
  71.4 5.6 %collective-permute-start = (f32[2,16384]{1,0:T(2,128)S(1)}, f32[2,16384]{1,0:T(2,128)S(1)}, u32[]{:S(2)}, u32[]{:S(2)}) collective-permute-start(f32[2,16384]{1,0:T(2,128)S(1)} %taps_blocks.1), channel_id=1, source_target_pairs={{0,1},{1,0},{2,3},{3,2},{4,5},{5,4},{6,7},{7,6},{8,9},{9,8},{10,11... | collective-permute-start | bytes 393224 | tf_op jit(solution)/shard_map/ppermute | solution.py:261
  77.1 6.3 %collective-permute-start.1 = (f32[2,16384]{1,0:T(2,128)S(1)}, f32[2,16384]{1,0:T(2,128)S(1)}, u32[]{:S(2)}, u32[]{:S(2)}) collective-permute-start(f32[2,16384]{1,0:T(2,128)S(1)} %add.9), channel_id=1, source_target_pairs={{0,3},{1,2},{2,1},{3,0},{4,7},{5,6},{6,5},{7,4},{8,11},{9,10},{10,... | collective-permute-start | bytes 393224 | tf_op jit(solution)/shard_map/ppermute | solution.py:261
  83.4 8.2 %collective-permute-start.2 = (f32[2,16384]{1,0:T(2,128)S(1)}, f32[2,16384]{1,0:T(2,128)S(1)}, u32[]{:S(2)}, u32[]{:S(2)}) collective-permute-start(f32[2,16384]{1,0:T(2,128)S(1)} %add.10), channel_id=1, source_target_pairs={{0,4},{1,5},{2,6},{3,7},{4,0},{5,1},{6,2},{7,3},{8,12},{9,13},{10,... | collective-permute-start | bytes 393224 | tf_op jit(solution)/shard_map/ppermute | solution.py:261

commit v6 on v5

--- a/solution.py
+++ b/solution.py
@@ -14,10 +14,8 @@
 CHAN = 8
 OUT_ROWS = 80
 BACK_ROWS = 64
-TAPS_ROWS = 16
 PAIRS = ((0, 2), (1, 3), (4, 6), (5, 7), (8, 9))
 VMEM_LIMIT = 40 * 1024 * 1024
-VMEM_FULL = 60 * 1024 * 1024
 
 
 def make_tables():
@@ -41,7 +39,7 @@
     forward_inner = np.block([[cosine, -sine], [sine, cosine]])
     inverse_inner = np.block([[cosine, sine], [-sine, cosine]])
     return (
-        tuple(t.astype(single) for t in (forward_outer, forward_inner, twist)),
+        np.stack([forward_outer, forward_inner[:, :SIDE], forward_inner[:, SIDE:]]).astype(single),
         tuple(t.astype(single) for t in (inverse_inner, inverse_outer, twist[:, coarse])),
     )
 
@@ -82,18 +80,17 @@
     return dot(jnp.concatenate([lh, lh, ll], axis=1), jnp.concatenate([rh, rl, rh], axis=0))
 
 
-def call(kernel, name, out_shape, operands, scratch=(), own_copies=False):
-    space = pl.ANY if own_copies else pltpu.VMEM
+def call(kernel, name, out_shape, operands, scratch=()):
     many = isinstance(out_shape[0], tuple)
     shapes = tuple(jax.ShapeDtypeStruct(s, jnp.float32) for s in (out_shape if many else (out_shape,)))
-    outs = (pl.BlockSpec(memory_space=space),) * len(shapes)
+    outs = (pl.BlockSpec(memory_space=pltpu.VMEM),) * len(shapes)
     return pl.pallas_call(
         kernel,
         out_shape=shapes if many else shapes[0],
-        in_specs=[pl.BlockSpec(memory_space=space)] * len(operands),
+        in_specs=[pl.BlockSpec(memory_space=pltpu.VMEM)] * len(operands),
         out_specs=outs if many else outs[0],
         scratch_shapes=list(scratch),
-        compiler_params=pltpu.CompilerParams(vmem_limit_bytes=VMEM_FULL if own_copies else VMEM_LIMIT),
+        compiler_params=pltpu.CompilerParams(vmem_limit_bytes=VMEM_LIMIT),
         name=name,
     )(*operands)
 
@@ -103,27 +100,35 @@
         rows[pl.ds(first * SIDE + a, count, stride=SIDE), :] = source[:, a * SIDE : (a + 1) * SIDE]
 
 
-def forward_kernel(*refs):
-    sources, out_ref, held, rows, sent, sems = refs[:6], refs[6], refs[7:13], refs[13], refs[14], refs[15]
-    copies = [pltpu.make_async_copy(s, h, sems.at[i]) for i, (s, h) in enumerate(zip(sources, held))]
-    for copy in copies:
-        copy.start()
-    seq_ref, cot_ref, taps_ref, outer_ref, inner_ref, twist_ref = held
-    copies[0].wait()
+def twist_kernel(twist_ref):
+    c = lax.broadcasted_iota(jnp.int32, (SIDE, SIDE), 0).astype(jnp.float32)
+    b = lax.broadcasted_iota(jnp.int32, (SIDE, SIDE), 1).astype(jnp.float32)
+    angle = (c + 0.25) * b * (2.0 * np.pi / BLOCK)
+    twist_ref[0] = jnp.cos(angle)
+    twist_ref[1] = jnp.sin(angle)
+
+
+def twist_table():
+    return pl.pallas_call(
+        twist_kernel,
+        out_shape=jax.ShapeDtypeStruct((2, SIDE, SIDE), jnp.float32),
+        out_specs=pl.BlockSpec(memory_space=pltpu.VMEM),
+        compiler_params=pltpu.CompilerParams(vmem_limit_bytes=4 * 1024 * 1024),
+        cost_estimate=pl.CostEstimate(flops=4_000_000_000, bytes_accessed=8_000_000, transcendentals=32768),
+        name="twist_table",
+    )()
+
+
+def forward_kernel(seq_ref, cot_ref, taps_ref, tables_ref, twist_ref, out_ref, rows):
     spread(seq_ref, rows, 0, 4)
-    copies[1].wait()
     spread(cot_ref, rows, 4, 4)
-    copies[2].wait()
     spread(taps_ref, rows, 8, 2)
-    for copy in copies[3:]:
-        copy.wait()
 
     signals = jnp.concatenate([rows[i * SIDE : (i + 1) * SIDE, :] for i in range(10)], axis=1)
-    opened = dot_wide(outer_ref[...], signals)
+    opened = dot_wide(tables_ref[0], signals)
     cosine, sine = twist_ref[0], twist_ref[1]
-    inner = inner_ref[...]
+    inner = jnp.concatenate([tables_ref[1], tables_ref[2]], axis=1)
     low = lax.broadcasted_iota(jnp.int32, (SIDE // 8, 8, SIDE), 1) < SUB
-    leaving = []
     for p, pair in enumerate(PAIRS):
         twisted = []
         for i in pair:
@@ -136,24 +141,28 @@
                 spectrum[i * SIDE : (i + 1) * SIDE, h * SIDE : (h + 1) * SIDE].reshape(SIDE // 8, 8, SIDE)
                 for i in range(2)
             )
-            sent[p, :, 0, 8 * h : 8 * h + 8, :] = jnp.where(low, first, pltpu.roll(second, SUB, 1))
-            sent[p, :, 1, 8 * h : 8 * h + 8, :] = jnp.where(low, pltpu.roll(first, SUB, 1), second)
-        copy = pltpu.make_async_copy(sent.at[p], out_ref.at[:, :, 16 * p : 16 * p + 16, :], sems.at[6 + p])
-        copy.start()
-        leaving.append(copy)
-    for copy in leaving:
-        copy.wait()
+            lines = slice(16 * p + 8 * h, 16 * p + 8 * h + 8)
+            out_ref[:, 0, lines, :] = jnp.where(low, first, pltpu.roll(second, SUB, 1))
+            out_ref[:, 1, lines, :] = jnp.where(low, pltpu.roll(first, SUB, 1), second)
 
 
 def forward_blocks(sequence, cotangent, taps):
-    operands = (sequence, cotangent, taps) + tuple(jnp.asarray(t) for t in FORWARD_TABLES)
-    scratch = [pltpu.VMEM(v.shape, v.dtype) for v in operands] + [
-        pltpu.VMEM((10 * SIDE, SIDE), jnp.float32),
-        pltpu.VMEM((5, BLOCKS // 2, 2, 16, SIDE), jnp.float32),
-        pltpu.SemaphoreType.DMA((11,)),
-    ]
-    shape = (BLOCKS // 2, 2, OUT_ROWS, SIDE)
-    return call(forward_kernel, "forward_blocks", shape, operands, scratch, True)
+    operands = (sequence, cotangent, taps, jnp.asarray(FORWARD_TABLES), twist_table())
+    scratch = [pltpu.VMEM((10 * SIDE, SIDE), jnp.float32)]
+    return call(forward_kernel, "forward_blocks", (BLOCKS // 2, 2, OUT_ROWS, SIDE), operands, scratch)
+
+
+def stacked(table):
+    high, low = split(table)
+    return jnp.concatenate(
+        [jnp.concatenate([high, high], axis=1), jnp.concatenate([low, jnp.zeros_like(low)], axis=1)], axis=0
+    )
+
+
+def dot_stacked(left, right):
+    both = dot(left, jnp.concatenate(split(right), axis=0))
+    half = both.shape[0] // 2
+    return both[:half] + both[half:]
 
 
 def points_of(in_ref, there, p):
@@ -167,44 +176,53 @@
     return points[:POINTS], points[POINTS:]
 
 
-def blocks_of(ref, p, width, table, real, imag):
-    blocks = dot_wide(table, jnp.concatenate([real, imag], axis=0))
+def blocks_of(ref, table, real, imag):
+    blocks = dot_stacked(table, jnp.concatenate([real, imag], axis=0))
     for h in range(2):
         for r in range(8):
-            ref[pl.ds(16 * p + 8 * h + r, BLOCKS, stride=width), :] = blocks[
+            ref[pl.ds(8 * h + r, BLOCKS, stride=16), :] = blocks[
                 BLOCKS * h : BLOCKS * (h + 1), r * SIDE : (r + 1) * SIDE
             ]
 
 
-def taps_products_kernel(in_ref, there_ref, adjoint_ref, taps_ref):
-    there = there_ref[...]
+def middle_kernel(in_ref, there_ref, back_ref, adjoint_ref, out_ref, taps_ref, sent, sems):
+    there, back, adjoint = there_ref[...], stacked(back_ref[...]), stacked(adjoint_ref[...])
+    leaving = []
+
+    def leave(p, table, real, imag):
+        blocks_of(sent.at[p].reshape(BLOCKS * 16, SIDE), table, real, imag)
+        copy = pltpu.make_async_copy(sent.at[p], out_ref.at[:, 16 * p : 16 * p + 16, :], sems.at[p])
+        copy.start()
+        leaving.append(copy)
+
+    hr, hi = points_of(in_ref, there, 4)
     real = imag = 0.0
     for q in range(2):
         xr, xi = points_of(in_ref, there, q)
+        leave(q, back, hr * xr - hi * xi, hr * xi + hi * xr)
         gr, gi = points_of(in_ref, there, 2 + q)
+        leave(2 + q, adjoint, hr * gr + hi * gi, hr * gi - hi * gr)
         real = real + (xr * gr + xi * gi)
         imag = imag + (xr * gi - xi * gr)
-    blocks_of(taps_ref, 0, TAPS_ROWS, adjoint_ref[...], real, imag)
-
-
-def taps_products(spectra):
-    operands = (spectra, jnp.asarray(THERE), jnp.asarray(ADJOINT))
-    return call(taps_products_kernel, "taps_products", (BLOCKS * TAPS_ROWS, SIDE), operands)
-
-
-def products_kernel(in_ref, there_ref, back_ref, adjoint_ref, out_ref):
-    there, back, adjoint = there_ref[...], back_ref[...], adjoint_ref[...]
-    hr, hi = points_of(in_ref, there, 4)
-    for q in range(2):
-        xr, xi = points_of(in_ref, there, q)
-        blocks_of(out_ref, q, BACK_ROWS, back, hr * xr - hi * xi, hr * xi + hi * xr)
-        gr, gi = points_of(in_ref, there, 2 + q)
-        blocks_of(out_ref, 2 + q, BACK_ROWS, adjoint, hr * gr + hi * gi, hr * gi - hi * gr)
-
-
-def products(spectra):
+    blocks_of(taps_ref, adjoint, real, imag)
+    for copy in leaving:
+        copy.wait()
+
+
+def middle_blocks(spectra):
     operands = (spectra,) + tuple(jnp.asarray(t) for t in (THERE, BACK, ADJOINT))
-    return call(products_kernel, "products", (BLOCKS * BACK_ROWS, SIDE), operands)
+    return pl.pallas_call(
+        middle_kernel,
+        out_shape=(
+            jax.ShapeDtypeStruct((BLOCKS, BACK_ROWS, SIDE), jnp.float32),
+            jax.ShapeDtypeStruct((BLOCKS * 16, SIDE), jnp.float32),
+        ),
+        in_specs=[pl.BlockSpec(memory_space=pltpu.VMEM)] * 4,
+        out_specs=(pl.BlockSpec(memory_space=pl.ANY), pl.BlockSpec(memory_space=pltpu.VMEM)),
+        scratch_shapes=[pltpu.VMEM((4, BLOCKS, 16, SIDE), jnp.float32), pltpu.SemaphoreType.DMA((4,))],
+        compiler_params=pltpu.CompilerParams(vmem_limit_bytes=VMEM_LIMIT),
+        name="middle_blocks",
+    )(*operands)
 
 
 def close(in_ref, inner_ref, outer_ref, twist_ref, rows, places):
@@ -269,8 +287,8 @@
 
 def body(sequence, filter_taps, skip_gain, cotangent):
     spectra = exchange(forward_blocks(sequence, cotangent, filter_taps)).reshape(BLOCKS * OUT_ROWS, SIDE)
-    taps = exchange(taps_products(spectra))
-    back = products(spectra)
+    back, taps = middle_blocks(spectra)
+    taps = exchange(taps)
     taps, back = lax.optimization_barrier((taps, back))
     taps_grad = sum_over_chan(taps_blocks(taps))
     convolved, seq_grad = inverse_blocks(exchange(back), sequence, cotangent, skip_gain)

time: 103 us -> 102 us (level)
  blocking collectives: 43.6 us -> 59.1 us
  waiting for transfers between devices: 27.2 us -> 18.8 us
  starting transfers between devices: 16.9 us -> 12 us
  Pallas kernels: 11.3 us -> 7.44 us
    all_to_all x1 -> x2, blocking collectives: 43.6 us -> 59.1 us  [exchange(): return lax.all_to_all(cut, 'ctx', split_axis=0, concat_axis=0, tiled=True)]
    all_to_all x2 -> x1, waiting for transfers between devices: 14.6 us -> 6.23 us  [exchange(): return lax.all_to_all(cut, 'ctx', split_axis=0, concat_axis=0, tiled=True)]
    pallas_call x5 -> x3, Pallas kernels: 11.3 us -> 4.54 us  [call(): pl.pallas_call(kernel, out_shape=shapes if many else shapes[0], in_specs=...]
    all_to_all x2 -> x1, starting transfers between devices: 9.53 us -> 4.55 us  [exchange(): return lax.all_to_all(cut, 'ctx', split_axis=0, concat_axis=0, tiled=True)]
    pallas_call x0 -> x2, Pallas kernels: none -> 2.9 us  [the longest x1 2.64 us: middle_blocks(): pl.pallas_call(middle_kernel, out_shape=(jax.ShapeDtypeStruct((BLOCKS, BA...]
  transfers between devices with their start and end apart: 5 -> 4, of which waited for: 5 -> 4; matrix products, arithmetic and copies ran while one was open for 1% -> 1% of each run, Pallas kernels for 4% -> 1%
where the time goes in v6:
time: 102 us; the launch traced here: 100 us
  blocking collectives  59.1 us (58%)
  waiting for transfers between devices  18.8 us (18%)
  starting transfers between devices  12 us (12%)
  Pallas kernels  7.44 us (7%)
  local copies, waits for them, and re-layouts  1.04 us (1%)
    all_to_all x2, blocking collectives, exchange(): return lax.all_to_all(cut, 'ctx', split_axis=0, concat_axis=0, tiled=True)  59.1 us
    ppermute x3, waiting for transfers between devices, flip_chan(): return lax.ppermute(values, 'chan', [(i, i ^ flip) for i in range(CHAN)])  12.6 us
    ppermute x3, starting transfers between devices, flip_chan(): return lax.ppermute(values, 'chan', [(i, i ^ flip) for i in range(CHAN)])  7.41 us
    all_to_all x1, waiting for transfers between devices, exchange(): return lax.all_to_all(cut, 'ctx', split_axis=0, concat_axis=0, tiled=True)  6.23 us
    all_to_all x1, starting transfers between devices, exchange(): return lax.all_to_all(cut, 'ctx', split_axis=0, concat_axis=0, tiled=True)  4.55 us
    pallas_call x3, Pallas kernels, call(): pl.pallas_call(kernel, out_shape=shapes if many else shapes[0], in_specs=...  4.54 us
    pallas_call x1, Pallas kernels, middle_blocks(): pl.pallas_call(middle_kernel, out_shape=(jax.ShapeDtypeStruct((BLOCKS, BA...  2.64 us
  transfers between devices with their start and end apart: 4, of which 4 were waited for; matrix products, arithmetic and copies ran while one was open for 1% of the time, Pallas kernels for 1%

profile of v6, /device:TPU:32, one launch (start us, length us, event | category | flops | bytes accessed | tf_op | source)
XLA Modules:
  0.0 100.1 jit_solution(17037926545840093185)
XLA Ops:
  0.6 0.0 copy-start.5
  0.6 0.0 copy-start.1
  0.7 0.0 copy-start.6
  0.7 0.0 copy-start.2
  0.7 0.3 twist_table.1.twist_ref
  0.9 0.7 copy-done.5
  1.6 0.1 copy-done.1
  1.7 0.0 copy-done.6
  1.7 0.1 copy-done.2
  1.8 1.4 %forward_blocks.1 = f32[16,2,80,128]{3,2,1,0:T(8,128)S(1)} custom-call(f32[4,16384]{1,0:T(4,128)S(1)} %copy-done.1, f32[4,16384]{1,0:T(4,128)S(1)} %copy-done.2, f32[2,16384]{1,0:T(2,128)S(1)} %copy-done.6, f32[3,256,128]{2,1,0:T(8,128)S(1)} %copy-done.5, f32[2,128,128]{2,1,0:T(8,128)S(1)} %twist_table.1.twist_ref), custom_call_target="tpu_custom_call" | custom-call | tf_op jit(solution)/shard_map/forward_blocks/pallas_call | solution.py:87
  3.3 0.0 copy-start.7
  3.3 0.0 copy-start.8
  3.3 0.0 copy-start.9
  3.3 43.4 %all_to_all.15 = f32[32,80,128]{2,1,0:T(8,128)S(1)} all-to-all(f32[32,80,128]{2,1,0:T(8,128)S(1)} %bitcast.5), channel_id=1, replica_groups=mesh['ctx'=32,'chan'=8] {'ctx'}, dimensions={0} | all-to-all | bytes 2621440 | tf_op jit(solution)/shard_map/all_to_all | solution.py:275
  46.7 0.0 copy-done.7
  46.7 0.0 copy-done.8
  46.7 0.0 copy-done.9
  46.7 2.6 %middle_blocks.1 = (f32[32,64,128]{2,1,0:T(8,128)}, f32[512,128]{1,0:T(8,128)S(1)}) custom-call(f32[2560,128]{1,0:T(8,128)S(1)} %bitcast.4, f32[128,64]{1,0:T(8,128)S(1)} %copy-done.7, f32[64,128]{1,0:T(8,128)S(1)} %copy-done.8, f32[64,128]{1,0:T(8,128)S(1)} %copy-done.9), custom_call_target="tpu_custom_call" | custom-call | tf_op jit(solution)/shard_map/middle_blocks/pallas_call | solution.py:214
  49.4 0.0 copy-start
  49.4 0.0 copy-start.3
  49.4 0.0 copy-start.4
  49.4 15.7 %all_to_all.16.in_ref = f32[32,16,128]{2,1,0:T(8,128)S(1)} all-to-all(f32[32,16,128]{2,1,0:T(8,128)S(1)} %bitcast.6), channel_id=1, replica_groups=mesh['ctx'=32,'chan'=8] {'ctx'}, dimensions={0} | all-to-all | bytes 524288 | tf_op jit(solution)/shard_map/all_to_all | solution.py:275
  65.1 4.5 %all-to-all-start.2 = ((f32[32,64,128]{2,1,0:T(8,128)}), f32[32,64,128]{2,1,0:T(8,128)S(1)}, u32[]{:S(2)}, u32[]{:S(2)}) async-start(f32[32,64,128]{2,1,0:T(8,128)} %get-tuple-element.11), calls=%async_computation.2 | async-start | bytes 2097152 | tf_op jit(solution)/shard_map/all_to_all | solution.py:275
  69.7 0.0 copy-done
  69.7 0.0 copy-done.3
  69.7 0.0 copy-done.4
  69.7 0.0 copy-start.10
  69.7 0.9 taps_blocks.1
  70.6 1.6 %collective-permute-start = (f32[2,16384]{1,0:T(2,128)S(1)}, f32[2,16384]{1,0:T(2,128)S(1)}, u32[]{:S(2)}, u32[]{:S(2)}) collective-permute-start(f32[2,16384]{1,0:T(2,128)S(1)} %taps_blocks.1), channel_id=1, source_target_pairs={{0,1},{1,0},{2,3},{3,2},{4,5},{5,4},{6,7},{7,6},{8,9},{9,8},{10,11... | collective-permute-start | bytes 393224 | tf_op jit(solution)/shard_map/ppermute | solution.py:279
  72.2 4.1 %collective-permute-done = f32[2,16384]{1,0:T(2,128)S(1)} collective-permute-done((f32[2,16384]{1,0:T(2,128)S(1)}, f32[2,16384]{1,0:T(2,128)S(1)}, u32[]{:S(2)}, u32[]{:S(2)}) %collective-permute-start) | collective-permute-done | bytes 131104 | tf_op jit(solution)/shard_map/ppermute | solution.py:279
  76.3 0.1 add.9
  76.4 2.8 %collective-permute-start.1 = (f32[2,16384]{1,0:T(2,128)S(1)}, f32[2,16384]{1,0:T(2,128)S(1)}, u32[]{:S(2)}, u32[]{:S(2)}) collective-permute-start(f32[2,16384]{1,0:T(2,128)S(1)} %add.9), channel_id=1, source_target_pairs={{0,3},{1,2},{2,1},{3,0},{4,7},{5,6},{6,5},{7,4},{8,11},{9,10},{10,... | collective-permute-start | bytes 393224 | tf_op jit(solution)/shard_map/ppermute | solution.py:279
  79.2 3.4 %collective-permute-done.1 = f32[2,16384]{1,0:T(2,128)S(1)} collective-permute-done((f32[2,16384]{1,0:T(2,128)S(1)}, f32[2,16384]{1,0:T(2,128)S(1)}, u32[]{:S(2)}, u32[]{:S(2)}) %collective-permute-start.1) | collective-permute-done | bytes 131104 | tf_op jit(solution)/shard_map/ppermute | solution.py:279
  82.6 0.1 add.10
  82.7 3.0 %collective-permute-start.2 = (f32[2,16384]{1,0:T(2,128)S(1)}, f32[2,16384]{1,0:T(2,128)S(1)}, u32[]{:S(2)}, u32[]{:S(2)}) collective-permute-start(f32[2,16384]{1,0:T(2,128)S(1)} %add.10), channel_id=1, source_target_pairs={{0,4},{1,5},{2,6},{3,7},{4,0},{5,1},{6,2},{7,3},{8,12},{9,13},{10,... | collective-permute-start | bytes 393224 | tf_op jit(solution)/shard_map/ppermute | solution.py:279
  85.7 0.0 copy-done.10
  85.7 0.1 copy.14.skip_ref
  85.8 5.1 %collective-permute-done.2 = f32[2,16384]{1,0:T(2,128)S(1)} collective-permute-done((f32[2,16384]{1,0:T(2,128)S(1)}, f32[2,16384]{1,0:T(2,128)S(1)}, u32[]{:S(2)}, u32[]{:S(2)}) %collective-permute-start.2) | collective-permute-done | bytes 131104 | tf_op jit(solution)/shard_map/ppermute | solution.py:279
  90.9 0.7 add.11
  91.6 6.2 %all-to-all-done.2.in_ref = f32[32,64,128]{2,1,0:T(8,128)S(1)} async-done(((f32[32,64,128]{2,1,0:T(8,128)}), f32[32,64,128]{2,1,0:T(8,128)S(1)}, u32[]{:S(2)}, u32[]{:S(2)}) %all-to-all-start.2) | async-done | bytes 1048608 | tf_op jit(solution)/shard_map/all_to_all | solution.py:275
  97.8 2.2 %inverse_blocks.1 = (f32[4,16384]{1,0:T(4,128)}, f32[4,16384]{1,0:T(4,128)}) custom-call(f32[32,64,128]{2,1,0:T(8,128)S(1)} %all-to-all-done.2.in_ref, f32[4,16384]{1,0:T(4,128)S(1)} %copy-done.1, f32[4,16384]{1,0:T(4,128)S(1)} %copy-done.2, f32[4,1]{1,0:T(4,128)S(1)} %copy.14.skip_ref, f32[256,256]{1,0:T(8,128)S(1)} %copy-done.3, f32[256,512]{1,0:T(8,128)S(1)} %copy-done, ...), custom_call_target="tpu_custom_call" | custom-call | tf_op jit(solution)/shard_map/inverse_blocks/pallas_call | solution.py:87
Async XLA Ops:
  0.6 1.0 copy-start.5
  0.6 1.1 %copy-start.1 = (f32[4,16384]{1,0:T(4,128)S(1)}, f32[4,16384]{1,0:T(4,128)}, u32[]{:S(2)}) copy-start(f32[4,16384]{1,0:T(4,128)} %seq_ref.3) | copy-start | bytes 786436
  0.7 1.1 %copy-start.6 = (f32[2,16384]{1,0:T(2,128)S(1)}, f32[2,16384]{1,0:T(2,128)}, u32[]{:S(2)}) copy-start(f32[2,16384]{1,0:T(2,128)} %taps_ref.1) | copy-start | bytes 393220
  0.7 1.2 %copy-start.2 = (f32[4,16384]{1,0:T(4,128)S(1)}, f32[4,16384]{1,0:T(4,128)}, u32[]{:S(2)}) copy-start(f32[4,16384]{1,0:T(4,128)} %cot_ref.3) | copy-start | bytes 786436
  3.3 43.5 %copy-start.7 = (f32[128,64]{1,0:T(8,128)S(1)}, f32[128,64]{1,0:T(8,128)}, u32[]{:S(2)}) copy-start(f32[128,64]{1,0:T(8,128)} %constant.15.clone.there_ref) | copy-start | bytes 98308
  3.3 43.5 %copy-start.8 = (f32[64,128]{1,0:T(8,128)S(1)}, f32[64,128]{1,0:T(8,128)}, u32[]{:S(2)}) copy-start(f32[64,128]{1,0:T(8,128)} %constant.16.clone.back_ref) | copy-start | bytes 98308
  3.3 43.4 %copy-start.9 = (f32[64,128]{1,0:T(8,128)S(1)}, f32[64,128]{1,0:T(8,128)}, u32[]{:S(2)}) copy-start(f32[64,128]{1,0:T(8,128)} %constant.17.clone.adjoint_ref) | copy-start | bytes 98308
  49.4 20.3 %copy-start = (f32[256,512]{1,0:T(8,128)S(1)}, f32[256,512]{1,0:T(8,128)}, u32[]{:S(2)}) copy-start(f32[256,512]{1,0:T(8,128)} %constant.19.clone.outer_ref) | copy-start | bytes 1572868
  49.4 20.3 %copy-start.3 = (f32[256,256]{1,0:T(8,128)S(1)}, f32[256,256]{1,0:T(8,128)}, u32[]{:S(2)}) copy-start(f32[256,256]{1,0:T(8,128)} %constant.18.clone.inner_ref) | copy-start | bytes 786436
  49.4 20.3 %copy-start.4 = (f32[2,256,128]{2,1,0:T(8,128)S(1)}, f32[2,256,128]{2,1,0:T(8,128)}, u32[]{:S(2)}) copy-start(f32[2,256,128]{2,1,0:T(8,128)} %constant.20.clone.twist_ref) | copy-start | bytes 786436
  65.1 32.7 %all-to-all-start.2 = ((f32[32,64,128]{2,1,0:T(8,128)}), f32[32,64,128]{2,1,0:T(8,128)S(1)}, u32[]{:S(2)}, u32[]{:S(2)}) async-start(f32[32,64,128]{2,1,0:T(8,128)} %get-tuple-element.11), calls=%async_computation.2 | async-start | bytes 2097152 | tf_op jit(solution)/shard_map/all_to_all | solution.py:275
  69.7 15.9 %copy-start.10 = (f32[4]{0:T(128)S(1)}, f32[4]{0:T(128)}, u32[]{:S(2)}) copy-start(f32[4]{0:T(128)} %param.13) | copy-start | bytes 52
  70.6 5.6 %collective-permute-start = (f32[2,16384]{1,0:T(2,128)S(1)}, f32[2,16384]{1,0:T(2,128)S(1)}, u32[]{:S(2)}, u32[]{:S(2)}) collective-permute-start(f32[2,16384]{1,0:T(2,128)S(1)} %taps_blocks.1), channel_id=1, source_target_pairs={{0,1},{1,0},{2,3},{3,2},{4,5},{5,4},{6,7},{7,6},{8,9},{9,8},{10,11... | collective-permute-start | bytes 393224 | tf_op jit(solution)/shard_map/ppermute | solution.py:279
  76.4 6.3 %collective-permute-start.1 = (f32[2,16384]{1,0:T(2,128)S(1)}, f32[2,16384]{1,0:T(2,128)S(1)}, u32[]{:S(2)}, u32[]{:S(2)}) collective-permute-start(f32[2,16384]{1,0:T(2,128)S(1)} %add.9), channel_id=1, source_target_pairs={{0,3},{1,2},{2,1},{3,0},{4,7},{5,6},{6,5},{7,4},{8,11},{9,10},{10,... | collective-permute-start | bytes 393224 | tf_op jit(solution)/shard_map/ppermute | solution.py:279
  82.7 8.2 %collective-permute-start.2 = (f32[2,16384]{1,0:T(2,128)S(1)}, f32[2,16384]{1,0:T(2,128)S(1)}, u32[]{:S(2)}, u32[]{:S(2)}) collective-permute-start(f32[2,16384]{1,0:T(2,128)S(1)} %add.10), channel_id=1, source_target_pairs={{0,4},{1,5},{2,6},{3,7},{4,0},{5,1},{6,2},{7,3},{8,12},{9,13},{10,... | collective-permute-start | bytes 393224 | tf_op jit(solution)/shard_map/ppermute | solution.py:279

commit v7 on v6

v7 whole, which is shorter than its diff:
```python
import numpy as np
import jax
import jax.numpy as jnp
from jax import lax
from jax.experimental import pallas as pl
from jax.experimental.pallas import tpu as pltpu
from jax.sharding import PartitionSpec as P

SIDE = 128
HALF = SIDE // 2
BLOCK = SIDE * SIDE
BLOCKS = 32
CHAN = 8
OWNERS = BLOCKS * CHAN
POINTS = 2 * BLOCKS
SIGNALS = 8
THERE_ROWS = 9
BACK_ROWS = 10
VMEM_LIMIT = 40 * 1024 * 1024


def make_tables():
    digit = np.arange(SIDE)
    turn = 2.0 * np.pi
    single = np.float32
    angle = turn * ((digit[:, None] + 0.25) * digit[None, :] / SIDE)
    cosine, sine = np.cos(angle), np.sin(angle)
    forward_outer = np.concatenate([cosine, -sine], axis=0)
    factor = (BLOCKS * BLOCK) ** (-0.5) / BLOCK
    inverse_outer = factor * np.concatenate([cosine.T, -sine.T], axis=1)
    angle = turn * ((digit[:, None] * digit[None, :]) % SIDE / SIDE)
    cosine, sine = np.cos(angle), np.sin(angle)
    order = np.arange(2 * SIDE).reshape(2, 2, HALF).transpose(1, 0, 2).reshape(-1)
    forward_inner = np.block([[cosine, -sine], [sine, cosine]])[:, order]
    inverse_inner = np.block([[cosine, sine], [-sine, cosine]])[order, :]
    angle = turn * ((digit[:, None] + 0.25) * digit[None, :] / BLOCK)
    twist = np.stack([np.cos(angle), np.sin(angle)])
    return (
        np.stack([forward_outer, forward_inner[:, :SIDE], forward_inner[:, SIDE:]]).astype(single),
        tuple(t.astype(single) for t in (inverse_inner, inverse_outer, twist)),
    )


def make_block_tables():
    block = np.arange(BLOCKS)
    point = np.arange(POINTS)
    angle = 2.0 * np.pi * ((point[:, None] * block[None, :]) % POINTS) / POINTS
    cosine, sine = np.cos(angle), np.sin(angle)
    tables = [np.block([[cosine, sine], [-sine, cosine]])]
    step = np.exp(-2j * np.pi * point / POINTS)
    for spill in (1.0 + 1j * step, 1.0 - 1j * np.conj(step)):
        back = np.exp(1j * angle.T) * spill[None, :] / POINTS
        tables.append(np.block([[back.real, -back.imag], [back.imag, back.real]]))
    return tuple(t.astype(np.float32) for t in tables)


FORWARD_TABLES, INVERSE_TABLES = make_tables()
BLOCK_TABLES = make_block_tables()


def split(values):
    high = values.astype(jnp.bfloat16)
    return high, (values - high.astype(jnp.float32)).astype(jnp.bfloat16)


def dot(left, right):
    return jnp.dot(left, right, preferred_element_type=jnp.float32)


def dot_three(left, right):
    (lh, ll), (rh, rl) = split(left), split(right)
    return dot(lh, rh) + (dot(lh, rl) + dot(ll, rh))


def dot_wide(left, right):
    (lh, ll), (rh, rl) = split(left), split(right)
    return dot(jnp.concatenate([lh, lh, ll], axis=1), jnp.concatenate([rh, rl, rh], axis=0))


def stacked(table):
    high, low = split(table)
    return jnp.concatenate(
        [jnp.concatenate([high, high], axis=1), jnp.concatenate([low, jnp.zeros_like(low)], axis=1)], axis=0
    )


def dot_stacked(left, right):
    both = dot(left, jnp.concatenate(split(right), axis=0))
    half = both.shape[0] // 2
    return both[:half] + both[half:]


def call(kernel, name, out_shape, operands, scratch=()):
    many = isinstance(out_shape[0], tuple)
    shapes = tuple(jax.ShapeDtypeStruct(s, jnp.float32) for s in (out_shape if many else (out_shape,)))
    outs = (pl.BlockSpec(memory_space=pltpu.VMEM),) * len(shapes)
    return pl.pallas_call(
        kernel,
        out_shape=shapes if many else shapes[0],
        in_specs=[pl.BlockSpec(memory_space=pltpu.VMEM)] * len(operands),
        out_specs=outs if many else outs[0],
        scratch_shapes=list(scratch),
        compiler_params=pltpu.CompilerParams(vmem_limit_bytes=VMEM_LIMIT),
        name=name,
    )(*operands)


def twist_kernel(twist_ref):
    c = lax.broadcasted_iota(jnp.int32, (SIDE, SIDE), 0).astype(jnp.float32)
    b = lax.broadcasted_iota(jnp.int32, (SIDE, SIDE), 1).astype(jnp.float32)
    angle = (c + 0.25) * b * (2.0 * np.pi / BLOCK)
    twist_ref[0] = jnp.cos(angle)
    twist_ref[1] = jnp.sin(angle)


def twist_table():
    return pl.pallas_call(
        twist_kernel,
        out_shape=jax.ShapeDtypeStruct((2, SIDE, SIDE), jnp.float32),
        out_specs=pl.BlockSpec(memory_space=pltpu.VMEM),
        compiler_params=pltpu.CompilerParams(vmem_limit_bytes=4 * 1024 * 1024),
        cost_estimate=pl.CostEstimate(flops=4_000_000_000, bytes_accessed=8_000_000, transcendentals=32768),
        name="twist_table",
    )()


def forward_kernel(seq_ref, cot_ref, taps_ref, tables_ref, twist_ref, out_ref, rows):
    for first, count, source in ((0, 4, seq_ref), (4, 4, cot_ref), (SIGNALS, 2, taps_ref)):
        for a in range(SIDE):
            rows[pl.ds(first * SIDE + a, count, stride=SIDE), :] = source[:, a * SIDE : (a + 1) * SIDE]

    def row(index):
        return rows[index * SIDE : (index + 1) * SIDE, :]

    mine = jnp.where(lax.axis_index("chan") % 2 == 0, row(SIGNALS), row(SIGNALS + 1))
    opened = dot_wide(tables_ref[0], jnp.concatenate([row(i) for i in range(SIGNALS)] + [mine], axis=1))
    cosine, sine = twist_ref[0], twist_ref[1]
    inner = jnp.concatenate([tables_ref[1], tables_ref[2]], axis=1)
    for group in ((0, 1), (2, 3), (4, 5), (6, 7), (8,)):
        twisted = []
        for i in group:
            real = opened[:SIDE, i * SIDE : (i + 1) * SIDE]
            imag = opened[SIDE:, i * SIDE : (i + 1) * SIDE]
            twisted.append(jnp.concatenate([real * cosine + imag * sine, imag * cosine - real * sine], axis=1))
        spectra = dot_three(jnp.concatenate(twisted, axis=0), inner)
        for place, i in enumerate(group):
            for half in range(2):
                out_ref[pl.ds(THERE_ROWS * half + i, SIDE, stride=2 * THERE_ROWS), :] = spectra[
                    place * SIDE : (place + 1) * SIDE, half * SIDE : (half + 1) * SIDE
                ]


def forward_blocks(sequence, cotangent, taps):
    operands = (sequence, cotangent, taps, jnp.asarray(FORWARD_TABLES), twist_table())
    scratch = [pltpu.VMEM((10 * SIDE, SIDE), jnp.float32)]
    return call(forward_kernel, "forward_blocks", (OWNERS * THERE_ROWS, SIDE), operands, scratch)


def middle_kernel(in_ref, there_ref, back_ref, adjoint_ref, out_ref):
    there, back, adjoint = there_ref[...], stacked(back_ref[...]), stacked(adjoint_ref[...])
    low = lax.broadcasted_iota(jnp.int32, (BLOCKS, SIDE), 1) < HALF

    def turn(values):
        return pltpu.roll(values, HALF, 1)

    def arrived(chan, row):
        return in_ref[pl.ds(chan * THERE_ROWS + row, BLOCKS, stride=CHAN * THERE_ROWS), :]

    def leave(chan, row, values):
        out_ref[pl.ds(chan * BACK_ROWS + row, BLOCKS, stride=CHAN * BACK_ROWS), :] = values

    def points_of(first_chan, second_chan, rows):
        reals, imags = [], []
        for r in rows:
            first, second = arrived(first_chan, r), arrived(second_chan, r)
            reals.append(jnp.where(low, first, turn(second)))
            imags.append(jnp.where(low, turn(first), second))
        sides = [jnp.concatenate(reals, axis=1), jnp.concatenate(imags, axis=1)]
        points = dot_wide(there, jnp.concatenate(sides, axis=0))
        return points[:POINTS], points[POINTS:]

    def blocks_of(table, real, imag):
        blocks = dot_stacked(table, jnp.concatenate([real, imag], axis=0))
        return blocks[:BLOCKS], blocks[BLOCKS:]

    filters = [points_of(f, f, (SIGNALS,)) for f in range(2)]
    hr, hi = (jnp.concatenate([filters[f][part] for f in (0, 0, 1, 1)], axis=1) for part in range(2))
    wide = 4 * SIDE
    real = imag = 0.0
    for first in range(0, CHAN, 2):
        pr, pi = points_of(first, first + 1, range(SIGNALS))
        xr, xi, gr, gi = pr[:, :wide], pi[:, :wide], pr[:, wide:], pi[:, wide:]
        real = real + (xr * gr + xi * gi)
        imag = imag + (xr * gi - xi * gr)
        for row, (br, bi) in (
            (0, blocks_of(back, hr * xr - hi * xi, hr * xi + hi * xr)),
            (4, blocks_of(adjoint, hr * gr + hi * gi, hr * gi - hi * gr)),
        ):
            for r in range(4):
                cr, ci = br[:, r * SIDE : (r + 1) * SIDE], bi[:, r * SIDE : (r + 1) * SIDE]
                leave(first, row + r, jnp.where(low, cr, turn(ci)))
                leave(first + 1, row + r, jnp.where(low, turn(cr), ci))

    def over_channels(values):
        sums = [values[:, f * 2 * SIDE : f * 2 * SIDE + SIDE] + values[:, f * 2 * SIDE + SIDE : (f + 1) * 2 * SIDE] for f in range(2)]
        return jnp.concatenate([s + turn(s) for s in sums], axis=1)

    br, bi = blocks_of(adjoint, over_channels(real), over_channels(imag))
    for f in range(2):
        tap = jnp.where(low, br[:, f * SIDE : (f + 1) * SIDE], bi[:, f * SIDE : (f + 1) * SIDE])
        for chan in range(CHAN):
            leave(chan, SIGNALS + f, tap)


def middle_blocks(spectra):
    operands = (spectra,) + tuple(jnp.asarray(t) for t in BLOCK_TABLES)
    return call(middle_kernel, "middle_blocks", (OWNERS * BACK_ROWS, SIDE), operands)


def inverse_kernel(in_ref, seq_ref, cot_ref, skip_ref, inner_ref, outer_ref, twist_ref, y_ref, g_ref, f_ref, rows):
    cosine, sine = twist_ref[0], twist_ref[1]
    inner, outer = inner_ref[...], outer_ref[...]
    for group in ((0, 1), (2, 3), (4, 5), (6, 7), (8, 9)):
        both = jnp.concatenate(
            [
                jnp.concatenate(
                    [in_ref[pl.ds(BACK_ROWS * half + i, SIDE, stride=2 * BACK_ROWS), :] for half in range(2)], axis=1
                )
                for i in group
            ],
            axis=0,
        )
        turned = dot_three(both, inner)
        columns = []
        for place in range(2):
            real = turned[place * SIDE : (place + 1) * SIDE, :SIDE]
            imag = turned[place * SIDE : (place + 1) * SIDE, SIDE:]
            columns.append(jnp.concatenate([real * cosine - imag * sine, imag * cosine + real * sine], axis=0))
        closed = dot_three(outer, jnp.concatenate(columns, axis=1))
        for place, i in enumerate(group):
            rows[i * SIDE : (i + 1) * SIDE, :] = closed[:, place * SIDE : (place + 1) * SIDE]
    skip = jnp.broadcast_to(skip_ref[...], (4, SIDE))
    for a in range(SIDE):
        lanes = slice(a * SIDE, (a + 1) * SIDE)
        y_ref[:, lanes] = rows[pl.ds(a, 4, stride=SIDE), :] + skip * seq_ref[:, lanes]
        g_ref[:, lanes] = rows[pl.ds(4 * SIDE + a, 4, stride=SIDE), :] + skip * cot_ref[:, lanes]
        f_ref[:, lanes] = rows[pl.ds(8 * SIDE + a, 2, stride=SIDE), :]


def inverse_blocks(spectra, sequence, cotangent, skip_gain):
    operands = (spectra, sequence, cotangent, skip_gain[:, None]) + tuple(jnp.asarray(t) for t in INVERSE_TABLES)
    scratch = [pltpu.VMEM((10 * SIDE, SIDE), jnp.float32)]
    return call(inverse_kernel, "inverse_blocks", ((4, BLOCK), (4, BLOCK), (2, BLOCK)), operands, scratch)


def exchange(rows, tall):
    cut = rows.reshape(OWNERS, -1, tall, SIDE)
    return lax.all_to_all(cut, ("ctx", "chan"), split_axis=0, concat_axis=0, tiled=True).reshape(rows.shape)


def body(sequence, filter_taps, skip_gain, cotangent):
    spectra = exchange(forward_blocks(sequence, cotangent, filter_taps), 1)
    products = exchange(middle_blocks(spectra), 2)
    return inverse_blocks(products, sequence, cotangent, skip_gain)


def solution(mesh):
    return jax.shard_map(
        body,
        mesh=mesh,
        in_specs=(P("chan", "ctx"), P(None, "ctx"), P("chan"), P("chan", "ctx")),
        out_specs=(P("chan", "ctx"), P("chan", "ctx"), P(None, "ctx")),
        check_vma=False,
    )
```

time: 102 us -> 102 us (level)
  waiting for transfers between devices: 18.8 us -> 36.3 us
  blocking collectives: 59.1 us -> 47.9 us
  starting transfers between devices: 12 us -> 7.18 us
    all_to_all x1, waiting for transfers between devices: 6.23 us -> 36.3 us  [exchange(): lax.all_to_all(cut, ('ctx', 'chan'), split_axis=0, concat_axis=0, tiled=T...]
    ppermute x3 -> x0, waiting for transfers between devices: 12.6 us -> none  [flip_chan(): return lax.ppermute(values, 'chan', [(i, i ^ flip) for i in range(CHAN)])]
    all_to_all x2 -> x1, blocking collectives: 59.1 us -> 47.9 us  [exchange(): lax.all_to_all(cut, ('ctx', 'chan'), split_axis=0, concat_axis=0, tiled=T...]
    ppermute x3 -> x0, starting transfers between devices: 7.41 us -> none  [flip_chan(): return lax.ppermute(values, 'chan', [(i, i ^ flip) for i in range(CHAN)])]
    pallas_call x3, Pallas kernels: 4.54 us -> 7.74 us  [call(): pl.pallas_call(kernel, out_shape=shapes if many else shapes[0], in_specs=...]
    pallas_call x1 -> x0, Pallas kernels: 2.64 us -> none  [middle_blocks(): pl.pallas_call(middle_kernel, out_shape=(jax.ShapeDtypeStruct((BLOCKS, BA...]
    all_to_all x1, starting transfers between devices: 4.55 us -> 7.18 us  [exchange(): lax.all_to_all(cut, ('ctx', 'chan'), split_axis=0, concat_axis=0, tiled=T...]
  transfers between devices with their start and end apart: 4 -> 1, of which waited for: 4 -> 1; matrix products, arithmetic and copies ran while one was open for 1% -> 0% of each run, Pallas kernels for 1% -> 0%
where the time goes in v7:
time: 102 us; the launch traced here: 101 us
  blocking collectives  47.9 us (47%)
  waiting for transfers between devices  36.3 us (36%)
  Pallas kernels  7.99 us (8%)
  starting transfers between devices  7.18 us (7%)
  local copies, waits for them, and re-layouts  1.03 us (1%)
    all_to_all x1, blocking collectives, exchange(): lax.all_to_all(cut, ('ctx', 'chan'), split_axis=0, concat_axis=0, tiled=T...  47.9 us
    all_to_all x1, waiting for transfers between devices, exchange(): lax.all_to_all(cut, ('ctx', 'chan'), split_axis=0, concat_axis=0, tiled=T...  36.3 us
    pallas_call x3, Pallas kernels, call(): pl.pallas_call(kernel, out_shape=shapes if many else shapes[0], in_specs=...  7.74 us
    all_to_all x1, starting transfers between devices, exchange(): lax.all_to_all(cut, ('ctx', 'chan'), split_axis=0, concat_axis=0, tiled=T...  7.18 us
  transfers between devices with their start and end apart: 1, of which 1 were waited for; matrix products, arithmetic and copies ran while one was open for 0% of the time, Pallas kernels for 0%

profile of v7, /device:TPU:32, one launch (start us, length us, event | category | flops | bytes accessed | tf_op | source)
XLA Modules:
  0.0 101.1 jit_solution(7579677786021956717)
XLA Ops:
  0.6 0.0 copy-start.2
  0.6 0.0 copy-start
  0.7 0.0 copy-start.4
  0.7 0.0 copy-start.1
  0.7 0.3 twist_table.1.twist_ref
  0.9 0.7 copy-done.2
  1.6 0.1 copy-done
  1.7 0.0 copy-done.4
  1.7 0.1 copy-done.1
  1.8 1.3 %forward_blocks.1 = f32[2304,128]{1,0:T(8,128)S(1)} custom-call(f32[4,16384]{1,0:T(4,128)S(1)} %copy-done, f32[4,16384]{1,0:T(4,128)S(1)} %copy-done.1, f32[2,16384]{1,0:T(2,128)S(1)} %copy-done.4, f32[3,256,128]{2,1,0:T(8,128)S(1)} %copy-done.2, f32[2,128,128]{2,1,0:T(8,128)S(1)} %twist_table.1.twist_ref), custom_call_target="tpu_custom_call" | custom-call | tf_op jit(solution)/shard_map/forward_blocks/pallas_call | solution.py:97
  3.1 0.0 copy-start.7
  3.1 0.0 copy-start.8
  3.2 0.0 copy-start.9
  3.2 47.9 %all_to_all.10 = f32[256,9,1,128]{3,2,1,0:T(1,128)S(1)} all-to-all(f32[256,9,1,128]{3,2,1,0:T(1,128)S(1)} %bitcast.7), channel_id=1, replica_groups=mesh['ctx'=32,'chan'=8] {'ctx','chan'}, dimensions={0} | all-to-all | bytes 2359296 | tf_op jit(solution)/shard_map/all_to_all | solution.py:258
  51.0 0.0 copy-done.7
  51.0 0.0 copy-done.8
  51.0 0.0 copy-done.9
  51.0 3.2 %middle_blocks.1 = f32[2560,128]{1,0:T(8,128)} custom-call(f32[2304,128]{1,0:T(8,128)S(1)} %bitcast.6, f32[128,64]{1,0:T(8,128)S(1)} %copy-done.7, f32[64,128]{1,0:T(8,128)S(1)} %copy-done.8, f32[64,128]{1,0:T(8,128)S(1)} %copy-done.9), custom_call_target="tpu_custom_call" | custom-call | tf_op jit(solution)/shard_map/middle_blocks/pallas_call | solution.py:97
  54.2 0.0 copy-start.10
  54.2 0.0 copy-start.3
  54.2 0.0 copy-start.5
  54.2 0.0 copy-start.6
  54.2 7.2 %all-to-all-start.1 = ((f32[256,5,2,128]{3,2,1,0:T(2,128)}), f32[256,5,2,128]{3,2,1,0:T(2,128)S(1)}, u32[]{:S(2)}, u32[]{:S(2)}) async-start(f32[256,5,2,128]{3,2,1,0:T(2,128)} %bitcast.2), calls=%async_computation.1 | async-start | bytes 2621440 | tf_op jit(solution)/shard_map/all_to_all | solution.py:258
  61.4 0.0 copy-done.10
  61.4 0.1 copy.17.skip_ref
  61.5 36.3 %all-to-all-done.1 = f32[256,5,2,128]{3,2,1,0:T(2,128)S(1)} async-done(((f32[256,5,2,128]{3,2,1,0:T(2,128)}), f32[256,5,2,128]{3,2,1,0:T(2,128)S(1)}, u32[]{:S(2)}, u32[]{:S(2)}) %all-to-all-start.1) | async-done | bytes 1310752 | tf_op jit(solution)/shard_map/all_to_all | solution.py:258
  97.8 0.0 copy-done.3
  97.8 0.0 copy-done.5
  97.8 0.0 copy-done.6
  97.8 3.3 %inverse_blocks.1 = (f32[4,16384]{1,0:T(4,128)}, f32[4,16384]{1,0:T(4,128)}, f32[2,16384]{1,0:T(2,128)}) custom-call(f32[2560,128]{1,0:T(8,128)S(1)} %bitcast.5, f32[4,16384]{1,0:T(4,128)S(1)} %copy-done, f32[4,16384]{1,0:T(4,128)S(1)} %copy-done.1, f32[4,1]{1,0:T(4,128)S(1)} %copy.17.skip_ref, f32[256,256]{1,0:T(8,128)S(1)} %copy-done.3, ...), custom_call_target="tpu_custom_call" | custom-call | tf_op jit(solution)/shard_map/inverse_blocks/pallas_call | solution.py:97
Async XLA Ops:
  0.6 1.0 copy-start.2
  0.6 1.1 %copy-start = (f32[4,16384]{1,0:T(4,128)S(1)}, f32[4,16384]{1,0:T(4,128)}, u32[]{:S(2)}) copy-start(f32[4,16384]{1,0:T(4,128)} %seq_ref.3) | copy-start | bytes 786436
  0.7 1.1 %copy-start.4 = (f32[2,16384]{1,0:T(2,128)S(1)}, f32[2,16384]{1,0:T(2,128)}, u32[]{:S(2)}) copy-start(f32[2,16384]{1,0:T(2,128)} %taps_ref.1) | copy-start | bytes 393220
  0.7 1.2 %copy-start.1 = (f32[4,16384]{1,0:T(4,128)S(1)}, f32[4,16384]{1,0:T(4,128)}, u32[]{:S(2)}) copy-start(f32[4,16384]{1,0:T(4,128)} %cot_ref.3) | copy-start | bytes 786436
  3.1 47.9 %copy-start.7 = (f32[128,64]{1,0:T(8,128)S(1)}, f32[128,64]{1,0:T(8,128)}, u32[]{:S(2)}) copy-start(f32[128,64]{1,0:T(8,128)} %constant.15.clone.there_ref) | copy-start | bytes 98308
  3.1 47.9 %copy-start.8 = (f32[64,128]{1,0:T(8,128)S(1)}, f32[64,128]{1,0:T(8,128)}, u32[]{:S(2)}) copy-start(f32[64,128]{1,0:T(8,128)} %constant.16.clone.back_ref) | copy-start | bytes 98308
  3.2 47.9 %copy-start.9 = (f32[64,128]{1,0:T(8,128)S(1)}, f32[64,128]{1,0:T(8,128)}, u32[]{:S(2)}) copy-start(f32[64,128]{1,0:T(8,128)} %constant.17.clone.adjoint_ref) | copy-start | bytes 98308
  54.2 7.2 %copy-start.10 = (f32[4]{0:T(128)S(1)}, f32[4]{0:T(128)}, u32[]{:S(2)}) copy-start(f32[4]{0:T(128)} %param.13) | copy-start | bytes 52
  54.2 43.6 %copy-start.3 = (f32[256,256]{1,0:T(8,128)S(1)}, f32[256,256]{1,0:T(8,128)}, u32[]{:S(2)}) copy-start(f32[256,256]{1,0:T(8,128)} %constant.18.clone.inner_ref) | copy-start | bytes 786436
  54.2 43.6 %copy-start.5 = (f32[128,256]{1,0:T(8,128)S(1)}, f32[128,256]{1,0:T(8,128)}, u32[]{:S(2)}) copy-start(f32[128,256]{1,0:T(8,128)} %constant.19.clone.outer_ref) | copy-start | bytes 393220
  54.2 43.6 %copy-start.6 = (f32[2,128,128]{2,1,0:T(8,128)S(1)}, f32[2,128,128]{2,1,0:T(8,128)}, u32[]{:S(2)}) copy-start(f32[2,128,128]{2,1,0:T(8,128)} %constant.20.clone.twist_ref) | copy-start | bytes 393220
  54.2 43.6 %all-to-all-start.1 = ((f32[256,5,2,128]{3,2,1,0:T(2,128)}), f32[256,5,2,128]{3,2,1,0:T(2,128)S(1)}, u32[]{:S(2)}, u32[]{:S(2)}) async-start(f32[256,5,2,128]{3,2,1,0:T(2,128)} %bitcast.2), calls=%async_computation.1 | async-start | bytes 2621440 | tf_op jit(solution)/shard_map/all_to_all | solution.py:258

commit v8 on v7

--- a/solution.py
+++ b/solution.py
@@ -77,19 +77,6 @@
     return dot(jnp.concatenate([lh, lh, ll], axis=1), jnp.concatenate([rh, rl, rh], axis=0))
 
 
-def stacked(table):
-    high, low = split(table)
-    return jnp.concatenate(
-        [jnp.concatenate([high, high], axis=1), jnp.concatenate([low, jnp.zeros_like(low)], axis=1)], axis=0
-    )
-
-
-def dot_stacked(left, right):
-    both = dot(left, jnp.concatenate(split(right), axis=0))
-    half = both.shape[0] // 2
-    return both[:half] + both[half:]
-
-
 def call(kernel, name, out_shape, operands, scratch=()):
     many = isinstance(out_shape[0], tuple)
     shapes = tuple(jax.ShapeDtypeStruct(s, jnp.float32) for s in (out_shape if many else (out_shape,)))
@@ -105,23 +92,36 @@
     )(*operands)
 
 
-def twist_kernel(twist_ref):
+def opening_kernel(skip_ref, twist_ref, gain_ref, gains, sem):
+    arriving = pltpu.make_async_copy(skip_ref, gains, sem)
+    arriving.start()
     c = lax.broadcasted_iota(jnp.int32, (SIDE, SIDE), 0).astype(jnp.float32)
     b = lax.broadcasted_iota(jnp.int32, (SIDE, SIDE), 1).astype(jnp.float32)
     angle = (c + 0.25) * b * (2.0 * np.pi / BLOCK)
     twist_ref[0] = jnp.cos(angle)
     twist_ref[1] = jnp.sin(angle)
-
-
-def twist_table():
+    arriving.wait()
+    channel = lax.broadcasted_iota(jnp.int32, (4, SIDE), 0)
+    gain = jnp.full((4, SIDE), gains[0], jnp.float32)
+    for i in range(1, 4):
+        gain = jnp.where(channel == i, gains[i], gain)
+    gain_ref[...] = gain
+
+
+def opening(skip_gain):
     return pl.pallas_call(
-        twist_kernel,
-        out_shape=jax.ShapeDtypeStruct((2, SIDE, SIDE), jnp.float32),
-        out_specs=pl.BlockSpec(memory_space=pltpu.VMEM),
+        opening_kernel,
+        out_shape=(
+            jax.ShapeDtypeStruct((2, SIDE, SIDE), jnp.float32),
+            jax.ShapeDtypeStruct((4, SIDE), jnp.float32),
+        ),
+        in_specs=[pl.BlockSpec(memory_space=pl.ANY)],
+        out_specs=(pl.BlockSpec(memory_space=pltpu.VMEM),) * 2,
+        scratch_shapes=[pltpu.SMEM((4,), jnp.float32), pltpu.SemaphoreType.DMA],
         compiler_params=pltpu.CompilerParams(vmem_limit_bytes=4 * 1024 * 1024),
         cost_estimate=pl.CostEstimate(flops=4_000_000_000, bytes_accessed=8_000_000, transcendentals=32768),
-        name="twist_table",
-    )()
+        name="opening",
+    )(skip_gain)
 
 
 def forward_kernel(seq_ref, cot_ref, taps_ref, tables_ref, twist_ref, out_ref, rows):
@@ -150,14 +150,14 @@
                 ]
 
 
-def forward_blocks(sequence, cotangent, taps):
-    operands = (sequence, cotangent, taps, jnp.asarray(FORWARD_TABLES), twist_table())
+def forward_blocks(sequence, cotangent, taps, twist):
+    operands = (sequence, cotangent, taps, jnp.asarray(FORWARD_TABLES), twist)
     scratch = [pltpu.VMEM((10 * SIDE, SIDE), jnp.float32)]
     return call(forward_kernel, "forward_blocks", (OWNERS * THERE_ROWS, SIDE), operands, scratch)
 
 
 def middle_kernel(in_ref, there_ref, back_ref, adjoint_ref, out_ref):
-    there, back, adjoint = there_ref[...], stacked(back_ref[...]), stacked(adjoint_ref[...])
+    there, back, adjoint = there_ref[...], back_ref[...], adjoint_ref[...]
     low = lax.broadcasted_iota(jnp.int32, (BLOCKS, SIDE), 1) < HALF
 
     def turn(values):
@@ -180,7 +180,7 @@
         return points[:POINTS], points[POINTS:]
 
     def blocks_of(table, real, imag):
-        blocks = dot_stacked(table, jnp.concatenate([real, imag], axis=0))
+        blocks = dot_three(table, jnp.concatenate([real, imag], axis=0))
         return blocks[:BLOCKS], blocks[BLOCKS:]
 
     filters = [points_of(f, f, (SIGNALS,)) for f in range(2)]
@@ -217,38 +217,30 @@
     return call(middle_kernel, "middle_blocks", (OWNERS * BACK_ROWS, SIDE), operands)
 
 
-def inverse_kernel(in_ref, seq_ref, cot_ref, skip_ref, inner_ref, outer_ref, twist_ref, y_ref, g_ref, f_ref, rows):
+def inverse_kernel(in_ref, seq_ref, cot_ref, gain_ref, inner_ref, outer_ref, twist_ref, y_ref, g_ref, f_ref, rows):
     cosine, sine = twist_ref[0], twist_ref[1]
     inner, outer = inner_ref[...], outer_ref[...]
-    for group in ((0, 1), (2, 3), (4, 5), (6, 7), (8, 9)):
-        both = jnp.concatenate(
-            [
-                jnp.concatenate(
-                    [in_ref[pl.ds(BACK_ROWS * half + i, SIDE, stride=2 * BACK_ROWS), :] for half in range(2)], axis=1
-                )
-                for i in group
-            ],
-            axis=0,
-        )
-        turned = dot_three(both, inner)
-        columns = []
-        for place in range(2):
-            real = turned[place * SIDE : (place + 1) * SIDE, :SIDE]
-            imag = turned[place * SIDE : (place + 1) * SIDE, SIDE:]
-            columns.append(jnp.concatenate([real * cosine - imag * sine, imag * cosine + real * sine], axis=0))
-        closed = dot_three(outer, jnp.concatenate(columns, axis=1))
-        for place, i in enumerate(group):
-            rows[i * SIDE : (i + 1) * SIDE, :] = closed[:, place * SIDE : (place + 1) * SIDE]
-    skip = jnp.broadcast_to(skip_ref[...], (4, SIDE))
+    gain = gain_ref[...]
+
+    columns = []
+    for i in range(10):
+        both = [in_ref[pl.ds(BACK_ROWS * half + i, SIDE, stride=2 * BACK_ROWS), :] for half in range(2)]
+        turned = dot_three(jnp.concatenate(both, axis=1), inner)
+        real, imag = turned[:, :SIDE], turned[:, SIDE:]
+        column = jnp.concatenate([real * cosine - imag * sine, imag * cosine + real * sine], axis=0)
+        columns.append(column)
+    closed = dot_three(outer, jnp.concatenate(columns, axis=1))
+    for i in range(10):
+        rows[i * SIDE : (i + 1) * SIDE, :] = closed[:, i * SIDE : (i + 1) * SIDE]
     for a in range(SIDE):
         lanes = slice(a * SIDE, (a + 1) * SIDE)
-        y_ref[:, lanes] = rows[pl.ds(a, 4, stride=SIDE), :] + skip * seq_ref[:, lanes]
-        g_ref[:, lanes] = rows[pl.ds(4 * SIDE + a, 4, stride=SIDE), :] + skip * cot_ref[:, lanes]
+        y_ref[:, lanes] = rows[pl.ds(a, 4, stride=SIDE), :] + gain * seq_ref[:, lanes]
+        g_ref[:, lanes] = rows[pl.ds(4 * SIDE + a, 4, stride=SIDE), :] + gain * cot_ref[:, lanes]
         f_ref[:, lanes] = rows[pl.ds(8 * SIDE + a, 2, stride=SIDE), :]
 
 
-def inverse_blocks(spectra, sequence, cotangent, skip_gain):
-    operands = (spectra, sequence, cotangent, skip_gain[:, None]) + tuple(jnp.asarray(t) for t in INVERSE_TABLES)
+def inverse_blocks(spectra, sequence, cotangent, gain):
+    operands = (spectra, sequence, cotangent, gain) + tuple(jnp.asarray(t) for t in INVERSE_TABLES)
     scratch = [pltpu.VMEM((10 * SIDE, SIDE), jnp.float32)]
     return call(inverse_kernel, "inverse_blocks", ((4, BLOCK), (4, BLOCK), (2, BLOCK)), operands, scratch)
 
@@ -259,9 +251,10 @@
 
 
 def body(sequence, filter_taps, skip_gain, cotangent):
-    spectra = exchange(forward_blocks(sequence, cotangent, filter_taps), 1)
+    twist, gain = opening(skip_gain)
+    spectra = exchange(forward_blocks(sequence, cotangent, filter_taps, twist), 1)
     products = exchange(middle_blocks(spectra), 2)
-    return inverse_blocks(products, sequence, cotangent, skip_gain)
+    return inverse_blocks(products, sequence, cotangent, gain)
 
 
 def solution(mesh):

time: 102 us -> 101 us (level)
  blocking collectives: 47.9 us -> 91.1 us
  waiting for transfers between devices: 36.3 us -> 0 us
  starting transfers between devices: 7.18 us -> 0 us
  Pallas kernels: 7.99 us -> 6.2 us
    all_to_all x1 -> x2, blocking collectives: 47.9 us -> 91.1 us  [exchange(): lax.all_to_all(cut, ('ctx', 'chan'), split_axis=0, concat_axis=0, tiled=T...]
    all_to_all x1 -> x0, waiting for transfers between devices: 36.3 us -> none  [exchange(): lax.all_to_all(cut, ('ctx', 'chan'), split_axis=0, concat_axis=0, tiled=T...]
    all_to_all x1 -> x0, starting transfers between devices: 7.18 us -> none  [exchange(): lax.all_to_all(cut, ('ctx', 'chan'), split_axis=0, concat_axis=0, tiled=T...]
    pallas_call x3, Pallas kernels: 7.74 us -> 5.65 us  [call(): pl.pallas_call(kernel, out_shape=shapes if many else shapes[0], in_specs=...]
  transfers between devices with their start and end apart: 1 -> 0, of which waited for: 1 -> 0; matrix products, arithmetic and copies ran while one was open for 0% -> 0% of each run, Pallas kernels for 0% -> 0%
where the time goes in v8:
time: 101 us; the launch traced here: 99.2 us
  blocking collectives  91.1 us (90%)
  Pallas kernels  6.2 us (6%)
  local copies, waits for them, and re-layouts  1.16 us (1%)
    all_to_all x2, blocking collectives, exchange(): lax.all_to_all(cut, ('ctx', 'chan'), split_axis=0, concat_axis=0, tiled=T...  91.1 us
    pallas_call x3, Pallas kernels, call(): pl.pallas_call(kernel, out_shape=shapes if many else shapes[0], in_specs=...  5.65 us

profile of v8, /device:TPU:32, one launch (start us, length us, event | category | flops | bytes accessed | tf_op | source)
XLA Modules:
  0.0 99.2 jit_solution(8305539769683516481)
XLA Ops:
  0.6 0.0 copy-start.2
  0.6 0.0 copy-start.1
  0.7 0.0 copy-start
  0.7 0.0 copy-start.10
  0.7 0.7 copy-done.10
  1.4 0.0 copy-start.4
  1.4 0.6 opening.1
  2.0 0.0 copy-done.2
  2.0 0.0 copy-done.1
  2.0 0.0 copy-done
  2.0 0.4 copy-done.4
  2.4 1.3 %forward_blocks.1 = f32[2304,128]{1,0:T(8,128)S(1)} custom-call(f32[4,16384]{1,0:T(4,128)S(1)} %copy-done, f32[4,16384]{1,0:T(4,128)S(1)} %copy-done.1, f32[2,16384]{1,0:T(2,128)S(1)} %copy-done.4, f32[3,256,128]{2,1,0:T(8,128)S(1)} %copy-done.2, f32[2,128,128]{2,1,0:T(8,128)S(1)} %get-tuple-element.5.twist_ref), custom_call_target="tpu_custom_call" | custom-call | tf_op jit(solution)/shard_map/forward_blocks/pallas_call | solution.py:84
  3.7 0.0 copy-start.7
  3.7 0.0 copy-start.8
  3.7 0.0 copy-start.9
  3.7 47.9 %all_to_all.10 = f32[256,9,1,128]{3,2,1,0:T(1,128)S(1)} all-to-all(f32[256,9,1,128]{3,2,1,0:T(1,128)S(1)} %bitcast.7), channel_id=1, replica_groups=mesh['ctx'=32,'chan'=8] {'ctx','chan'}, dimensions={0} | all-to-all | bytes 2359296 | tf_op jit(solution)/shard_map/all_to_all | solution.py:250
  51.6 0.0 copy-done.7
  51.6 0.0 copy-done.8
  51.6 0.0 copy-done.9
  51.6 2.0 %middle_blocks.1 = f32[2560,128]{1,0:T(8,128)S(1)} custom-call(f32[2304,128]{1,0:T(8,128)S(1)} %bitcast.6, f32[128,64]{1,0:T(8,128)S(1)} %copy-done.7, f32[64,128]{1,0:T(8,128)S(1)} %copy-done.9, f32[64,128]{1,0:T(8,128)S(1)} %copy-done.8), custom_call_target="tpu_custom_call" | custom-call | tf_op jit(solution)/shard_map/middle_blocks/pallas_call | solution.py:84
  53.6 0.0 copy-start.3
  53.6 0.0 copy-start.5
  53.7 0.0 copy-start.6
  53.7 43.2 %all_to_all.11 = f32[256,5,2,128]{3,2,1,0:T(2,128)S(1)} all-to-all(f32[256,5,2,128]{3,2,1,0:T(2,128)S(1)} %bitcast.5), channel_id=1, replica_groups=mesh['ctx'=32,'chan'=8] {'ctx','chan'}, dimensions={0} | all-to-all | bytes 2621440 | tf_op jit(solution)/shard_map/all_to_all | solution.py:250
  96.9 0.0 copy-done.3
  96.9 0.0 copy-done.5
  96.9 0.0 copy-done.6
  96.9 2.3 %inverse_blocks.1 = (f32[4,16384]{1,0:T(4,128)}, f32[4,16384]{1,0:T(4,128)}, f32[2,16384]{1,0:T(2,128)}) custom-call(f32[2560,128]{1,0:T(8,128)S(1)} %bitcast.4, f32[4,16384]{1,0:T(4,128)S(1)} %copy-done, f32[4,16384]{1,0:T(4,128)S(1)} %copy-done.1, f32[4,128]{1,0:T(4,128)S(1)} %get-tuple-element.6.gain_ref, f32[256,256]{1,0:T(8,128)S(1)} %copy-done.3, ...), custom_call_target="tpu_custom_call" | custom-call | tf_op jit(solution)/shard_map/inverse_blocks/pallas_call | solution.py:84
Async XLA Ops:
  0.6 1.3 %copy-start.2 = (f32[3,256,128]{2,1,0:T(8,128)S(1)}, f32[3,256,128]{2,1,0:T(8,128)}, u32[]{:S(2)}) copy-start(f32[3,256,128]{2,1,0:T(8,128)} %constant.14.clone.tables_ref) | copy-start | bytes 1179652
  0.6 1.3 %copy-start.1 = (f32[4,16384]{1,0:T(4,128)S(1)}, f32[4,16384]{1,0:T(4,128)}, u32[]{:S(2)}) copy-start(f32[4,16384]{1,0:T(4,128)} %cot_ref.3) | copy-start | bytes 786436
  0.7 1.3 %copy-start = (f32[4,16384]{1,0:T(4,128)S(1)}, f32[4,16384]{1,0:T(4,128)}, u32[]{:S(2)}) copy-start(f32[4,16384]{1,0:T(4,128)} %seq_ref.3) | copy-start | bytes 786436
  0.7 0.7 copy-start.10
  1.4 1.0 copy-start.4
  3.7 47.9 %copy-start.7 = (f32[128,64]{1,0:T(8,128)S(1)}, f32[128,64]{1,0:T(8,128)}, u32[]{:S(2)}) copy-start(f32[128,64]{1,0:T(8,128)} %constant.15.clone.there_ref) | copy-start | bytes 98308
  3.7 47.9 %copy-start.8 = (f32[64,128]{1,0:T(8,128)S(1)}, f32[64,128]{1,0:T(8,128)}, u32[]{:S(2)}) copy-start(f32[64,128]{1,0:T(8,128)} %constant.17.clone.adjoint_ref) | copy-start | bytes 98308
  3.7 47.9 %copy-start.9 = (f32[64,128]{1,0:T(8,128)S(1)}, f32[64,128]{1,0:T(8,128)}, u32[]{:S(2)}) copy-start(f32[64,128]{1,0:T(8,128)} %constant.16.clone.back_ref) | copy-start | bytes 98308
  53.6 43.3 %copy-start.3 = (f32[256,256]{1,0:T(8,128)S(1)}, f32[256,256]{1,0:T(8,128)}, u32[]{:S(2)}) copy-start(f32[256,256]{1,0:T(8,128)} %constant.18.clone.inner_ref) | copy-start | bytes 786436
  53.6 43.2 %copy-start.5 = (f32[2,128,128]{2,1,0:T(8,128)S(1)}, f32[2,128,128]{2,1,0:T(8,128)}, u32[]{:S(2)}) copy-start(f32[2,128,128]{2,1,0:T(8,128)} %constant.20.clone.twist_ref) | copy-start | bytes 393220
  53.7 43.2 %copy-start.6 = (f32[128,256]{1,0:T(8,128)S(1)}, f32[128,256]{1,0:T(8,128)}, u32[]{:S(2)}) copy-start(f32[128,256]{1,0:T(8,128)} %constant.19.clone.outer_ref) | copy-start | bytes 393220

commit v9 on v8

--- a/solution.py
+++ b/solution.py
@@ -92,36 +92,23 @@
     )(*operands)
 
 
-def opening_kernel(skip_ref, twist_ref, gain_ref, gains, sem):
-    arriving = pltpu.make_async_copy(skip_ref, gains, sem)
-    arriving.start()
+def twist_kernel(twist_ref):
     c = lax.broadcasted_iota(jnp.int32, (SIDE, SIDE), 0).astype(jnp.float32)
     b = lax.broadcasted_iota(jnp.int32, (SIDE, SIDE), 1).astype(jnp.float32)
     angle = (c + 0.25) * b * (2.0 * np.pi / BLOCK)
     twist_ref[0] = jnp.cos(angle)
     twist_ref[1] = jnp.sin(angle)
-    arriving.wait()
-    channel = lax.broadcasted_iota(jnp.int32, (4, SIDE), 0)
-    gain = jnp.full((4, SIDE), gains[0], jnp.float32)
-    for i in range(1, 4):
-        gain = jnp.where(channel == i, gains[i], gain)
-    gain_ref[...] = gain
-
-
-def opening(skip_gain):
+
+
+def twist_table():
     return pl.pallas_call(
-        opening_kernel,
-        out_shape=(
-            jax.ShapeDtypeStruct((2, SIDE, SIDE), jnp.float32),
-            jax.ShapeDtypeStruct((4, SIDE), jnp.float32),
-        ),
-        in_specs=[pl.BlockSpec(memory_space=pl.ANY)],
-        out_specs=(pl.BlockSpec(memory_space=pltpu.VMEM),) * 2,
-        scratch_shapes=[pltpu.SMEM((4,), jnp.float32), pltpu.SemaphoreType.DMA],
+        twist_kernel,
+        out_shape=jax.ShapeDtypeStruct((2, SIDE, SIDE), jnp.float32),
+        out_specs=pl.BlockSpec(memory_space=pltpu.VMEM),
         compiler_params=pltpu.CompilerParams(vmem_limit_bytes=4 * 1024 * 1024),
         cost_estimate=pl.CostEstimate(flops=4_000_000_000, bytes_accessed=8_000_000, transcendentals=32768),
-        name="opening",
-    )(skip_gain)
+        name="twist_table",
+    )()
 
 
 def forward_kernel(seq_ref, cot_ref, taps_ref, tables_ref, twist_ref, out_ref, rows):
@@ -150,8 +137,8 @@
                 ]
 
 
-def forward_blocks(sequence, cotangent, taps, twist):
-    operands = (sequence, cotangent, taps, jnp.asarray(FORWARD_TABLES), twist)
+def forward_blocks(sequence, cotangent, taps):
+    operands = (sequence, cotangent, taps, jnp.asarray(FORWARD_TABLES), twist_table())
     scratch = [pltpu.VMEM((10 * SIDE, SIDE), jnp.float32)]
     return call(forward_kernel, "forward_blocks", (OWNERS * THERE_ROWS, SIDE), operands, scratch)
 
@@ -217,10 +204,10 @@
     return call(middle_kernel, "middle_blocks", (OWNERS * BACK_ROWS, SIDE), operands)
 
 
-def inverse_kernel(in_ref, seq_ref, cot_ref, gain_ref, inner_ref, outer_ref, twist_ref, y_ref, g_ref, f_ref, rows):
+def inverse_kernel(in_ref, seq_ref, cot_ref, skip_ref, inner_ref, outer_ref, twist_ref, y_ref, g_ref, f_ref, rows):
     cosine, sine = twist_ref[0], twist_ref[1]
     inner, outer = inner_ref[...], outer_ref[...]
-    gain = gain_ref[...]
+    gain = jnp.concatenate([jnp.broadcast_to(skip_ref[:, i : i + 1], (1, SIDE)) for i in range(4)], axis=0)
 
     columns = []
     for i in range(10):
@@ -239,8 +226,8 @@
         f_ref[:, lanes] = rows[pl.ds(8 * SIDE + a, 2, stride=SIDE), :]
 
 
-def inverse_blocks(spectra, sequence, cotangent, gain):
-    operands = (spectra, sequence, cotangent, gain) + tuple(jnp.asarray(t) for t in INVERSE_TABLES)
+def inverse_blocks(spectra, sequence, cotangent, skip_gain):
+    operands = (spectra, sequence, cotangent, skip_gain[None, :]) + tuple(jnp.asarray(t) for t in INVERSE_TABLES)
     scratch = [pltpu.VMEM((10 * SIDE, SIDE), jnp.float32)]
     return call(inverse_kernel, "inverse_blocks", ((4, BLOCK), (4, BLOCK), (2, BLOCK)), operands, scratch)
 
@@ -251,10 +238,9 @@
 
 
 def body(sequence, filter_taps, skip_gain, cotangent):
-    twist, gain = opening(skip_gain)
-    spectra = exchange(forward_blocks(sequence, cotangent, filter_taps, twist), 1)
+    spectra = exchange(forward_blocks(sequence, cotangent, filter_taps), 1)
     products = exchange(middle_blocks(spectra), 2)
-    return inverse_blocks(products, sequence, cotangent, gain)
+    return inverse_blocks(products, sequence, cotangent, skip_gain)
 
 
 def solution(mesh):

time: 101 us -> 100 us (0.990)
  no operation moved by 1% of the time
where the time goes in v9:
time: 100 us; the launch traced here: 98.6 us
  blocking collectives  91.1 us (91%)
  Pallas kernels  5.86 us (6%)
    all_to_all x2, blocking collectives, exchange(): lax.all_to_all(cut, ('ctx', 'chan'), split_axis=0, concat_axis=0, tiled=T...  91.1 us
    pallas_call x3, Pallas kernels, call(): pl.pallas_call(kernel, out_shape=shapes if many else shapes[0], in_specs=...  5.6 us

profile of v9, /device:TPU:32, one launch (start us, length us, event | category | flops | bytes accessed | tf_op | source)
XLA Modules:
  0.0 98.6 jit_solution(8310927181042767425)
XLA Ops:
  0.6 0.0 copy-start.2
  0.6 0.0 copy-start.1
  0.7 0.0 copy-start
  0.7 0.0 copy-start.4
  0.7 0.3 twist_table.1.twist_ref
  0.9 0.7 copy-done.2
  1.6 0.1 copy-done.1
  1.7 0.1 copy-done
  1.8 0.0 copy-done.4
  1.8 1.3 %forward_blocks.1 = f32[2304,128]{1,0:T(8,128)S(1)} custom-call(f32[4,16384]{1,0:T(4,128)S(1)} %copy-done, f32[4,16384]{1,0:T(4,128)S(1)} %copy-done.1, f32[2,16384]{1,0:T(2,128)S(1)} %copy-done.4, f32[3,256,128]{2,1,0:T(8,128)S(1)} %copy-done.2, f32[2,128,128]{2,1,0:T(8,128)S(1)} %twist_table.1.twist_ref), custom_call_target="tpu_custom_call" | custom-call | tf_op jit(solution)/shard_map/forward_blocks/pallas_call | solution.py:84
  3.1 0.0 copy-start.7
  3.1 0.0 copy-start.8
  3.1 0.0 copy-start.9
  3.2 47.9 %all_to_all.10 = f32[256,9,1,128]{3,2,1,0:T(1,128)S(1)} all-to-all(f32[256,9,1,128]{3,2,1,0:T(1,128)S(1)} %bitcast.8), channel_id=1, replica_groups=mesh['ctx'=32,'chan'=8] {'ctx','chan'}, dimensions={0} | all-to-all | bytes 2359296 | tf_op jit(solution)/shard_map/all_to_all | solution.py:237
  51.0 0.0 copy-done.7
  51.0 0.0 copy-done.8
  51.0 0.0 copy-done.9
  51.0 2.0 %middle_blocks.1 = f32[2560,128]{1,0:T(8,128)S(1)} custom-call(f32[2304,128]{1,0:T(8,128)S(1)} %bitcast.7, f32[128,64]{1,0:T(8,128)S(1)} %copy-done.7, f32[64,128]{1,0:T(8,128)S(1)} %copy-done.9, f32[64,128]{1,0:T(8,128)S(1)} %copy-done.8), custom_call_target="tpu_custom_call" | custom-call | tf_op jit(solution)/shard_map/middle_blocks/pallas_call | solution.py:84
  53.1 0.0 copy-start.3
  53.1 0.0 copy-start.5
  53.1 0.0 copy-start.6
  53.1 0.0 copy-start.10
  53.1 43.2 %all_to_all.11 = f32[256,5,2,128]{3,2,1,0:T(2,128)S(1)} all-to-all(f32[256,5,2,128]{3,2,1,0:T(2,128)S(1)} %bitcast.6), channel_id=1, replica_groups=mesh['ctx'=32,'chan'=8] {'ctx','chan'}, dimensions={0} | all-to-all | bytes 2621440 | tf_op jit(solution)/shard_map/all_to_all | solution.py:237
  96.3 0.0 copy-done.3
  96.3 0.0 copy-done.5
  96.3 0.0 copy-done.6
  96.3 0.0 copy-done.10
  96.4 2.3 %inverse_blocks.1 = (f32[4,16384]{1,0:T(4,128)}, f32[4,16384]{1,0:T(4,128)}, f32[2,16384]{1,0:T(2,128)}) custom-call(f32[2560,128]{1,0:T(8,128)S(1)} %bitcast.5, f32[4,16384]{1,0:T(4,128)S(1)} %copy-done, f32[4,16384]{1,0:T(4,128)S(1)} %copy-done.1, f32[1,4]{1,0:T(1,128)S(1)} %bitcast.9, f32[256,256]{1,0:T(8,128)S(1)} %copy-done.3, ...), custom_call_target="tpu_custom_call" | custom-call | tf_op jit(solution)/shard_map/inverse_blocks/pallas_call | solution.py:84
Async XLA Ops:
  0.6 1.0 %copy-start.2 = (f32[3,256,128]{2,1,0:T(8,128)S(1)}, f32[3,256,128]{2,1,0:T(8,128)}, u32[]{:S(2)}) copy-start(f32[3,256,128]{2,1,0:T(8,128)} %constant.14.clone.tables_ref) | copy-start | bytes 1179652
  0.6 1.1 %copy-start.1 = (f32[4,16384]{1,0:T(4,128)S(1)}, f32[4,16384]{1,0:T(4,128)}, u32[]{:S(2)}) copy-start(f32[4,16384]{1,0:T(4,128)} %cot_ref.3) | copy-start | bytes 786436
  0.7 1.1 %copy-start = (f32[4,16384]{1,0:T(4,128)S(1)}, f32[4,16384]{1,0:T(4,128)}, u32[]{:S(2)}) copy-start(f32[4,16384]{1,0:T(4,128)} %seq_ref.3) | copy-start | bytes 786436
  0.7 1.2 %copy-start.4 = (f32[2,16384]{1,0:T(2,128)S(1)}, f32[2,16384]{1,0:T(2,128)}, u32[]{:S(2)}) copy-start(f32[2,16384]{1,0:T(2,128)} %taps_ref.1) | copy-start | bytes 393220
  3.1 47.9 %copy-start.7 = (f32[128,64]{1,0:T(8,128)S(1)}, f32[128,64]{1,0:T(8,128)}, u32[]{:S(2)}) copy-start(f32[128,64]{1,0:T(8,128)} %constant.15.clone.there_ref) | copy-start | bytes 98308
  3.1 47.9 %copy-start.8 = (f32[64,128]{1,0:T(8,128)S(1)}, f32[64,128]{1,0:T(8,128)}, u32[]{:S(2)}) copy-start(f32[64,128]{1,0:T(8,128)} %constant.17.clone.adjoint_ref) | copy-start | bytes 98308
  3.1 47.9 %copy-start.9 = (f32[64,128]{1,0:T(8,128)S(1)}, f32[64,128]{1,0:T(8,128)}, u32[]{:S(2)}) copy-start(f32[64,128]{1,0:T(8,128)} %constant.16.clone.back_ref) | copy-start | bytes 98308
  53.1 43.3 %copy-start.3 = (f32[256,256]{1,0:T(8,128)S(1)}, f32[256,256]{1,0:T(8,128)}, u32[]{:S(2)}) copy-start(f32[256,256]{1,0:T(8,128)} %constant.18.clone.inner_ref) | copy-start | bytes 786436
  53.1 43.3 %copy-start.5 = (f32[2,128,128]{2,1,0:T(8,128)S(1)}, f32[2,128,128]{2,1,0:T(8,128)}, u32[]{:S(2)}) copy-start(f32[2,128,128]{2,1,0:T(8,128)} %constant.20.clone.twist_ref) | copy-start | bytes 393220
  53.1 43.2 %copy-start.6 = (f32[128,256]{1,0:T(8,128)S(1)}, f32[128,256]{1,0:T(8,128)}, u32[]{:S(2)}) copy-start(f32[128,256]{1,0:T(8,128)} %constant.19.clone.outer_ref) | copy-start | bytes 393220
  53.1 43.2 %copy-start.10 = (f32[4]{0:T(128)S(1)}, f32[4]{0:T(128)}, u32[]{:S(2)}) copy-start(f32[4]{0:T(128)} %param.13) | copy-start | bytes 52

commit v10 on v9

--- a/solution.py
+++ b/solution.py
@@ -216,7 +216,7 @@
         real, imag = turned[:, :SIDE], turned[:, SIDE:]
         column = jnp.concatenate([real * cosine - imag * sine, imag * cosine + real * sine], axis=0)
         columns.append(column)
-    closed = dot_three(outer, jnp.concatenate(columns, axis=1))
+    closed = dot_wide(outer, jnp.concatenate(columns, axis=1))
     for i in range(10):
         rows[i * SIDE : (i + 1) * SIDE, :] = closed[:, i * SIDE : (i + 1) * SIDE]
     for a in range(SIDE):

time: 100 us -> 99.6 us (level)
  no operation moved by 1% of the time
where the time goes in v10:
time: 99.6 us; the launch traced here: 98.3 us
  blocking collectives  91.1 us (91%)
  Pallas kernels  5.54 us (6%)
    all_to_all x2, blocking collectives, exchange(): lax.all_to_all(cut, ('ctx', 'chan'), split_axis=0, concat_axis=0, tiled=T...  91.1 us
    pallas_call x3, Pallas kernels, call(): pl.pallas_call(kernel, out_shape=shapes if many else shapes[0], in_specs=...  5.28 us

profile of v10, /device:TPU:32, one launch (start us, length us, event | category | flops | bytes accessed | tf_op | source)
XLA Modules:
  0.0 98.3 jit_solution(17124786277921005465)
XLA Ops:
  0.6 0.0 copy-start.2
  0.6 0.0 copy-start.1
  0.7 0.0 copy-start
  0.7 0.0 copy-start.4
  0.7 0.3 twist_table.1.twist_ref
  0.9 0.7 copy-done.2
  1.6 0.1 copy-done.1
  1.7 0.1 copy-done
  1.8 0.0 copy-done.4
  1.8 1.3 %forward_blocks.1 = f32[2304,128]{1,0:T(8,128)S(1)} custom-call(f32[4,16384]{1,0:T(4,128)S(1)} %copy-done, f32[4,16384]{1,0:T(4,128)S(1)} %copy-done.1, f32[2,16384]{1,0:T(2,128)S(1)} %copy-done.4, f32[3,256,128]{2,1,0:T(8,128)S(1)} %copy-done.2, f32[2,128,128]{2,1,0:T(8,128)S(1)} %twist_table.1.twist_ref), custom_call_target="tpu_custom_call" | custom-call | tf_op jit(solution)/shard_map/forward_blocks/pallas_call | solution.py:84
  3.1 0.0 copy-start.7
  3.1 0.0 copy-start.8
  3.1 0.0 copy-start.9
  3.2 47.9 %all_to_all.10 = f32[256,9,1,128]{3,2,1,0:T(1,128)S(1)} all-to-all(f32[256,9,1,128]{3,2,1,0:T(1,128)S(1)} %bitcast.8), channel_id=1, replica_groups=mesh['ctx'=32,'chan'=8] {'ctx','chan'}, dimensions={0} | all-to-all | bytes 2359296 | tf_op jit(solution)/shard_map/all_to_all | solution.py:237
  51.0 0.0 copy-done.7
  51.0 0.0 copy-done.8
  51.0 0.0 copy-done.9
  51.0 2.0 %middle_blocks.1 = f32[2560,128]{1,0:T(8,128)S(1)} custom-call(f32[2304,128]{1,0:T(8,128)S(1)} %bitcast.7, f32[128,64]{1,0:T(8,128)S(1)} %copy-done.7, f32[64,128]{1,0:T(8,128)S(1)} %copy-done.9, f32[64,128]{1,0:T(8,128)S(1)} %copy-done.8), custom_call_target="tpu_custom_call" | custom-call | tf_op jit(solution)/shard_map/middle_blocks/pallas_call | solution.py:84
  53.1 0.0 copy-start.3
  53.1 0.0 copy-start.5
  53.1 0.0 copy-start.6
  53.1 0.0 copy-start.10
  53.1 43.2 %all_to_all.11 = f32[256,5,2,128]{3,2,1,0:T(2,128)S(1)} all-to-all(f32[256,5,2,128]{3,2,1,0:T(2,128)S(1)} %bitcast.6), channel_id=1, replica_groups=mesh['ctx'=32,'chan'=8] {'ctx','chan'}, dimensions={0} | all-to-all | bytes 2621440 | tf_op jit(solution)/shard_map/all_to_all | solution.py:237
  96.3 0.0 copy-done.3
  96.3 0.0 copy-done.5
  96.3 0.0 copy-done.6
  96.3 0.0 copy-done.10
  96.4 2.0 %inverse_blocks.1 = (f32[4,16384]{1,0:T(4,128)}, f32[4,16384]{1,0:T(4,128)}, f32[2,16384]{1,0:T(2,128)}) custom-call(f32[2560,128]{1,0:T(8,128)S(1)} %bitcast.5, f32[4,16384]{1,0:T(4,128)S(1)} %copy-done, f32[4,16384]{1,0:T(4,128)S(1)} %copy-done.1, f32[1,4]{1,0:T(1,128)S(1)} %bitcast.9, f32[256,256]{1,0:T(8,128)S(1)} %copy-done.3, ...), custom_call_target="tpu_custom_call" | custom-call | tf_op jit(solution)/shard_map/inverse_blocks/pallas_call | solution.py:84
Async XLA Ops:
  0.6 1.0 %copy-start.2 = (f32[3,256,128]{2,1,0:T(8,128)S(1)}, f32[3,256,128]{2,1,0:T(8,128)}, u32[]{:S(2)}) copy-start(f32[3,256,128]{2,1,0:T(8,128)} %constant.14.clone.tables_ref) | copy-start | bytes 1179652
  0.6 1.1 %copy-start.1 = (f32[4,16384]{1,0:T(4,128)S(1)}, f32[4,16384]{1,0:T(4,128)}, u32[]{:S(2)}) copy-start(f32[4,16384]{1,0:T(4,128)} %cot_ref.3) | copy-start | bytes 786436
  0.7 1.1 %copy-start = (f32[4,16384]{1,0:T(4,128)S(1)}, f32[4,16384]{1,0:T(4,128)}, u32[]{:S(2)}) copy-start(f32[4,16384]{1,0:T(4,128)} %seq_ref.3) | copy-start | bytes 786436
  0.7 1.2 %copy-start.4 = (f32[2,16384]{1,0:T(2,128)S(1)}, f32[2,16384]{1,0:T(2,128)}, u32[]{:S(2)}) copy-start(f32[2,16384]{1,0:T(2,128)} %taps_ref.1) | copy-start | bytes 393220
  3.1 47.9 %copy-start.7 = (f32[128,64]{1,0:T(8,128)S(1)}, f32[128,64]{1,0:T(8,128)}, u32[]{:S(2)}) copy-start(f32[128,64]{1,0:T(8,128)} %constant.15.clone.there_ref) | copy-start | bytes 98308
  3.1 47.9 %copy-start.8 = (f32[64,128]{1,0:T(8,128)S(1)}, f32[64,128]{1,0:T(8,128)}, u32[]{:S(2)}) copy-start(f32[64,128]{1,0:T(8,128)} %constant.17.clone.adjoint_ref) | copy-start | bytes 98308
  3.1 47.9 %copy-start.9 = (f32[64,128]{1,0:T(8,128)S(1)}, f32[64,128]{1,0:T(8,128)}, u32[]{:S(2)}) copy-start(f32[64,128]{1,0:T(8,128)} %constant.16.clone.back_ref) | copy-start | bytes 98308
  53.1 43.3 %copy-start.3 = (f32[256,256]{1,0:T(8,128)S(1)}, f32[256,256]{1,0:T(8,128)}, u32[]{:S(2)}) copy-start(f32[256,256]{1,0:T(8,128)} %constant.18.clone.inner_ref) | copy-start | bytes 786436
  53.1 43.3 %copy-start.5 = (f32[2,128,128]{2,1,0:T(8,128)S(1)}, f32[2,128,128]{2,1,0:T(8,128)}, u32[]{:S(2)}) copy-start(f32[2,128,128]{2,1,0:T(8,128)} %constant.20.clone.twist_ref) | copy-start | bytes 393220
  53.1 43.2 %copy-start.6 = (f32[128,256]{1,0:T(8,128)S(1)}, f32[128,256]{1,0:T(8,128)}, u32[]{:S(2)}) copy-start(f32[128,256]{1,0:T(8,128)} %constant.19.clone.outer_ref) | copy-start | bytes 393220
  53.1 43.2 %copy-start.10 = (f32[4]{0:T(128)S(1)}, f32[4]{0:T(128)}, u32[]{:S(2)}) copy-start(f32[4]{0:T(128)} %param.13) | copy-start | bytes 52

commit v11 on v10

--- a/solution.py
+++ b/solution.py
@@ -7,13 +7,11 @@
 from jax.sharding import PartitionSpec as P
 
 SIDE = 128
-HALF = SIDE // 2
 BLOCK = SIDE * SIDE
 BLOCKS = 32
 CHAN = 8
 OWNERS = BLOCKS * CHAN
 POINTS = 2 * BLOCKS
-SIGNALS = 8
 THERE_ROWS = 9
 BACK_ROWS = 10
 VMEM_LIMIT = 40 * 1024 * 1024
@@ -30,9 +28,8 @@
     inverse_outer = factor * np.concatenate([cosine.T, -sine.T], axis=1)
     angle = turn * ((digit[:, None] * digit[None, :]) % SIDE / SIDE)
     cosine, sine = np.cos(angle), np.sin(angle)
-    order = np.arange(2 * SIDE).reshape(2, 2, HALF).transpose(1, 0, 2).reshape(-1)
-    forward_inner = np.block([[cosine, -sine], [sine, cosine]])[:, order]
-    inverse_inner = np.block([[cosine, sine], [-sine, cosine]])[order, :]
+    forward_inner = np.block([[cosine, -sine], [sine, cosine]])
+    inverse_inner = np.block([[cosine, sine], [-sine, cosine]])
     angle = turn * ((digit[:, None] + 0.25) * digit[None, :] / BLOCK)
     twist = np.stack([np.cos(angle), np.sin(angle)])
     return (
@@ -111,19 +108,26 @@
     )()
 
 
+def place_of(signal):
+    kind, channel = divmod(signal, 4)
+    return (channel, 8) if kind == 2 else (channel // 2, 4 * kind + 2 * (channel % 2))
+
+
 def forward_kernel(seq_ref, cot_ref, taps_ref, tables_ref, twist_ref, out_ref, rows):
-    for first, count, source in ((0, 4, seq_ref), (4, 4, cot_ref), (SIGNALS, 2, taps_ref)):
+    for first, count, source in ((0, 4, seq_ref), (4, 4, cot_ref), (8, 2, taps_ref)):
         for a in range(SIDE):
             rows[pl.ds(first * SIDE + a, count, stride=SIDE), :] = source[:, a * SIDE : (a + 1) * SIDE]
 
-    def row(index):
-        return rows[index * SIDE : (index + 1) * SIDE, :]
-
-    mine = jnp.where(lax.axis_index("chan") % 2 == 0, row(SIGNALS), row(SIGNALS + 1))
-    opened = dot_wide(tables_ref[0], jnp.concatenate([row(i) for i in range(SIGNALS)] + [mine], axis=1))
+    signals = jnp.concatenate([rows[i * SIDE : (i + 1) * SIDE, :] for i in range(10)], axis=1)
+    opened = dot_wide(tables_ref[0], signals)
     cosine, sine = twist_ref[0], twist_ref[1]
     inner = jnp.concatenate([tables_ref[1], tables_ref[2]], axis=1)
-    for group in ((0, 1), (2, 3), (4, 5), (6, 7), (8,)):
+    sends_real = lax.axis_index("chan") % 2 == 0
+
+    def leave(filt, row, values):
+        out_ref[pl.ds(THERE_ROWS * filt + row, SIDE, stride=2 * THERE_ROWS), :] = values
+
+    for group in ((0, 1), (2, 3), (4, 5), (6, 7), (8, 9)):
         twisted = []
         for i in group:
             real = opened[:SIDE, i * SIDE : (i + 1) * SIDE]
@@ -131,10 +135,14 @@
             twisted.append(jnp.concatenate([real * cosine + imag * sine, imag * cosine - real * sine], axis=1))
         spectra = dot_three(jnp.concatenate(twisted, axis=0), inner)
         for place, i in enumerate(group):
-            for half in range(2):
-                out_ref[pl.ds(THERE_ROWS * half + i, SIDE, stride=2 * THERE_ROWS), :] = spectra[
-                    place * SIDE : (place + 1) * SIDE, half * SIDE : (half + 1) * SIDE
-                ]
+            real = spectra[place * SIDE : (place + 1) * SIDE, :SIDE]
+            imag = spectra[place * SIDE : (place + 1) * SIDE, SIDE:]
+            filt, row = place_of(i)
+            if row == 8:
+                leave(filt, row, jnp.where(sends_real, real, imag))
+            else:
+                leave(filt, row, real)
+                leave(filt, row + 1, imag)
 
 
 def forward_blocks(sequence, cotangent, taps):
@@ -145,58 +153,48 @@
 
 def middle_kernel(in_ref, there_ref, back_ref, adjoint_ref, out_ref):
     there, back, adjoint = there_ref[...], back_ref[...], adjoint_ref[...]
-    low = lax.broadcasted_iota(jnp.int32, (BLOCKS, SIDE), 1) < HALF
-
-    def turn(values):
-        return pltpu.roll(values, HALF, 1)
-
-    def arrived(chan, row):
-        return in_ref[pl.ds(chan * THERE_ROWS + row, BLOCKS, stride=CHAN * THERE_ROWS), :]
-
-    def leave(chan, row, values):
-        out_ref[pl.ds(chan * BACK_ROWS + row, BLOCKS, stride=CHAN * BACK_ROWS), :] = values
-
-    def points_of(first_chan, second_chan, rows):
-        reals, imags = [], []
-        for r in rows:
-            first, second = arrived(first_chan, r), arrived(second_chan, r)
-            reals.append(jnp.where(low, first, turn(second)))
-            imags.append(jnp.where(low, turn(first), second))
-        sides = [jnp.concatenate(reals, axis=1), jnp.concatenate(imags, axis=1)]
+
+    def points_of(places):
+        sides = [
+            jnp.concatenate(
+                [
+                    in_ref[pl.ds(chan * THERE_ROWS + row, BLOCKS, stride=CHAN * THERE_ROWS), :]
+                    for chan, row in places(part)
+                ],
+                axis=1,
+            )
+            for part in range(2)
+        ]
         points = dot_wide(there, jnp.concatenate(sides, axis=0))
         return points[:POINTS], points[POINTS:]
 
-    def blocks_of(table, real, imag):
-        blocks = dot_three(table, jnp.concatenate([real, imag], axis=0))
-        return blocks[:BLOCKS], blocks[BLOCKS:]
-
-    filters = [points_of(f, f, (SIGNALS,)) for f in range(2)]
-    hr, hi = (jnp.concatenate([filters[f][part] for f in (0, 0, 1, 1)], axis=1) for part in range(2))
-    wide = 4 * SIDE
-    real = imag = 0.0
-    for first in range(0, CHAN, 2):
-        pr, pi = points_of(first, first + 1, range(SIGNALS))
-        xr, xi, gr, gi = pr[:, :wide], pi[:, :wide], pr[:, wide:], pi[:, wide:]
-        real = real + (xr * gr + xi * gi)
-        imag = imag + (xr * gi - xi * gr)
-        for row, (br, bi) in (
-            (0, blocks_of(back, hr * xr - hi * xi, hr * xi + hi * xr)),
-            (4, blocks_of(adjoint, hr * gr + hi * gi, hr * gi - hi * gr)),
-        ):
-            for r in range(4):
-                cr, ci = br[:, r * SIDE : (r + 1) * SIDE], bi[:, r * SIDE : (r + 1) * SIDE]
-                leave(first, row + r, jnp.where(low, cr, turn(ci)))
-                leave(first + 1, row + r, jnp.where(low, turn(cr), ci))
+    def leave(table, places, real, imag):
+        blocks = dot_wide(table, jnp.concatenate([real, imag], axis=0))
+        for part in range(2):
+            lines = slice(part * BLOCKS, (part + 1) * BLOCKS)
+            for n, (chan, row) in places:
+                out_ref[pl.ds(chan * BACK_ROWS + row + part, BLOCKS, stride=CHAN * BACK_ROWS), :] = blocks[
+                    lines, n * SIDE : (n + 1) * SIDE
+                ]
 
     def over_channels(values):
-        sums = [values[:, f * 2 * SIDE : f * 2 * SIDE + SIDE] + values[:, f * 2 * SIDE + SIDE : (f + 1) * 2 * SIDE] for f in range(2)]
-        return jnp.concatenate([s + turn(s) for s in sums], axis=1)
-
-    br, bi = blocks_of(adjoint, over_channels(real), over_channels(imag))
-    for f in range(2):
-        tap = jnp.where(low, br[:, f * SIDE : (f + 1) * SIDE], bi[:, f * SIDE : (f + 1) * SIDE])
-        for chan in range(CHAN):
-            leave(chan, SIGNALS + f, tap)
+        return sum(values[:, n * SIDE : (n + 1) * SIDE] for n in range(len(first_kind)))
+
+    first_kind = [(chan, row) for chan in range(CHAN) for row in (0, 2)]
+    second_kind = [(chan, row + 4) for chan, row in first_kind]
+    hr, hi = points_of(lambda part: [(part, 8)])
+    hr, hi = (jnp.concatenate([part] * len(first_kind), axis=1) for part in (hr, hi))
+    pr, pi = points_of(lambda part: [(chan, row + part) for chan, row in first_kind + second_kind])
+    wide = len(first_kind) * SIDE
+    xr, xi, gr, gi = pr[:, :wide], pi[:, :wide], pr[:, wide:], pi[:, wide:]
+    leave(back, list(enumerate(first_kind)), hr * xr - hi * xi, hr * xi + hi * xr)
+    leave(adjoint, list(enumerate(second_kind)), hr * gr + hi * gi, hr * gi - hi * gr)
+    leave(
+        adjoint,
+        [(0, (chan, 8)) for chan in range(CHAN)],
+        over_channels(xr * gr + xi * gi),
+        over_channels(xr * gi - xi * gr),
+    )
 
 
 def middle_blocks(spectra):
@@ -211,7 +209,8 @@
 
     columns = []
     for i in range(10):
-        both = [in_ref[pl.ds(BACK_ROWS * half + i, SIDE, stride=2 * BACK_ROWS), :] for half in range(2)]
+        filt, row = place_of(i)
+        both = [in_ref[pl.ds(BACK_ROWS * filt + row + p, SIDE, stride=2 * BACK_ROWS), :] for p in range(2)]
         turned = dot_three(jnp.concatenate(both, axis=1), inner)
         real, imag = turned[:, :SIDE], turned[:, SIDE:]
         column = jnp.concatenate([real * cosine - imag * sine, imag * cosine + real * sine], axis=0)

time: 99.6 us -> 99.2 us (level)
  no operation moved by 1% of the time
where the time goes in v11:
time: 99.2 us; the launch traced here: 97.9 us
  blocking collectives  91.1 us (92%)
  Pallas kernels  5.14 us (5%)
    all_to_all x2, blocking collectives, exchange(): lax.all_to_all(cut, ('ctx', 'chan'), split_axis=0, concat_axis=0, tiled=T...  91.1 us
    pallas_call x3, Pallas kernels, call(): pl.pallas_call(kernel, out_shape=shapes if many else shapes[0], in_specs=...  4.88 us

profile of v11, /device:TPU:32, one launch (start us, length us, event | category | flops | bytes accessed | tf_op | source)
XLA Modules:
  0.0 97.9 jit_solution(11297022278843910120)
XLA Ops:
  0.6 0.0 copy-start.2
  0.6 0.0 copy-start.1
  0.7 0.0 copy-start
  0.7 0.0 copy-start.4
  0.7 0.3 twist_table.1.twist_ref
  0.9 0.7 copy-done.2
  1.6 0.1 copy-done.1
  1.7 0.1 copy-done
  1.8 0.0 copy-done.4
  1.8 1.4 %forward_blocks.1 = f32[2304,128]{1,0:T(8,128)S(1)} custom-call(f32[4,16384]{1,0:T(4,128)S(1)} %copy-done, f32[4,16384]{1,0:T(4,128)S(1)} %copy-done.1, f32[2,16384]{1,0:T(2,128)S(1)} %copy-done.4, f32[3,256,128]{2,1,0:T(8,128)S(1)} %copy-done.2, f32[2,128,128]{2,1,0:T(8,128)S(1)} %twist_table.1.twist_ref), custom_call_target="tpu_custom_call" | custom-call | tf_op jit(solution)/shard_map/forward_blocks/pallas_call | solution.py:81
  3.2 0.0 copy-start.7
  3.3 0.0 copy-start.8
  3.3 0.0 copy-start.9
  3.3 47.9 %all_to_all.10 = f32[256,9,1,128]{3,2,1,0:T(1,128)S(1)} all-to-all(f32[256,9,1,128]{3,2,1,0:T(1,128)S(1)} %bitcast.8), channel_id=1, replica_groups=mesh['ctx'=32,'chan'=8] {'ctx','chan'}, dimensions={0} | all-to-all | bytes 2359296 | tf_op jit(solution)/shard_map/all_to_all | solution.py:236
  51.1 0.0 copy-done.7
  51.1 0.0 copy-done.8
  51.1 0.0 copy-done.9
  51.2 1.5 %middle_blocks.1 = f32[2560,128]{1,0:T(8,128)S(1)} custom-call(f32[2304,128]{1,0:T(8,128)S(1)} %bitcast.7, f32[128,64]{1,0:T(8,128)S(1)} %copy-done.7, f32[64,128]{1,0:T(8,128)S(1)} %copy-done.9, f32[64,128]{1,0:T(8,128)S(1)} %copy-done.8), custom_call_target="tpu_custom_call" | custom-call | tf_op jit(solution)/shard_map/middle_blocks/pallas_call | solution.py:81
  52.7 0.0 copy-start.3
  52.7 0.0 copy-start.5
  52.7 0.0 copy-start.6
  52.7 0.0 copy-start.10
  52.7 43.2 %all_to_all.11 = f32[256,5,2,128]{3,2,1,0:T(2,128)S(1)} all-to-all(f32[256,5,2,128]{3,2,1,0:T(2,128)S(1)} %bitcast.6), channel_id=1, replica_groups=mesh['ctx'=32,'chan'=8] {'ctx','chan'}, dimensions={0} | all-to-all | bytes 2621440 | tf_op jit(solution)/shard_map/all_to_all | solution.py:236
  95.9 0.0 copy-done.3
  95.9 0.0 copy-done.5
  95.9 0.0 copy-done.6
  95.9 0.0 copy-done.10
  95.9 2.0 %inverse_blocks.1 = (f32[4,16384]{1,0:T(4,128)}, f32[4,16384]{1,0:T(4,128)}, f32[2,16384]{1,0:T(2,128)}) custom-call(f32[2560,128]{1,0:T(8,128)S(1)} %bitcast.5, f32[4,16384]{1,0:T(4,128)S(1)} %copy-done, f32[4,16384]{1,0:T(4,128)S(1)} %copy-done.1, f32[1,4]{1,0:T(1,128)S(1)} %bitcast.9, f32[256,256]{1,0:T(8,128)S(1)} %copy-done.3, ...), custom_call_target="tpu_custom_call" | custom-call | tf_op jit(solution)/shard_map/inverse_blocks/pallas_call | solution.py:81
Async XLA Ops:
  0.6 1.0 %copy-start.2 = (f32[3,256,128]{2,1,0:T(8,128)S(1)}, f32[3,256,128]{2,1,0:T(8,128)}, u32[]{:S(2)}) copy-start(f32[3,256,128]{2,1,0:T(8,128)} %constant.14.clone.tables_ref) | copy-start | bytes 1179652
  0.6 1.1 %copy-start.1 = (f32[4,16384]{1,0:T(4,128)S(1)}, f32[4,16384]{1,0:T(4,128)}, u32[]{:S(2)}) copy-start(f32[4,16384]{1,0:T(4,128)} %cot_ref.3) | copy-start | bytes 786436
  0.7 1.1 %copy-start = (f32[4,16384]{1,0:T(4,128)S(1)}, f32[4,16384]{1,0:T(4,128)}, u32[]{:S(2)}) copy-start(f32[4,16384]{1,0:T(4,128)} %seq_ref.3) | copy-start | bytes 786436
  0.7 1.2 %copy-start.4 = (f32[2,16384]{1,0:T(2,128)S(1)}, f32[2,16384]{1,0:T(2,128)}, u32[]{:S(2)}) copy-start(f32[2,16384]{1,0:T(2,128)} %taps_ref.1) | copy-start | bytes 393220
  3.2 47.9 %copy-start.7 = (f32[128,64]{1,0:T(8,128)S(1)}, f32[128,64]{1,0:T(8,128)}, u32[]{:S(2)}) copy-start(f32[128,64]{1,0:T(8,128)} %constant.15.clone.there_ref) | copy-start | bytes 98308
  3.3 47.9 %copy-start.8 = (f32[64,128]{1,0:T(8,128)S(1)}, f32[64,128]{1,0:T(8,128)}, u32[]{:S(2)}) copy-start(f32[64,128]{1,0:T(8,128)} %constant.17.clone.adjoint_ref) | copy-start | bytes 98308
  3.3 47.9 %copy-start.9 = (f32[64,128]{1,0:T(8,128)S(1)}, f32[64,128]{1,0:T(8,128)}, u32[]{:S(2)}) copy-start(f32[64,128]{1,0:T(8,128)} %constant.16.clone.back_ref) | copy-start | bytes 98308
  52.7 43.3 %copy-start.3 = (f32[256,256]{1,0:T(8,128)S(1)}, f32[256,256]{1,0:T(8,128)}, u32[]{:S(2)}) copy-start(f32[256,256]{1,0:T(8,128)} %constant.18.clone.inner_ref) | copy-start | bytes 786436
  52.7 43.2 %copy-start.5 = (f32[2,128,128]{2,1,0:T(8,128)S(1)}, f32[2,128,128]{2,1,0:T(8,128)}, u32[]{:S(2)}) copy-start(f32[2,128,128]{2,1,0:T(8,128)} %constant.20.clone.twist_ref) | copy-start | bytes 393220
  52.7 43.2 %copy-start.6 = (f32[128,256]{1,0:T(8,128)S(1)}, f32[128,256]{1,0:T(8,128)}, u32[]{:S(2)}) copy-start(f32[128,256]{1,0:T(8,128)} %constant.19.clone.outer_ref) | copy-start | bytes 393220
  52.7 43.2 %copy-start.10 = (f32[4]{0:T(128)S(1)}, f32[4]{0:T(128)}, u32[]{:S(2)}) copy-start(f32[4]{0:T(128)} %param.13) | copy-start | bytes 52

commit v12 on v11

--- a/solution.py
+++ b/solution.py
@@ -113,12 +113,15 @@
     return (channel, 8) if kind == 2 else (channel // 2, 4 * kind + 2 * (channel % 2))
 
 
-def forward_kernel(seq_ref, cot_ref, taps_ref, tables_ref, twist_ref, out_ref, rows):
-    for first, count, source in ((0, 4, seq_ref), (4, 4, cot_ref), (8, 2, taps_ref)):
-        for a in range(SIDE):
-            rows[pl.ds(first * SIDE + a, count, stride=SIDE), :] = source[:, a * SIDE : (a + 1) * SIDE]
-
-    signals = jnp.concatenate([rows[i * SIDE : (i + 1) * SIDE, :] for i in range(10)], axis=1)
+def forward_kernel(seq_ref, cot_ref, taps_ref, tables_ref, twist_ref, out_ref):
+    signals = jnp.concatenate(
+        [
+            source[i : i + 1, :].reshape(SIDE, SIDE)
+            for count, source in ((4, seq_ref), (4, cot_ref), (2, taps_ref))
+            for i in range(count)
+        ],
+        axis=1,
+    )
     opened = dot_wide(tables_ref[0], signals)
     cosine, sine = twist_ref[0], twist_ref[1]
     inner = jnp.concatenate([tables_ref[1], tables_ref[2]], axis=1)
@@ -147,8 +150,7 @@
 
 def forward_blocks(sequence, cotangent, taps):
     operands = (sequence, cotangent, taps, jnp.asarray(FORWARD_TABLES), twist_table())
-    scratch = [pltpu.VMEM((10 * SIDE, SIDE), jnp.float32)]
-    return call(forward_kernel, "forward_blocks", (OWNERS * THERE_ROWS, SIDE), operands, scratch)
+    return call(forward_kernel, "forward_blocks", (OWNERS * THERE_ROWS, SIDE), operands)
 
 
 def middle_kernel(in_ref, there_ref, back_ref, adjoint_ref, out_ref):
@@ -202,10 +204,9 @@
     return call(middle_kernel, "middle_blocks", (OWNERS * BACK_ROWS, SIDE), operands)
 
 
-def inverse_kernel(in_ref, seq_ref, cot_ref, skip_ref, inner_ref, outer_ref, twist_ref, y_ref, g_ref, f_ref, rows):
+def inverse_kernel(in_ref, seq_ref, cot_ref, skip_ref, inner_ref, outer_ref, twist_ref, y_ref, g_ref, f_ref):
     cosine, sine = twist_ref[0], twist_ref[1]
     inner, outer = inner_ref[...], outer_ref[...]
-    gain = jnp.concatenate([jnp.broadcast_to(skip_ref[:, i : i + 1], (1, SIDE)) for i in range(4)], axis=0)
 
     columns = []
     for i in range(10):
@@ -216,19 +217,21 @@
         column = jnp.concatenate([real * cosine - imag * sine, imag * cosine + real * sine], axis=0)
         columns.append(column)
     closed = dot_wide(outer, jnp.concatenate(columns, axis=1))
-    for i in range(10):
-        rows[i * SIDE : (i + 1) * SIDE, :] = closed[:, i * SIDE : (i + 1) * SIDE]
-    for a in range(SIDE):
-        lanes = slice(a * SIDE, (a + 1) * SIDE)
-        y_ref[:, lanes] = rows[pl.ds(a, 4, stride=SIDE), :] + gain * seq_ref[:, lanes]
-        g_ref[:, lanes] = rows[pl.ds(4 * SIDE + a, 4, stride=SIDE), :] + gain * cot_ref[:, lanes]
-        f_ref[:, lanes] = rows[pl.ds(8 * SIDE + a, 2, stride=SIDE), :]
+
+    def line(signal):
+        return closed[:, signal * SIDE : (signal + 1) * SIDE].reshape(1, BLOCK)
+
+    for c in range(4):
+        gain = skip_ref[:, c : c + 1]
+        y_ref[c : c + 1, :] = line(c) + gain * seq_ref[c : c + 1, :]
+        g_ref[c : c + 1, :] = line(4 + c) + gain * cot_ref[c : c + 1, :]
+    for c in range(2):
+        f_ref[c : c + 1, :] = line(8 + c)
 
 
 def inverse_blocks(spectra, sequence, cotangent, skip_gain):
     operands = (spectra, sequence, cotangent, skip_gain[None, :]) + tuple(jnp.asarray(t) for t in INVERSE_TABLES)
-    scratch = [pltpu.VMEM((10 * SIDE, SIDE), jnp.float32)]
-    return call(inverse_kernel, "inverse_blocks", ((4, BLOCK), (4, BLOCK), (2, BLOCK)), operands, scratch)
+    return call(inverse_kernel, "inverse_blocks", ((4, BLOCK), (4, BLOCK), (2, BLOCK)), operands)
 
 
 def exchange(rows, tall):

time: 99.2 us -> 98.6 us (level)
  no operation moved by 1% of the time
where the time goes in v12:
time: 98.6 us; the launch traced here: 97.3 us
  blocking collectives  91.1 us (92%)
  Pallas kernels  4.48 us (5%)
    all_to_all x2, blocking collectives, exchange(): lax.all_to_all(cut, ('ctx', 'chan'), split_axis=0, concat_axis=0, tiled=T...  91.1 us
    pallas_call x3, Pallas kernels, call(): pl.pallas_call(kernel, out_shape=shapes if many else shapes[0], in_specs=...  4.23 us

profile of v12, /device:TPU:32, one launch (start us, length us, event | category | flops | bytes accessed | tf_op | source)
XLA Modules:
  0.0 97.3 jit_solution(10338463658437427206)
XLA Ops:
  0.6 0.0 copy-start.2
  0.6 0.0 copy-start.1
  0.7 0.0 copy-start
  0.7 0.0 copy-start.4
  0.7 0.3 twist_table.1.twist_ref
  0.9 0.7 copy-done.2
  1.6 0.1 copy-done.1
  1.7 0.1 copy-done
  1.8 0.0 copy-done.4
  1.8 1.1 %forward_blocks.1 = f32[2304,128]{1,0:T(8,128)S(1)} custom-call(f32[4,16384]{1,0:T(4,128)S(1)} %copy-done, f32[4,16384]{1,0:T(4,128)S(1)} %copy-done.1, f32[2,16384]{1,0:T(2,128)S(1)} %copy-done.4, f32[3,256,128]{2,1,0:T(8,128)S(1)} %copy-done.2, f32[2,128,128]{2,1,0:T(8,128)S(1)} %twist_table.1.twist_ref), custom_call_target="tpu_custom_call" | custom-call | tf_op jit(solution)/shard_map/forward_blocks/pallas_call | solution.py:81
  2.9 0.0 copy-start.7
  2.9 0.0 copy-start.8
  2.9 0.0 copy-start.9
  2.9 47.9 %all_to_all.10 = f32[256,9,1,128]{3,2,1,0:T(1,128)S(1)} all-to-all(f32[256,9,1,128]{3,2,1,0:T(1,128)S(1)} %bitcast.8), channel_id=1, replica_groups=mesh['ctx'=32,'chan'=8] {'ctx','chan'}, dimensions={0} | all-to-all | bytes 2359296 | tf_op jit(solution)/shard_map/all_to_all | solution.py:239
  50.8 0.0 copy-done.7
  50.8 0.0 copy-done.8
  50.8 0.0 copy-done.9
  50.8 1.5 %middle_blocks.1 = f32[2560,128]{1,0:T(8,128)S(1)} custom-call(f32[2304,128]{1,0:T(8,128)S(1)} %bitcast.7, f32[128,64]{1,0:T(8,128)S(1)} %copy-done.7, f32[64,128]{1,0:T(8,128)S(1)} %copy-done.9, f32[64,128]{1,0:T(8,128)S(1)} %copy-done.8), custom_call_target="tpu_custom_call" | custom-call | tf_op jit(solution)/shard_map/middle_blocks/pallas_call | solution.py:81
  52.3 0.0 copy-start.3
  52.3 0.0 copy-start.5
  52.3 0.0 copy-start.6
  52.3 0.0 copy-start.10
  52.3 43.2 %all_to_all.11 = f32[256,5,2,128]{3,2,1,0:T(2,128)S(1)} all-to-all(f32[256,5,2,128]{3,2,1,0:T(2,128)S(1)} %bitcast.6), channel_id=1, replica_groups=mesh['ctx'=32,'chan'=8] {'ctx','chan'}, dimensions={0} | all-to-all | bytes 2621440 | tf_op jit(solution)/shard_map/all_to_all | solution.py:239
  95.6 0.0 copy-done.3
  95.6 0.0 copy-done.5
  95.6 0.0 copy-done.6
  95.6 0.0 copy-done.10
  95.6 1.7 %inverse_blocks.1 = (f32[4,16384]{1,0:T(4,128)}, f32[4,16384]{1,0:T(4,128)}, f32[2,16384]{1,0:T(2,128)}) custom-call(f32[2560,128]{1,0:T(8,128)S(1)} %bitcast.5, f32[4,16384]{1,0:T(4,128)S(1)} %copy-done, f32[4,16384]{1,0:T(4,128)S(1)} %copy-done.1, f32[1,4]{1,0:T(1,128)S(1)} %bitcast.9, f32[256,256]{1,0:T(8,128)S(1)} %copy-done.3, ...), custom_call_target="tpu_custom_call" | custom-call | tf_op jit(solution)/shard_map/inverse_blocks/pallas_call | solution.py:81
Async XLA Ops:
  0.6 1.0 %copy-start.2 = (f32[3,256,128]{2,1,0:T(8,128)S(1)}, f32[3,256,128]{2,1,0:T(8,128)}, u32[]{:S(2)}) copy-start(f32[3,256,128]{2,1,0:T(8,128)} %constant.14.clone.tables_ref) | copy-start | bytes 1179652
  0.6 1.1 %copy-start.1 = (f32[4,16384]{1,0:T(4,128)S(1)}, f32[4,16384]{1,0:T(4,128)}, u32[]{:S(2)}) copy-start(f32[4,16384]{1,0:T(4,128)} %cot_ref.3) | copy-start | bytes 786436
  0.7 1.1 %copy-start = (f32[4,16384]{1,0:T(4,128)S(1)}, f32[4,16384]{1,0:T(4,128)}, u32[]{:S(2)}) copy-start(f32[4,16384]{1,0:T(4,128)} %seq_ref.3) | copy-start | bytes 786436
  0.7 1.2 %copy-start.4 = (f32[2,16384]{1,0:T(2,128)S(1)}, f32[2,16384]{1,0:T(2,128)}, u32[]{:S(2)}) copy-start(f32[2,16384]{1,0:T(2,128)} %taps_ref.1) | copy-start | bytes 393220
  2.9 47.9 %copy-start.7 = (f32[128,64]{1,0:T(8,128)S(1)}, f32[128,64]{1,0:T(8,128)}, u32[]{:S(2)}) copy-start(f32[128,64]{1,0:T(8,128)} %constant.15.clone.there_ref) | copy-start | bytes 98308
  2.9 47.9 %copy-start.8 = (f32[64,128]{1,0:T(8,128)S(1)}, f32[64,128]{1,0:T(8,128)}, u32[]{:S(2)}) copy-start(f32[64,128]{1,0:T(8,128)} %constant.17.clone.adjoint_ref) | copy-start | bytes 98308
  2.9 47.9 %copy-start.9 = (f32[64,128]{1,0:T(8,128)S(1)}, f32[64,128]{1,0:T(8,128)}, u32[]{:S(2)}) copy-start(f32[64,128]{1,0:T(8,128)} %constant.16.clone.back_ref) | copy-start | bytes 98308
  52.3 43.3 %copy-start.3 = (f32[256,256]{1,0:T(8,128)S(1)}, f32[256,256]{1,0:T(8,128)}, u32[]{:S(2)}) copy-start(f32[256,256]{1,0:T(8,128)} %constant.18.clone.inner_ref) | copy-start | bytes 786436
  52.3 43.3 %copy-start.5 = (f32[2,128,128]{2,1,0:T(8,128)S(1)}, f32[2,128,128]{2,1,0:T(8,128)}, u32[]{:S(2)}) copy-start(f32[2,128,128]{2,1,0:T(8,128)} %constant.20.clone.twist_ref) | copy-start | bytes 393220
  52.3 43.3 %copy-start.6 = (f32[128,256]{1,0:T(8,128)S(1)}, f32[128,256]{1,0:T(8,128)}, u32[]{:S(2)}) copy-start(f32[128,256]{1,0:T(8,128)} %constant.19.clone.outer_ref) | copy-start | bytes 393220
  52.3 43.3 %copy-start.10 = (f32[4]{0:T(128)S(1)}, f32[4]{0:T(128)}, u32[]{:S(2)}) copy-start(f32[4]{0:T(128)} %param.13) | copy-start | bytes 52

commit v13 on v12

--- a/solution.py
+++ b/solution.py
@@ -33,7 +33,7 @@
     angle = turn * ((digit[:, None] + 0.25) * digit[None, :] / BLOCK)
     twist = np.stack([np.cos(angle), np.sin(angle)])
     return (
-        np.stack([forward_outer, forward_inner[:, :SIDE], forward_inner[:, SIDE:]]).astype(single),
+        np.stack([forward_outer, forward_inner[:, :SIDE]]).astype(single),
         tuple(t.astype(single) for t in (inverse_inner, inverse_outer, twist)),
     )
 
@@ -124,7 +124,8 @@
     )
     opened = dot_wide(tables_ref[0], signals)
     cosine, sine = twist_ref[0], twist_ref[1]
-    inner = jnp.concatenate([tables_ref[1], tables_ref[2]], axis=1)
+    across = tables_ref[1]
+    inner = jnp.concatenate([across, jnp.concatenate([-across[SIDE:], across[:SIDE]], axis=0)], axis=1)
     sends_real = lax.axis_index("chan") % 2 == 0
 
     def leave(filt, row, values):

time: 98.6 us -> 98.5 us (level)
  no operation moved by 1% of the time
where the time goes in v13:
time: 98.5 us; the launch traced here: 97.2 us
  blocking collectives  91.1 us (92%)
  Pallas kernels  4.48 us (5%)
    all_to_all x2, blocking collectives, exchange(): lax.all_to_all(cut, ('ctx', 'chan'), split_axis=0, concat_axis=0, tiled=T...  91.1 us
    pallas_call x3, Pallas kernels, call(): pl.pallas_call(kernel, out_shape=shapes if many else shapes[0], in_specs=...  4.23 us

profile of v13, /device:TPU:32, one launch (start us, length us, event | category | flops | bytes accessed | tf_op | source)
XLA Modules:
  0.0 97.2 jit_solution(13776843252932394816)
XLA Ops:
  0.6 0.0 copy-start.3
  0.6 0.0 copy-start.1
  0.7 0.0 copy-start
  0.7 0.0 copy-start.4
  0.7 0.3 twist_table.1.twist_ref
  0.9 0.6 copy-done.3
  1.6 0.1 copy-done.1
  1.7 0.1 copy-done
  1.7 0.0 copy-done.4
  1.8 1.1 %forward_blocks.1 = f32[2304,128]{1,0:T(8,128)S(1)} custom-call(f32[4,16384]{1,0:T(4,128)S(1)} %copy-done, f32[4,16384]{1,0:T(4,128)S(1)} %copy-done.1, f32[2,16384]{1,0:T(2,128)S(1)} %copy-done.4, f32[2,256,128]{2,1,0:T(8,128)S(1)} %copy-done.3, f32[2,128,128]{2,1,0:T(8,128)S(1)} %twist_table.1.twist_ref), custom_call_target="tpu_custom_call" | custom-call | tf_op jit(solution)/shard_map/forward_blocks/pallas_call | solution.py:81
  2.8 0.0 copy-start.7
  2.9 0.0 copy-start.8
  2.9 0.0 copy-start.9
  2.9 47.9 %all_to_all.10 = f32[256,9,1,128]{3,2,1,0:T(1,128)S(1)} all-to-all(f32[256,9,1,128]{3,2,1,0:T(1,128)S(1)} %bitcast.8), channel_id=1, replica_groups=mesh['ctx'=32,'chan'=8] {'ctx','chan'}, dimensions={0} | all-to-all | bytes 2359296 | tf_op jit(solution)/shard_map/all_to_all | solution.py:240
  50.7 0.0 copy-done.7
  50.7 0.0 copy-done.8
  50.7 0.0 copy-done.9
  50.8 1.5 %middle_blocks.1 = f32[2560,128]{1,0:T(8,128)S(1)} custom-call(f32[2304,128]{1,0:T(8,128)S(1)} %bitcast.7, f32[128,64]{1,0:T(8,128)S(1)} %copy-done.7, f32[64,128]{1,0:T(8,128)S(1)} %copy-done.9, f32[64,128]{1,0:T(8,128)S(1)} %copy-done.8), custom_call_target="tpu_custom_call" | custom-call | tf_op jit(solution)/shard_map/middle_blocks/pallas_call | solution.py:81
  52.3 0.0 copy-start.2
  52.3 0.0 copy-start.5
  52.3 0.0 copy-start.6
  52.3 0.0 copy-start.10
  52.3 43.2 %all_to_all.11 = f32[256,5,2,128]{3,2,1,0:T(2,128)S(1)} all-to-all(f32[256,5,2,128]{3,2,1,0:T(2,128)S(1)} %bitcast.6), channel_id=1, replica_groups=mesh['ctx'=32,'chan'=8] {'ctx','chan'}, dimensions={0} | all-to-all | bytes 2621440 | tf_op jit(solution)/shard_map/all_to_all | solution.py:240
  95.5 0.0 copy-done.2
  95.5 0.0 copy-done.5
  95.5 0.0 copy-done.6
  95.5 0.0 copy-done.10
  95.5 1.7 %inverse_blocks.1 = (f32[4,16384]{1,0:T(4,128)}, f32[4,16384]{1,0:T(4,128)}, f32[2,16384]{1,0:T(2,128)}) custom-call(f32[2560,128]{1,0:T(8,128)S(1)} %bitcast.5, f32[4,16384]{1,0:T(4,128)S(1)} %copy-done, f32[4,16384]{1,0:T(4,128)S(1)} %copy-done.1, f32[1,4]{1,0:T(1,128)S(1)} %bitcast.9, f32[256,256]{1,0:T(8,128)S(1)} %copy-done.2, ...), custom_call_target="tpu_custom_call" | custom-call | tf_op jit(solution)/shard_map/inverse_blocks/pallas_call | solution.py:81
Async XLA Ops:
  0.6 1.0 copy-start.3
  0.6 1.0 %copy-start.1 = (f32[4,16384]{1,0:T(4,128)S(1)}, f32[4,16384]{1,0:T(4,128)}, u32[]{:S(2)}) copy-start(f32[4,16384]{1,0:T(4,128)} %cot_ref.3) | copy-start | bytes 786436
  0.7 1.1 %copy-start = (f32[4,16384]{1,0:T(4,128)S(1)}, f32[4,16384]{1,0:T(4,128)}, u32[]{:S(2)}) copy-start(f32[4,16384]{1,0:T(4,128)} %seq_ref.3) | copy-start | bytes 786436
  0.7 1.1 %copy-start.4 = (f32[2,16384]{1,0:T(2,128)S(1)}, f32[2,16384]{1,0:T(2,128)}, u32[]{:S(2)}) copy-start(f32[2,16384]{1,0:T(2,128)} %taps_ref.1) | copy-start | bytes 393220
  2.8 47.9 %copy-start.7 = (f32[128,64]{1,0:T(8,128)S(1)}, f32[128,64]{1,0:T(8,128)}, u32[]{:S(2)}) copy-start(f32[128,64]{1,0:T(8,128)} %constant.15.clone.there_ref) | copy-start | bytes 98308
  2.9 47.9 %copy-start.8 = (f32[64,128]{1,0:T(8,128)S(1)}, f32[64,128]{1,0:T(8,128)}, u32[]{:S(2)}) copy-start(f32[64,128]{1,0:T(8,128)} %constant.17.clone.adjoint_ref) | copy-start | bytes 98308
  2.9 47.9 %copy-start.9 = (f32[64,128]{1,0:T(8,128)S(1)}, f32[64,128]{1,0:T(8,128)}, u32[]{:S(2)}) copy-start(f32[64,128]{1,0:T(8,128)} %constant.16.clone.back_ref) | copy-start | bytes 98308
  52.3 43.3 %copy-start.2 = (f32[256,256]{1,0:T(8,128)S(1)}, f32[256,256]{1,0:T(8,128)}, u32[]{:S(2)}) copy-start(f32[256,256]{1,0:T(8,128)} %constant.18.clone.inner_ref) | copy-start | bytes 786436
  52.3 43.3 %copy-start.5 = (f32[2,128,128]{2,1,0:T(8,128)S(1)}, f32[2,128,128]{2,1,0:T(8,128)}, u32[]{:S(2)}) copy-start(f32[2,128,128]{2,1,0:T(8,128)} %constant.20.clone.twist_ref) | copy-start | bytes 393220
  52.3 43.2 %copy-start.6 = (f32[128,256]{1,0:T(8,128)S(1)}, f32[128,256]{1,0:T(8,128)}, u32[]{:S(2)}) copy-start(f32[128,256]{1,0:T(8,128)} %constant.19.clone.outer_ref) | copy-start | bytes 393220
  52.3 43.2 %copy-start.10 = (f32[4]{0:T(128)S(1)}, f32[4]{0:T(128)}, u32[]{:S(2)}) copy-start(f32[4]{0:T(128)} %param.13) | copy-start | bytes 52

commit v14 on v13

--- a/solution.py
+++ b/solution.py
@@ -33,7 +33,7 @@
     angle = turn * ((digit[:, None] + 0.25) * digit[None, :] / BLOCK)
     twist = np.stack([np.cos(angle), np.sin(angle)])
     return (
-        np.stack([forward_outer, forward_inner[:, :SIDE]]).astype(single),
+        forward_inner[:, :SIDE].astype(single),
         tuple(t.astype(single) for t in (inverse_inner, inverse_outer, twist)),
     )
 
@@ -95,12 +95,18 @@
     angle = (c + 0.25) * b * (2.0 * np.pi / BLOCK)
     twist_ref[0] = jnp.cos(angle)
     twist_ref[1] = jnp.sin(angle)
+    quarter_turns = (4 * lax.broadcasted_iota(jnp.int32, (SIDE, SIDE), 0) + 1) * lax.broadcasted_iota(
+        jnp.int32, (SIDE, SIDE), 1
+    )
+    angle = (quarter_turns & (4 * SIDE - 1)).astype(jnp.float32) * (2.0 * np.pi / (4 * SIDE))
+    twist_ref[2] = jnp.cos(angle)
+    twist_ref[3] = -jnp.sin(angle)
 
 
 def twist_table():
     return pl.pallas_call(
         twist_kernel,
-        out_shape=jax.ShapeDtypeStruct((2, SIDE, SIDE), jnp.float32),
+        out_shape=jax.ShapeDtypeStruct((4, SIDE, SIDE), jnp.float32),
         out_specs=pl.BlockSpec(memory_space=pltpu.VMEM),
         compiler_params=pltpu.CompilerParams(vmem_limit_bytes=4 * 1024 * 1024),
         cost_estimate=pl.CostEstimate(flops=4_000_000_000, bytes_accessed=8_000_000, transcendentals=32768),
@@ -122,9 +128,9 @@
         ],
         axis=1,
     )
-    opened = dot_wide(tables_ref[0], signals)
+    opened = dot_wide(jnp.concatenate([twist_ref[2], twist_ref[3]], axis=0), signals)
     cosine, sine = twist_ref[0], twist_ref[1]
-    across = tables_ref[1]
+    across = tables_ref[...]
     inner = jnp.concatenate([across, jnp.concatenate([-across[SIDE:], across[:SIDE]], axis=0)], axis=1)
     sends_real = lax.axis_index("chan") % 2 == 0
 

time: 98.5 us -> 98.5 us (level)
  no operation moved by 1% of the time
where the time goes in v14:
time: 98.5 us; the launch traced here: 97.2 us
  blocking collectives  91.1 us (92%)
  Pallas kernels  4.73 us (5%)
    all_to_all x2, blocking collectives, exchange(): lax.all_to_all(cut, ('ctx', 'chan'), split_axis=0, concat_axis=0, tiled=T...  91.1 us
    pallas_call x3, Pallas kernels, call(): pl.pallas_call(kernel, out_shape=shapes if many else shapes[0], in_specs=...  4.23 us

profile of v14, /device:TPU:32, one launch (start us, length us, event | category | flops | bytes accessed | tf_op | source)
XLA Modules:
  0.0 97.2 jit_solution(15208860061639166599)
XLA Ops:
  0.6 0.0 copy-start.6
  0.6 0.0 copy-start.1
  0.7 0.0 copy-start
  0.7 0.0 copy-start.3
  0.7 0.5 twist_table.1.twist_ref
  1.2 0.4 copy-done.6
  1.5 0.1 copy-done.1
  1.7 0.1 copy-done
  1.7 0.0 copy-done.3
  1.8 1.1 %forward_blocks.1 = f32[2304,128]{1,0:T(8,128)S(1)} custom-call(f32[4,16384]{1,0:T(4,128)S(1)} %copy-done, f32[4,16384]{1,0:T(4,128)S(1)} %copy-done.1, f32[2,16384]{1,0:T(2,128)S(1)} %copy-done.3, f32[256,128]{1,0:T(8,128)S(1)} %copy-done.6, f32[4,128,128]{2,1,0:T(8,128)S(1)} %twist_table.1.twist_ref), custom_call_target="tpu_custom_call" | custom-call | tf_op jit(solution)/shard_map/forward_blocks/pallas_call | solution.py:81
  2.8 0.0 copy-start.7
  2.8 0.0 copy-start.8
  2.9 0.0 copy-start.9
  2.9 47.9 %all_to_all.10 = f32[256,9,1,128]{3,2,1,0:T(1,128)S(1)} all-to-all(f32[256,9,1,128]{3,2,1,0:T(1,128)S(1)} %bitcast.8), channel_id=1, replica_groups=mesh['ctx'=32,'chan'=8] {'ctx','chan'}, dimensions={0} | all-to-all | bytes 2359296 | tf_op jit(solution)/shard_map/all_to_all | solution.py:246
  50.7 0.0 copy-done.7
  50.7 0.0 copy-done.8
  50.7 0.0 copy-done.9
  50.7 1.5 %middle_blocks.1 = f32[2560,128]{1,0:T(8,128)S(1)} custom-call(f32[2304,128]{1,0:T(8,128)S(1)} %bitcast.7, f32[128,64]{1,0:T(8,128)S(1)} %copy-done.7, f32[64,128]{1,0:T(8,128)S(1)} %copy-done.9, f32[64,128]{1,0:T(8,128)S(1)} %copy-done.8), custom_call_target="tpu_custom_call" | custom-call | tf_op jit(solution)/shard_map/middle_blocks/pallas_call | solution.py:81
  52.2 0.0 copy-start.2
  52.3 0.0 copy-start.4
  52.3 0.0 copy-start.5
  52.3 0.0 copy-start.10
  52.3 43.2 %all_to_all.11 = f32[256,5,2,128]{3,2,1,0:T(2,128)S(1)} all-to-all(f32[256,5,2,128]{3,2,1,0:T(2,128)S(1)} %bitcast.6), channel_id=1, replica_groups=mesh['ctx'=32,'chan'=8] {'ctx','chan'}, dimensions={0} | all-to-all | bytes 2621440 | tf_op jit(solution)/shard_map/all_to_all | solution.py:246
  95.5 0.0 copy-done.2
  95.5 0.0 copy-done.4
  95.5 0.0 copy-done.5
  95.5 0.0 copy-done.10
  95.5 1.7 %inverse_blocks.1 = (f32[4,16384]{1,0:T(4,128)}, f32[4,16384]{1,0:T(4,128)}, f32[2,16384]{1,0:T(2,128)}) custom-call(f32[2560,128]{1,0:T(8,128)S(1)} %bitcast.5, f32[4,16384]{1,0:T(4,128)S(1)} %copy-done, f32[4,16384]{1,0:T(4,128)S(1)} %copy-done.1, f32[1,4]{1,0:T(1,128)S(1)} %bitcast.9, f32[256,256]{1,0:T(8,128)S(1)} %copy-done.2, ...), custom_call_target="tpu_custom_call" | custom-call | tf_op jit(solution)/shard_map/inverse_blocks/pallas_call | solution.py:81
Async XLA Ops:
  0.6 0.9 copy-start.6
  0.6 1.0 %copy-start.1 = (f32[4,16384]{1,0:T(4,128)S(1)}, f32[4,16384]{1,0:T(4,128)}, u32[]{:S(2)}) copy-start(f32[4,16384]{1,0:T(4,128)} %cot_ref.3) | copy-start | bytes 786436
  0.7 1.1 %copy-start = (f32[4,16384]{1,0:T(4,128)S(1)}, f32[4,16384]{1,0:T(4,128)}, u32[]{:S(2)}) copy-start(f32[4,16384]{1,0:T(4,128)} %seq_ref.3) | copy-start | bytes 786436
  0.7 1.1 %copy-start.3 = (f32[2,16384]{1,0:T(2,128)S(1)}, f32[2,16384]{1,0:T(2,128)}, u32[]{:S(2)}) copy-start(f32[2,16384]{1,0:T(2,128)} %taps_ref.1) | copy-start | bytes 393220
  2.8 47.9 %copy-start.7 = (f32[128,64]{1,0:T(8,128)S(1)}, f32[128,64]{1,0:T(8,128)}, u32[]{:S(2)}) copy-start(f32[128,64]{1,0:T(8,128)} %constant.15.clone.there_ref) | copy-start | bytes 98308
  2.8 47.9 %copy-start.8 = (f32[64,128]{1,0:T(8,128)S(1)}, f32[64,128]{1,0:T(8,128)}, u32[]{:S(2)}) copy-start(f32[64,128]{1,0:T(8,128)} %constant.17.clone.adjoint_ref) | copy-start | bytes 98308
  2.9 47.9 %copy-start.9 = (f32[64,128]{1,0:T(8,128)S(1)}, f32[64,128]{1,0:T(8,128)}, u32[]{:S(2)}) copy-start(f32[64,128]{1,0:T(8,128)} %constant.16.clone.back_ref) | copy-start | bytes 98308
  52.2 43.3 %copy-start.2 = (f32[256,256]{1,0:T(8,128)S(1)}, f32[256,256]{1,0:T(8,128)}, u32[]{:S(2)}) copy-start(f32[256,256]{1,0:T(8,128)} %constant.18.clone.inner_ref) | copy-start | bytes 786436
  52.3 43.3 %copy-start.4 = (f32[2,128,128]{2,1,0:T(8,128)S(1)}, f32[2,128,128]{2,1,0:T(8,128)}, u32[]{:S(2)}) copy-start(f32[2,128,128]{2,1,0:T(8,128)} %constant.20.clone.twist_ref) | copy-start | bytes 393220
  52.3 43.2 %copy-start.5 = (f32[128,256]{1,0:T(8,128)S(1)}, f32[128,256]{1,0:T(8,128)}, u32[]{:S(2)}) copy-start(f32[128,256]{1,0:T(8,128)} %constant.19.clone.outer_ref) | copy-start | bytes 393220
  52.3 43.2 %copy-start.10 = (f32[4]{0:T(128)S(1)}, f32[4]{0:T(128)}, u32[]{:S(2)}) copy-start(f32[4]{0:T(128)} %param.13) | copy-start | bytes 52
